TPU v7x, 32 devices: a whole 2x2x4 slice. The times are simulated.
32 devices in a mesh: dp: 8 (over z, x), blk: 4 (over y, core).
Axes of the slice: x: 2, y: 2, z: 4, core: 2. Of those that a mesh axis runs over, the one named last changes fastest.
Arguments:
- block_input: bfloat16 [2, 32, 1024, 512], P(None, 'dp', 'blk'), may hold values from -6 to 6
- segment_ids: int32 [32, 1024], P('dp', 'blk'), may hold values from 0 to 3, as said below
- gain_one: float32 [512], replicated, may hold values from 0.5 to 1.5
- w_query: bfloat16 [512, 512], replicated, may hold values from -0.25 to 0.25
- w_key: bfloat16 [512, 512], replicated, may hold values from -0.25 to 0.25
- w_value: bfloat16 [512, 512], replicated, may hold values from -0.25 to 0.25
- w_out: bfloat16 [512, 512], replicated, may hold values from -1 to 1
- gain_two: float32 [512], replicated, may hold values from 0.5 to 1.5
- w_ctrl: bfloat16 [512, 2], replicated, may hold values from -0.1875 to 0.1875
- w_in: bfloat16 [2, 512, 2048], replicated, may hold values from -1.5 to 1.5
- w_back: bfloat16 [2, 2048, 512], replicated, may hold values from -3 to 3
- cotangent: bfloat16 [2, 32, 1024, 512], P(None, 'dp', 'blk'), may hold values from -6 to 6
Outputs:
- activations: bfloat16 [2, 32, 1024, 512], P(None, 'dp', 'blk')
- grad_input: bfloat16 [2, 32, 1024, 512], P(None, 'dp', 'blk')
- grad_gain_one: float32 [512], replicated
- grad_query: float32 [512, 512], replicated
- grad_key: float32 [512, 512], replicated
- grad_value: float32 [512, 512], replicated
- grad_out: float32 [512, 512], replicated
- grad_gain_two: float32 [512], replicated
- grad_ctrl: float32 [512, 2], replicated
- grad_in: float32 [2, 512, 2048], replicated
- grad_back: float32 [2, 2048, 512], replicated
Inputs may be any that keep to these rules, and one draw needn't show every extreme that they name: `segment_ids`: ids start at 0 and never fall along a row; they rise by one at each document start, and document k >= 1 begins fewer than 128 positions away from k * 256.
All inputs are finite; a program needn't handle non-finite values.
Results may differ from a plain program's by a relative error of at most 0.03.
Values may be sent and summed in bfloat16 or wider, within the bound.
A program may use at most 256 MiB of HBM per device.

v0:
```python
import jax
import jax.numpy as jnp
from jax import lax
from jax.sharding import PartitionSpec as P

HEAD_DIM = 64
GROUP = 32


EPSILON = 1e-05
NEGATIVE = -1000000000.0


def normalize(values, scale_gain):
    return (
        values * lax.rsqrt(jnp.mean(values * values, axis=-1, keepdims=True) + EPSILON) * scale_gain
    )


def local(
    block_input,
    segment_ids,
    gain_one,
    w_query,
    w_key,
    w_value,
    w_out,
    gain_two,
    w_ctrl,
    w_in,
    w_back,
    cotangent,
):
    num_micro, seq_local, tok_rows, model_width = block_input.shape
    batch_rows = num_micro * seq_local
    all_rows = batch_rows * tok_rows
    head_count = model_width // HEAD_DIM
    experts = w_ctrl.shape[1]
    blk_count = lax.axis_size("blk")
    blk_index = lax.axis_index("blk")
    first_pos = blk_index * tok_rows
    last_pos = first_pos + tok_rows - 1
    query_pos = first_pos + jnp.arange(tok_rows, dtype=jnp.int32)
    inputs = block_input.reshape(all_rows, model_width).astype(jnp.float32)
    normed_one, pull_one = jax.vjp(normalize, inputs, gain_one)
    normed_one = normed_one.astype(jnp.bfloat16)
    queries = jnp.dot(normed_one, w_query, preferred_element_type=jnp.float32).astype(jnp.bfloat16)
    keys_local = jnp.dot(normed_one, w_key, preferred_element_type=jnp.float32).astype(jnp.bfloat16)
    values_local = jnp.dot(normed_one, w_value, preferred_element_type=jnp.float32).astype(
        jnp.bfloat16
    )
    query_four = queries.reshape(batch_rows, tok_rows, head_count, HEAD_DIM)
    segments = jnp.concatenate([jnp.zeros_like(segment_ids), segment_ids], axis=0)
    segment_send = segments.astype(jnp.bfloat16)
    send = (
        keys_local.reshape(batch_rows, tok_rows, model_width),
        values_local.reshape(batch_rows, tok_rows, model_width),
        segment_send,
    )

    def scores_for(key_piece, seg_piece, start):
        count = key_piece.shape[1]
        key_four = key_piece.reshape(batch_rows, count, head_count, HEAD_DIM)
        logits_raw = (
            jnp.einsum("bqhd,bkhd->bhqk", query_four, key_four, preferred_element_type=jnp.float32)
            * 0.125
        )
        key_pos = start + jnp.arange(count, dtype=jnp.int32)
        causal = key_pos[None, :] <= query_pos[:, None]
        same_doc = seg_piece[:, None, :] == segment_send[:, :, None]
        allowed = causal[None, None] & same_doc[:, None]
        return jnp.where(allowed, logits_raw, NEGATIVE)

    initial = (
        jnp.full((batch_rows, head_count, tok_rows), -1e30, jnp.float32),
        jnp.zeros((batch_rows, head_count, tok_rows), jnp.float32),
        jnp.zeros((batch_rows, head_count, tok_rows, HEAD_DIM), jnp.float32),
    )
    start = jnp.int32(0)
    key_piece = lax.all_gather(send[0], "blk", axis=1, tiled=True)
    value_piece = lax.all_gather(send[1], "blk", axis=1, tiled=True)
    seg_piece = lax.all_gather(send[2], "blk", axis=1, tiled=True)
    count = key_piece.shape[1]

    def attend_visit(state):
        run_max, run_sum, run_total = state
        scores = scores_for(key_piece, seg_piece, start)
        new_max = jnp.maximum(run_max, jnp.max(scores, axis=-1))
        weights = jnp.exp(scores - new_max[..., None])
        value_four = value_piece.reshape(batch_rows, count, head_count, HEAD_DIM)
        update = jnp.einsum(
            "bhqk,bkhd->bhqd",
            weights.astype(jnp.bfloat16),
            value_four,
            preferred_element_type=jnp.float32,
        )
        return (new_max, jnp.sum(weights, axis=-1), update)

    state = lax.cond(start > last_pos, lambda state: state, attend_visit, initial)
    run_max, run_sum, run_total = state
    log_total = run_max + jnp.log(run_sum)
    attn_four = jnp.transpose(run_total / run_sum[..., None], (0, 2, 1, 3))
    attn_low = attn_four.reshape(all_rows, model_width).astype(jnp.bfloat16)
    hidden_state = inputs + jnp.dot(attn_low, w_out, preferred_element_type=jnp.float32)
    normed_two, pull_two = jax.vjp(normalize, hidden_state, gain_two)
    normed_two = normed_two.astype(jnp.bfloat16)
    groups = all_rows // GROUP
    logits = jnp.dot(normed_two, w_ctrl, preferred_element_type=jnp.float32).reshape(
        groups, GROUP, experts
    )
    gate = jax.nn.softmax(logits, axis=1)
    gate_low = gate.astype(jnp.bfloat16)
    grouped = normed_two.reshape(groups, GROUP, model_width)
    merged = jnp.einsum(
        "gte,gtd->ged", gate_low, grouped, preferred_element_type=jnp.float32
    ).astype(jnp.bfloat16)
    inner = jnp.einsum("ged,edf->gef", merged, w_in, preferred_element_type=jnp.float32)
    activated, pull_gelu = jax.vjp(jax.nn.gelu, inner)
    hidden_units = activated.astype(jnp.bfloat16)
    expert_out = jnp.einsum(
        "gef,efd->ged", hidden_units, w_back, preferred_element_type=jnp.float32
    )
    mixed = jnp.einsum("gte,ged->gtd", gate, expert_out).reshape(all_rows, model_width)
    output = (hidden_state + mixed).astype(jnp.bfloat16).reshape(block_input.shape)
    grad_output = cotangent.reshape(all_rows, model_width).astype(jnp.float32)
    grad_grouped = grad_output.reshape(groups, GROUP, model_width)
    grad_expert = jnp.einsum("gte,gtd->ged", gate, grad_grouped).astype(jnp.bfloat16)
    grad_gate = jnp.einsum("gtd,ged->gte", grad_grouped, expert_out)
    grad_back = jnp.einsum(
        "gef,ged->efd", hidden_units, grad_expert, preferred_element_type=jnp.float32
    )
    grad_hidden = jnp.einsum(
        "ged,efd->gef", grad_expert, w_back, preferred_element_type=jnp.float32
    )
    grad_inner = pull_gelu(grad_hidden)[0].astype(jnp.bfloat16)
    grad_in = jnp.einsum("ged,gef->edf", merged, grad_inner, preferred_element_type=jnp.float32)
    grad_merged = jnp.einsum(
        "gef,edf->ged", grad_inner, w_in, preferred_element_type=jnp.float32
    ).astype(jnp.bfloat16)
    grad_gate = grad_gate + jnp.einsum(
        "gtd,ged->gte", grouped, grad_merged, preferred_element_type=jnp.float32
    )
    grad_logits = (gate * (grad_gate - jnp.sum(gate * grad_gate, axis=1, keepdims=True))).astype(
        jnp.bfloat16
    )
    grad_logits = grad_logits.reshape(all_rows, experts)
    grad_ctrl = jnp.einsum("rd,re->de", normed_two, grad_logits, preferred_element_type=jnp.float32)
    grad_normed_two = jnp.einsum(
        "gte,ged->gtd", gate_low, grad_merged, preferred_element_type=jnp.float32
    ).reshape(all_rows, model_width)
    grad_normed_two = grad_normed_two + jnp.einsum(
        "re,de->rd", grad_logits, w_ctrl, preferred_element_type=jnp.float32
    )
    grad_hidden_part, grad_gain_two = pull_two(grad_normed_two)
    grad_state = grad_output + grad_hidden_part
    grad_branch = grad_state.astype(jnp.bfloat16)
    grad_out = jnp.einsum("rd,re->de", attn_low, grad_branch, preferred_element_type=jnp.float32)
    grad_attn = jnp.einsum(
        "re,de->rd", grad_branch, w_out, preferred_element_type=jnp.float32
    ).astype(jnp.bfloat16)
    grad_attn_four = grad_attn.reshape(batch_rows, tok_rows, head_count, HEAD_DIM)
    delta = jnp.einsum("bqhd,bqhd->bhq", grad_attn_four.astype(jnp.float32), attn_four)
    keys_all = (
        lax.all_gather(send[0], "blk", axis=1, tiled=True),
        lax.all_gather(send[1], "blk", axis=1, tiled=True),
        lax.all_gather(send[2], "blk", axis=1, tiled=True),
    )
    key_all, value_all, seg_all = keys_all
    full_len = blk_count * tok_rows
    zero_grads = jnp.zeros((batch_rows, full_len, head_count, HEAD_DIM), jnp.float32)

    def back_step(block_at, state):
        start = block_at * tok_rows
        key_piece = lax.dynamic_slice_in_dim(key_all, start, tok_rows, 1)
        value_piece = lax.dynamic_slice_in_dim(value_all, start, tok_rows, 1)
        seg_piece = lax.dynamic_slice_in_dim(seg_all, start, tok_rows, 1)

        def back_visit(inner_state):
            query_sum, key_full, value_full = inner_state
            scores = scores_for(key_piece, seg_piece, start)
            probs = jnp.exp(scores - log_total[..., None])
            key_four = key_piece.reshape(batch_rows, tok_rows, head_count, HEAD_DIM)
            value_four = value_piece.reshape(batch_rows, tok_rows, head_count, HEAD_DIM)
            grad_probs = jnp.einsum(
                "bqhd,bkhd->bhqk", grad_attn_four, value_four, preferred_element_type=jnp.float32
            )
            grad_scores = (probs * (grad_probs - delta[..., None])).astype(jnp.bfloat16)
            query_sum = (
                query_sum
                + jnp.einsum(
                    "bhqk,bkhd->bhqd", grad_scores, key_four, preferred_element_type=jnp.float32
                )
                * 0.125
            )
            key_grad = (
                jnp.einsum(
                    "bhqk,bqhd->bkhd", grad_scores, query_four, preferred_element_type=jnp.float32
                )
                * 0.125
            )
            value_grad = jnp.einsum(
                "bhqk,bqhd->bkhd",
                probs.astype(jnp.bfloat16),
                grad_attn_four,
                preferred_element_type=jnp.float32,
            )
            key_full = lax.dynamic_update_slice_in_dim(key_full, key_grad, start, 1)
            value_full = lax.dynamic_update_slice_in_dim(value_full, value_grad, start, 1)
            return (query_sum, key_full, value_full)

        return lax.cond(start > last_pos, lambda inner_state: inner_state, back_visit, state)

    query_sum, key_full, value_full = lax.fori_loop(
        0,
        blk_count,
        back_step,
        (
            jnp.zeros((batch_rows, head_count, tok_rows, HEAD_DIM), jnp.float32),
            zero_grads,
            zero_grads,
        ),
    )
    key_share, value_share = (
        lax.psum_scatter(
            key_full.astype(jnp.bfloat16), "blk", scatter_dimension=1, tiled=True
        ).astype(jnp.float32),
        lax.psum_scatter(
            value_full.astype(jnp.bfloat16), "blk", scatter_dimension=1, tiled=True
        ).astype(jnp.float32),
    )
    grad_keys = key_share.reshape(all_rows, model_width).astype(jnp.bfloat16)
    grad_values = value_share.reshape(all_rows, model_width).astype(jnp.bfloat16)
    grad_queries = (
        jnp.transpose(query_sum, (0, 2, 1, 3)).reshape(all_rows, model_width).astype(jnp.bfloat16)
    )
    grad_query = jnp.einsum(
        "rd,re->de", normed_one, grad_queries, preferred_element_type=jnp.float32
    )
    grad_key = jnp.einsum("rd,re->de", normed_one, grad_keys, preferred_element_type=jnp.float32)
    grad_value = jnp.einsum(
        "rd,re->de", normed_one, grad_values, preferred_element_type=jnp.float32
    )
    grad_normed_one = jnp.einsum(
        "re,de->rd", grad_queries, w_query, preferred_element_type=jnp.float32
    )
    grad_normed_one = grad_normed_one + jnp.einsum(
        "re,de->rd", grad_keys, w_key, preferred_element_type=jnp.float32
    )
    grad_normed_one = grad_normed_one + jnp.einsum(
        "re,de->rd", grad_values, w_value, preferred_element_type=jnp.float32
    )
    grad_input_part, grad_gain_one = pull_one(grad_normed_one)
    grad_inputs = (grad_state + grad_input_part).astype(jnp.bfloat16).reshape(block_input.shape)
    (
        grad_gain_one,
        grad_query,
        grad_key,
        grad_value,
        grad_out,
        grad_gain_two,
        grad_ctrl,
        grad_in,
        grad_back,
    ) = lax.psum(
        (
            grad_gain_one,
            grad_query,
            grad_key,
            grad_value,
            grad_out,
            grad_gain_two,
            grad_ctrl,
            grad_in,
            grad_back,
        ),
        ("dp", "blk"),
    )
    return (
        output,
        grad_inputs,
        grad_gain_one,
        grad_query,
        grad_key,
        grad_value,
        grad_out,
        grad_gain_two,
        grad_ctrl,
        grad_in,
        grad_back,
    )


def solution(mesh):
    in_specs = (
        P(None, "dp", "blk", None),
        P("dp", "blk"),
        P(),
        P(),
        P(),
        P(),
        P(),
        P(),
        P(),
        P(),
        P(),
        P(None, "dp", "blk", None),
    )
    out_specs = (
        P(None, "dp", "blk", None),
        P(None, "dp", "blk", None),
        P(),
        P(),
        P(),
        P(),
        P(),
        P(),
        P(),
        P(),
        P(),
    )
    return jax.shard_map(local, mesh=mesh, in_specs=in_specs, out_specs=out_specs, check_vma=False)
```

profile of v0, /device:TPU:0, one launch (start us, length us, event | category | flops | bytes accessed | tf_op | source)
XLA Modules:
  0.0 981.3 jit_solution(11265039246994889223)
XLA Ops:
  14.1 2.4 copy.67
  16.6 2.8 convolution_convert_fusion.1
  21.9 4.2 convolution_convert_fusion.2
  26.1 3.1 copy.68
  33.1 6.4 all_gather.12
  39.5 39.4 %all-gather.3.cloned.1.call-done = bf16[8,1024,512]{1,2,0:T(8,128)(2,1)} async-done(((bf16[8,256,512]{1,2,0:T(8,128)(2,1)}), bf16[8,1024,512]{1,2,0:T(8,128)(2,1)}) %all-gather.3.cloned.1.call-update) | async-done | bytes 8388624 | tf_op jit(solution)/shard_map/all_gather | solution.py:80
  78.9 61.6 %all-gather.5.cloned.1.call-done = bf16[8,1024,512]{1,2,0:T(8,128)(2,1)} async-done(((bf16[8,256,512]{1,2,0:T(8,128)(2,1)}), bf16[8,1024,512]{1,2,0:T(8,128)(2,1)}) %all-gather.5.cloned.1.call-update) | async-done | bytes 8388624 | tf_op jit(solution)/shard_map/all_gather | solution.py:81
  140.4 82.9 %conditional.2 = (f32[8,8,256]{2,1,0:T(8,128)S(1)}, f32[8,8,256]{2,1,0:T(8,128)S(1)}, f32[8,8,256,64]{2,3,1,0:T(8,128)}, f32[8,8,256]{2,1,0:T(8,128)S(1)}) conditional(s32[]{:T(128)} %convert_element_type.140, (s32[]{:T(128)}, bf16[8,1024]{1,0:T(8,128)(2,1)S(1)}, bf16[8,256]{1,0:T(8,128)(2,1)S(1)}, bf16[8,1024,512]{1,2,0:T(8,128)(2,1)}, ...), branch_computations={%region_1.4_spmd, %region_4.5_spmd} | conditional | flops 4488151040 | bytes 233856032 | solution.py:99
  142.4 30.2 %fusion.2 = (f32[8,8,256]{2,1,0:T(8,128)S(1)}, f32[8,8,256,1024]{3,2,1,0:T(8,128)}) fusion(pred[8,256,1024]{2,1,0:T(8,128)(4,1)S(1)} %compare_and_fusion, bf16[8,1024,8,64]{1,3,2,0:T(8,128)(2,1)} %bitcast.171, bf16[8,256,8,64]{1,0,3,2:T(8,128)(2,1)} %get-tuple-element.513), kind=kOutput, calls=%fused_computation.3 | convolution fusion | flops 2197798912 | bytes 79757312 | tf_op jit(solution)/shard_map/cond/branch_0_fun/bqhd,bkhd->bhqk/dot_general | solution.py:65
  172.6 21.5 %fusion.4 = f32[8,8,256]{2,1,0:T(8,128)S(1)} fusion(f32[8,8,256,1024]{3,2,1,0:T(8,128)} %get-tuple-element.577, f32[8,8,256]{2,1,0:T(8,128)S(1)} %broadcast_maximum_fusion, pred[8,256,1024]{2,1,0:T(8,128)(4,1)S(1)} %compare_and_fusion), kind=kLoop, calls=%fused_computation.5 | loop fusion | flops 67092480 | bytes 69337088 | tf_op jit(solution)/shard_map/cond/branch_0_fun/reduce_sum | solution.py:97
  194.1 29.1 %fusion.5 = f32[8,8,256,64]{2,3,1,0:T(8,128)} fusion(bf16[8,1024,8,64]{1,3,2,0:T(8,128)(2,1)} %bitcast.176, f32[8,8,256,1024]{3,2,1,0:T(8,128)} %get-tuple-element.577, f32[8,8,256]{2,1,0:T(8,128)S(1)} %broadcast_maximum_fusion, pred[8,256,1024]{2,1,0:T(8,128)(4,1)S(1)} %compare_and_fusion), kind=kOutput, calls=%fused_computation.6 | convolution fusion | flops 2214592512 | bytes 81854464 | tf_op jit(solution)/shard_map/cond/branch_0_fun/bhqk,bkhd->bhqd/dot_general | solution.py:91
  223.3 2.8 bitcast_convert_fusion
  234.0 2.4 fusion.81
  240.1 2.7 fusion.54
  245.7 2.8 fusion.63
  249.5 5.6 multiply_reduce_fusion.1
  256.0 2.8 fusion.27
  260.9 2.6 convolution_convert_fusion
  263.5 2.9 copy.81
  271.1 2.4 multiply_reduce_fusion
  273.5 2.5 broadcast.234
  276.0 4.5 broadcast_in_dim.76
  280.5 4.5 broadcast_in_dim.76.clone
  285.0 45.2 %while.18 = (s32[]{:T(128)}, f32[8,8,256,64]{2,3,1,0:T(8,128)}, bf16[8,1024,8,64]{1,3,2,0:T(8,128)(2,1)}, bf16[8,1024,8,64]{1,3,2,0:T(8,128)(2,1)}, s32[]{:T(128...) while((s32[]{:T(128)}, f32[8,8,256,64]{2,3,1,0:T(8,128)}, ...), condition=%wide.region_13.14_spmd.clone, body=%wide.region_10.13_spmd.clone.sunk | while | flops 2731606528 | bytes 125655472 | solution.py:213
  285.1 44.9 %conditional.5 = ((f32[8,8,256,64]{2,3,1,0:T(8,128)}, bf16[8,1024,8,64]{1,3,2,0:T(8,128)(2,1)}, bf16[8,1024,8,64]{1,3,2,0:T(8,128)(2,1)})) conditional(s32[]{:T(128)} %convert_element_type.236, (s32[]{:T(128)}, s32[]{:T(128)}, bf16[8,1024]{1,0:T(8,128)(2,1)S(1)}, bf16[8,256]{1,0:T(8,128)(2,1)S(1)}, bf16[8,1024,512]{1,2,0:T(8,128)(2,1)}, ...), branch_computations={%region_11.11_spmd, %region_12.12_spmd} | conditional | flops 2731606528 | bytes 125654128 | solution.py:211
  285.2 4.0 constant_dynamic-slice_fusion
  289.2 9.7 fusion.73
  299.5 9.7 fusion.12
  309.2 5.6 multiply_add_fusion
  314.8 5.7 bitcast_dynamic-update-slice_fusion.1
  320.5 9.6 bitcast_dynamic-update-slice_fusion
  339.3 4.7 fusion.59
  346.3 4.6 fusion.56
  350.8 185.8 %reduce-scatter.5.cloned.1.call-done = bf16[8,256,8,64]{1,3,2,0:T(8,128)(2,1)} async-done(((bf16[8,1024,8,64]{1,3,2,0:T(8,128)(2,1)}), bf16[8,256,8,64]{1,3,2,0:T(8,128)(2,1)}) %reduce-scatter.5.cloned.1.call-update) | async-done | bytes 2097168 | tf_op jit(solution)/shard_map/reduce_scatter | solution.py:227
  536.6 2.9 copy.86
  541.5 70.1 %reduce-scatter.3.cloned.1.call-done = bf16[8,256,8,64]{1,3,2,0:T(8,128)(2,1)} async-done(((bf16[8,1024,8,64]{1,3,2,0:T(8,128)(2,1)}), bf16[8,256,8,64]{1,3,2,0:T(8,128)(2,1)}) %reduce-scatter.3.cloned.1.call-update) | async-done | bytes 2097168 | tf_op jit(solution)/shard_map/reduce_scatter | solution.py:224
  611.6 3.0 copy.85
  616.6 2.5 fusion.78
  624.1 3.1 fusion.75
  629.4 4.3 fusion.34
  633.7 41.2 %all-reduce.1 = (f32[512]{0:T(512)}, f32[512]{0:T(512)}, f32[512,2]{0,1:T(2,128)}) all-reduce(f32[512]{0:T(512)S(1)} %get-tuple-element.537, f32[512]{0:T(512)S(1)} %copy-done.51, f32[512,2]{0,1:T(2,128)S(1)} %fusion.80), channel_id=1, replica_groups=mesh['dp'=8,'blk'=4] {'dp','blk'}, use_global_device_ids=true, to_apply=%region_18.19 | all-reduce | flops 2048 | bytes 16384 | tf_op jit(solution)/shard_map/psum | solution.py:264
  674.9 5.7 fusion.29
  680.6 275.1 %all-reduce.5.cloned.1.call-done = (f32[512,512]{1,0:T(8,128)}, f32[512,512]{1,0:T(8,128)}, f32[512,512]{1,0:T(8,128)}, f32[512,512]{1,0:T(8,128)}, f32[2,512,2048]{2,1,0:T(8,128)}, /*index=5*/f32[2,2048,512]{2,1,0:T(8,128)}) async-done(((f32[512,512]{1,0:T(8,128)}, f32[512,512]{1,0:T(8,128)}, f32[512,512]{1,0:T(8,128)}, f32[512,512]{1,0:T(8,128)}, f32[2,512,2048]{2,1,0:T(8,128)}, ...) | async-done | bytes 20971536 | tf_op jit(solution)/shard_map/psum | solution.py:264
  955.7 2.4 copy.169
  958.1 2.9 copy.170
  963.3 2.4 copy.172
  965.7 4.2 copy.173
  970.9 3.4 copy.174
  (188 shorter events, 64.2 us)
Async XLA Ops:
  7.2 9.4 copy-start
  7.2 5.6 copy-start.38
  7.2 71.7 %all-gather.3.cloned.1.call-start = ((), (), s32[]{:S(2)}) async-start(), calls=%async_computation.2 | async-start | bytes 10485760 | tf_op jit(solution)/shard_map/all_gather | solution.py:80
  10.6 3.5 copy-start.41
  16.5 123.9 %all-gather.5.cloned.1.call-start = ((), (), s32[]{:S(2)}) async-start(), calls=%async_computation.3 | async-start | bytes 10485760 | tf_op jit(solution)/shard_map/all_gather | solution.py:81
  19.4 2.5 copy-start.52
  19.4 2.5 copy-start.36
  21.9 514.8 %reduce-scatter.5.cloned.1.call-start = ((), (), s32[]{:S(2)}) async-start(), calls=%async_computation.5 | async-start | bytes 10485760 | tf_op jit(solution)/shard_map/reduce_scatter | solution.py:227
  226.1 2.0 copy-start.2
  228.1 3.6 copy-start.49
  229.7 2.0 copy-start.5
  229.7 2.4 copy-start.50
  232.1 16.4 %copy-start.4 = (bf16[2048,512]{1,0:T(8,128)(2,1)}, bf16[2048,512]{1,0:T(8,128)(2,1)S(1)}, u32[]{:S(2)}) copy-start(bf16[2048,512]{1,0:T(8,128)(2,1)S(1)} %multiply_convert_fusion) | copy-start | bytes 6291460
  233.1 3.3 copy-start.12
  233.9 2.5 copy-start.24
  233.9 3.5 copy-start.23
  236.4 6.4 copy-start.34
  237.4 5.3 copy-start.10
  244.3 4.2 copy-start.26
  249.4 5.6 copy-start.45
  249.4 5.6 copy-start.6
  249.5 5.9 copy-start.14
  249.5 6.5 copy-start.19
  258.8 2.1 copy-start.7
  268.9 2.2 copy-start.13
  314.8 5.7 copy-start.30
  330.2 281.4 %reduce-scatter.3.cloned.1.call-start = ((), (), s32[]{:S(2)}) async-start(), calls=%async_computation.4 | async-start | bytes 10485760 | tf_op jit(solution)/shard_map/reduce_scatter | solution.py:224
  330.7 625.0 %all-reduce.5.cloned.1.call-start = ((), (), s32[]{:S(2)}) async-start(), calls=%async_computation.6 | async-start | bytes 41943040 | tf_op jit(solution)/shard_map/psum | solution.py:264
  331.0 2.3 copy-start.1
  332.4 3.3 copy-start.32
  335.6 3.6 copy-start.25
  335.6 3.6 copy-start.27
  339.3 4.8 copy-start.8
  339.3 4.8 copy-start.29
  344.0 2.2 copy-start.11
  344.0 2.2 copy-start.35
  611.6 5.0 copy-start.33
  615.3 3.9 copy-start.21
  621.4 2.7 copy-start.37
  624.1 3.1 copy-start.17
  624.1 3.1 copy-start.39
  627.2 2.2 copy-start.22
  627.2 2.2 copy-start.42
  629.4 4.3 copy-start.51
  629.4 45.5 %copy-start.44 = (f32[2,2,4,128]{3,1,2,0:T(2,128)S(1)}, f32[2,2,4,128]{3,1,2,0:T(2,128)}, u32[]{:S(2)}) copy-start(f32[2,2,4,128]{3,1,2,0:T(2,128)} %copy-done.43) | copy-start | bytes 24580
  955.7 10.0 %copy-start.20 = (f32[2,512,2048]{2,1,0:T(8,128)S(1)}, f32[2,512,2048]{2,1,0:T(8,128)}, u32[]{:S(2)}) copy-start(f32[2,512,2048]{2,1,0:T(8,128)} %get-tuple-element.752) | copy-start | bytes 25165828
  963.3 6.6 slice-start
  965.7 5.2 slice-start.1
  (12 other events, 16.9 us)
Sparse Core Ops, SparseCore 0:
  16.6 62.1 all-gather.2
  81.0 59.3 all-gather.4
  330.3 206.3 reduce-scatter.4
  539.8 71.6 reduce-scatter.2
  621.5 334.1 all-reduce.4
where the time goes:
time: 987 us; the launch traced here: 981 us
  waiting for transfers between devices  632 us (64%)
  matrix products  162 us (16%)
  local copies, waits for them, and re-layouts  78.8 us (8%)
  blocking collectives  47.6 us (5%)
  other arithmetic  45 us (5%)
  between operations  14.9 us (2%)
    psum x1, waiting for transfers between devices, local(): lax.psum((grad_gain_one, grad_query, grad_key, grad_value, grad_out, grad...  275 us
    reduce_scatter x1, waiting for transfers between devices, local(): lax.psum_scatter(value_full.astype(jnp.bfloat16), 'blk', scatter_dimensio...  186 us
    reduce_scatter x1, waiting for transfers between devices, local(): lax.psum_scatter(key_full.astype(jnp.bfloat16), 'blk', scatter_dimension=...  70.1 us
    all_gather x1, waiting for transfers between devices, local(): value_piece = lax.all_gather(send[1], 'blk', axis=1, tiled=True)  61.6 us
    unnamed x123, local copies, waits for them, and re-layouts  43.8 us
    psum x1, blocking collectives, local(): lax.psum((grad_gain_one, grad_query, grad_key, grad_value, grad_out, grad...  41.2 us
    dot_general x2, matrix products, scores_for(): jnp.einsum('bqhd,bkhd->bhqk', query_four, key_four, preferred_element_typ...  40 us
    all_gather x1, waiting for transfers between devices, local(): key_piece = lax.all_gather(send[0], 'blk', axis=1, tiled=True)  39.4 us
  transfers between devices with their start and end apart: 5, of which 5 were waited for; matrix products, arithmetic and copies ran while one was open for 5% of the time, Pallas kernels for 0%

commit v1 on v0

v1 whole, which is shorter than its diff:
```python
import functools

import jax
import jax.numpy as jnp
from jax import lax
from jax.experimental import pallas as pl
from jax.experimental.pallas import tpu as pltpu
from jax.sharding import PartitionSpec as P

HEAD_DIM = 64
GROUP = 32
EPSILON = 1e-05
BLOCK = 256
CHUNK = 512
SCALE = 0.125
MASKED = -1e30
VMEM_LIMIT = 60 * 1024 * 1024
BF = jnp.bfloat16
F32 = jnp.float32


def dot(a, b, ca, cb):
    return lax.dot_general(a, b, (((ca,), (cb,)), ((), ())), preferred_element_type=F32)


def nn(a, b):
    return dot(a, b, 1, 0)


def nt(a, b):
    return dot(a, b, 1, 1)


def tn(a, b):
    return dot(a, b, 0, 0)


def key_range(packed, i):
    low = max(0, i * BLOCK - BLOCK - BLOCK // 2) if packed else 0
    return low, (i + 1) * BLOCK - low


def head_masks():
    lane = lax.broadcasted_iota(jnp.int32, (1, 2 * HEAD_DIM), 1)
    first = (lane < HEAD_DIM).astype(F32).astype(BF)
    return first, (lane >= HEAD_DIM).astype(F32).astype(BF)


def group_match(rows, tokens):
    row = lax.broadcasted_iota(jnp.int32, (rows, tokens), 0)
    col = lax.broadcasted_iota(jnp.int32, (rows, tokens), 1)
    return (row % (tokens // GROUP)) == (col // GROUP)


def fill_bias(bias_ref, start_ref, packed, i):
    low, count = key_range(packed, i)
    q_pos = i * BLOCK + lax.broadcasted_iota(jnp.int32, (1, BLOCK), 1)
    if packed:
        k_pos = low + lax.broadcasted_iota(jnp.int32, (count, BLOCK), 0)
        allowed = (k_pos <= q_pos) & (k_pos >= start_ref[...])
        bias_ref[0:count, :] = jnp.where(allowed, 0.0, MASKED)
    else:
        k_pos = i * BLOCK + lax.broadcasted_iota(jnp.int32, (BLOCK, BLOCK), 0)
        bias_ref[0:BLOCK, :] = jnp.where(k_pos <= q_pos, 0.0, MASKED)


def add_bias(scores, bias_ref, packed, count):
    if packed:
        return scores + bias_ref[0:count, :]
    last = scores[count - BLOCK :, :] + bias_ref[0:BLOCK, :]
    if count == BLOCK:
        return last
    return jnp.concatenate([scores[: count - BLOCK, :], last], axis=0)


def rms(values):
    return lax.rsqrt(jnp.mean(values * values, axis=-1, keepdims=True) + EPSILON)


def forward_kernel(
    packed, blocks, x_ref, start_ref, g1_ref, wqkv_ref, wkvt_ref, wo_ref, g2_ref, wc_ref,
    q_ref, k_ref, v_ref, kt_ref, ob_ref, lse_ref, h_ref, gate_ref, mg_ref,
    k_all, vt_all, bias,
):
    step = pl.program_id(0)
    width = x_ref.shape[1]
    pairs = width // (2 * HEAD_DIM)
    x = x_ref[...].astype(F32)
    n1 = (x * rms(x) * g1_ref[...]).astype(BF)
    qkv = nn(n1, wqkv_ref[...]).astype(BF)
    q_ref[...] = qkv[:, :width]
    k_ref[...] = qkv[:, width : 2 * width]
    v_ref[...] = qkv[:, 2 * width :]
    kvt = nt(wkvt_ref[...], n1).astype(BF)
    kt_ref[...] = kvt[:width]
    at = pl.multiple_of(step * BLOCK, BLOCK)
    k_all[pl.ds(at, BLOCK), :] = qkv[:, width : 2 * width]
    vt_all[:, pl.ds(at, BLOCK)] = kvt[width:]
    masks = head_masks()

    def attend(i):
        low, count = key_range(packed, i)
        fill_bias(bias, start_ref, packed, i)

        def pair(hp, carry):
            lanes = pl.ds(pl.multiple_of(hp * 2 * HEAD_DIM, 2 * HEAD_DIM), 2 * HEAD_DIM)
            q_pair = q_ref[:, lanes]
            k_pair = k_all[low : low + count, lanes]
            for h in range(2):
                scores = add_bias(nt(k_pair, q_pair * masks[h]), bias, packed, count)
                top = jnp.max(scores, axis=0, keepdims=True)
                p = jnp.exp((scores - top) * SCALE)
                total = jnp.sum(p, axis=0, keepdims=True)
                rows = pl.ds(pl.multiple_of(hp * 2 * HEAD_DIM + h * HEAD_DIM, HEAD_DIM), HEAD_DIM)
                o = nn(vt_all[rows, low : low + count], p.astype(BF))
                ob_ref[rows, :] = (o * (1.0 / total)).astype(BF)
                lse_ref[pl.ds(hp * 2 + h, 1), :] = top * SCALE + jnp.log(total)
            return carry

        lax.fori_loop(0, pairs, pair, 0)

    for i in range(blocks):
        pl.when(step == i)(functools.partial(attend, i))

    h = x + tn(ob_ref[...], wo_ref[...])
    h_ref[...] = h
    n2 = (h * rms(h) * g2_ref[...]).astype(BF)
    logits = nt(wc_ref[...], n2)
    rows = logits.shape[0]
    match = group_match(rows, BLOCK)
    logits = jnp.where(match, logits, MASKED)
    e = jnp.where(match, jnp.exp(logits - jnp.max(logits, axis=1, keepdims=True)), 0.0)
    gate = e / jnp.sum(e, axis=1, keepdims=True)
    gate_ref[...] = gate
    mg = nn(gate.astype(BF), n2).astype(BF).astype(F32)
    half = rows // mg_ref.shape[0]
    for j in range(mg_ref.shape[0]):
        mg_ref[j] = mg[j * half : (j + 1) * half]


def gelu_both(u):
    c = 0.7978845608028654
    t = jnp.tanh(c * (u + 0.044715 * (u * u * u)))
    act = 0.5 * u * (1.0 + t)
    slope = 0.5 * (1.0 + t) + 0.5 * u * (1.0 - t * t) * (c * (1.0 + 3 * 0.044715 * (u * u)))
    return act, slope


def experts_kernel(
    micros, blocks, *refs,
):
    mgs, gates = refs[:micros], refs[micros : 2 * micros]
    cot_ref, win_ref, wback_ref = refs[2 * micros : 2 * micros + 3]
    eo_ref, dmg_ref, mgb_ref, deob_ref, deo = refs[2 * micros + 3 :]
    e, c = pl.program_id(0), pl.program_id(1)
    per = BLOCK // GROUP
    n_exp = deo.shape[0]

    @pl.when((e == 0) & (c == 0))
    def _():
        for m in range(micros):
            for i in range(blocks):
                part = gates[m][:, i * BLOCK : (i + 1) * BLOCK].astype(BF)
                d = nn(part, cot_ref[m, i * BLOCK : (i + 1) * BLOCK, :])
                for j in range(n_exp):
                    at = (m * blocks + i) * per
                    deo[j, at : at + per, :] = d[j * per : (j + 1) * per]

    mg = jnp.concatenate([r[0] for r in mgs], axis=0).astype(BF)
    deo_b = deo[e].astype(BF)

    @pl.when(c == 0)
    def _():
        mgb_ref[0] = mg
        deob_ref[0] = deo_b

    act, slope = gelu_both(nn(mg, win_ref[0]))
    eo_part = nn(act.astype(BF), wback_ref[0])
    du = (slope * nt(deo_b, wback_ref[0])).astype(BF)
    dmg_part = nt(du, win_ref[0])

    @pl.when(c == 0)
    def _():
        eo_ref[0] = eo_part
        dmg_ref[0] = dmg_part

    @pl.when(c > 0)
    def _():
        eo_ref[0] += eo_part
        dmg_ref[0] += dmg_part


def backward_kernel(
    packed, blocks, first, x_ref, cot_ref, h_ref, gate_ref, eo_ref, dmg_ref, ob_ref, lse_ref,
    q_ref, k_ref, v_ref, kt_ref, start_ref, g1_ref, g2_ref, wc_ref, wqt_ref, wk_ref, wv_ref,
    wo_ref, *refs,
):
    if first:
        before, refs = None, refs
    else:
        before, refs = refs[:4], refs[4:]
    act_ref, gi_ref, gq_ref, gkv_ref, go_ref, small_ref, dk_acc, dv_acc, dqt, dob, dobt, delta, bias = refs
    step = pl.program_id(0)
    width = x_ref.shape[1]
    pairs = width // (2 * HEAD_DIM)
    heads = width // HEAD_DIM

    @pl.when(step == 0)
    def _():
        dk_acc[...] = jnp.zeros_like(dk_acc)
        dv_acc[...] = jnp.zeros_like(dv_acc)
        if first:
            for r in (gq_ref, gkv_ref, go_ref, small_ref):
                r[...] = jnp.zeros_like(r)
        else:
            for r, b in zip((gq_ref, gkv_ref, go_ref, small_ref), before):
                r[...] = b[...]

    h = h_ref[...]
    cot_b = cot_ref[...]
    dout = cot_b.astype(F32)
    r2 = rms(h)
    z = h * r2
    n2 = (z * g2_ref[...]).astype(BF)
    gate = gate_ref[...]
    rows = gate.shape[0]
    gate_b = gate.astype(BF)
    gate_low = (gate - gate_b.astype(F32)).astype(BF)
    eo = jnp.concatenate([eo_ref[j] for j in range(eo_ref.shape[0])], axis=0)
    dmg = jnp.concatenate([dmg_ref[j] for j in range(dmg_ref.shape[0])], axis=0).astype(BF)
    eo_b = eo.astype(BF)
    eo_low = (eo - eo_b.astype(F32)).astype(BF)
    mixed = tn(
        jnp.concatenate([gate_b, gate_low, gate_b], axis=0),
        jnp.concatenate([eo_b, eo_b, eo_low], axis=0),
    )
    act_ref[...] = (h + mixed).astype(BF)
    dw2 = nt(jnp.concatenate([eo_b, eo_low], axis=0), cot_b)
    dw = dw2[:rows] + dw2[rows:] + nt(dmg, n2)
    wdw = gate * dw
    dlog = (wdw - gate * jnp.sum(wdw, axis=1, keepdims=True)).astype(BF)
    dn2 = tn(
        jnp.concatenate([gate_b, dlog], axis=0),
        jnp.concatenate([dmg, wc_ref[...]], axis=0),
    )
    small_ref[0:rows, :] += nn(dlog, n2)
    dg2 = dn2 * z
    small_ref[rows : rows + 1, :] += jnp.sum(dg2, axis=0, keepdims=True)
    a = dn2 * g2_ref[...]
    dh = dout + r2 * (a - z * jnp.mean(a * z, axis=-1, keepdims=True))
    da = dh.astype(BF)
    dob[...] = nt(da, wo_ref[...]).astype(BF)
    dobt[...] = nt(wo_ref[...], da).astype(BF)
    go_ref[...] += nn(ob_ref[...], da)
    prod = dobt[...].astype(F32) * ob_ref[...].astype(F32)
    for hd in range(heads):
        delta[hd : hd + 1, :] = jnp.sum(
            prod[hd * HEAD_DIM : (hd + 1) * HEAD_DIM], axis=0, keepdims=True
        )
    masks = head_masks()

    def attend(i):
        low, count = key_range(packed, i)
        fill_bias(bias, start_ref, packed, i)
        keys = slice(low, low + count)

        def pair(hp, carry):
            lanes = pl.ds(pl.multiple_of(hp * 2 * HEAD_DIM, 2 * HEAD_DIM), 2 * HEAD_DIM)
            q_pair, dob_pair = q_ref[:, lanes], dob[:, lanes]
            k_pair, v_pair = k_ref[keys, lanes], v_ref[keys, lanes]
            dk_sum = dv_sum = None
            for h in range(2):
                qm, dm = q_pair * masks[h], dob_pair * masks[h]
                scores = add_bias(nt(k_pair, qm), bias, packed, count)
                p = jnp.exp(scores * SCALE - lse_ref[pl.ds(hp * 2 + h, 1), :])
                dp = nt(v_pair, dm)
                ds = (p * (dp - delta[pl.ds(hp * 2 + h, 1), :])).astype(BF)
                rows_h = pl.ds(pl.multiple_of(hp * 2 * HEAD_DIM + h * HEAD_DIM, HEAD_DIM), HEAD_DIM)
                dqt[rows_h, :] = (nn(kt_ref[rows_h, keys], ds) * SCALE).astype(BF)
                dk_part, dv_part = nn(ds, qm), nn(p.astype(BF), dm)
                dk_sum = dk_part if dk_sum is None else dk_sum + dk_part
                dv_sum = dv_part if dv_sum is None else dv_sum + dv_part
            dk_acc[keys, lanes] += dk_sum
            dv_acc[keys, lanes] += dv_sum
            return carry

        lax.fori_loop(0, pairs, pair, 0)

    for i in range(blocks):
        pl.when(step == blocks - 1 - i)(functools.partial(attend, i))

    at = pl.ds(pl.multiple_of((blocks - 1 - step) * BLOCK, BLOCK), BLOCK)
    dk = (dk_acc[at, :] * SCALE).astype(BF)
    dv = dv_acc[at, :].astype(BF)
    x = x_ref[...].astype(F32)
    r1 = rms(x)
    z1 = x * r1
    n1 = (z1 * g1_ref[...]).astype(BF)
    dq_t = dqt[...]
    dn1 = tn(dq_t, wqt_ref[...]) + nt(dk, wk_ref[...]) + nt(dv, wv_ref[...])
    gq_ref[...] += nn(dq_t, n1)
    gkv_ref[...] += tn(n1, jnp.concatenate([dk, dv], axis=1))
    small_ref[rows + 8 : rows + 9, :] += jnp.sum(dn1 * z1, axis=0, keepdims=True)
    b = dn1 * g1_ref[...]
    gi = dh + r1 * (b - z1 * jnp.mean(b * z1, axis=-1, keepdims=True))
    gi_ref[...] = gi.astype(BF)


def whole(shape):
    return pl.BlockSpec(shape, lambda *_: (0,) * len(shape))


def params(flag=None):
    return pltpu.CompilerParams(vmem_limit_bytes=VMEM_LIMIT)


def forward_call(packed, x, start, g1, wqkv, wkvt, wo, g2, wc):
    length, width = x.shape
    blocks = length // BLOCK
    rows = wc.shape[0]
    per = BLOCK // GROUP
    experts = rows // per
    row_block = pl.BlockSpec((BLOCK, width), lambda i: (i, 0))
    col_block = pl.BlockSpec((width, BLOCK), lambda i: (0, i))
    out = lambda shape, dtype: jax.ShapeDtypeStruct(shape, dtype)
    return pl.pallas_call(
        functools.partial(forward_kernel, packed, blocks),
        grid=(blocks,),
        in_specs=[
            row_block, pl.BlockSpec((1, BLOCK), lambda i: (0, i)), whole(g1.shape), whole(wqkv.shape),
            whole(wkvt.shape), whole(wo.shape), whole(g2.shape), whole(wc.shape),
        ],
        out_specs=[
            row_block, row_block, row_block, col_block, col_block,
            pl.BlockSpec((width // HEAD_DIM, BLOCK), lambda i: (0, i)),
            row_block,
            pl.BlockSpec((rows, BLOCK), lambda i: (0, i)),
            pl.BlockSpec((experts, per, width), lambda i: (0, i, 0)),
        ],
        out_shape=[
            out((length, width), BF), out((length, width), BF), out((length, width), BF),
            out((width, length), BF), out((width, length), BF),
            out((width // HEAD_DIM, length), F32),
            out((length, width), F32),
            out((rows, length), F32),
            out((experts, length // GROUP, width), F32),
        ],
        scratch_shapes=[
            pltpu.VMEM((length, width), BF), pltpu.VMEM((width, length), BF),
            pltpu.VMEM((length, BLOCK), F32),
        ],
        compiler_params=params(),
        name="attention_forward",
    )(x, start, g1, wqkv, wkvt, wo, g2, wc)


def experts_call(mgs, gates, cot, w_in, w_back):
    micros, length, width = cot.shape
    experts, _, ff = w_in.shape
    blocks = length // BLOCK
    groups = micros * length // GROUP
    chunk = min(CHUNK, ff)
    by_expert = lambda n: pl.BlockSpec((1, n, width), lambda e, c: (e, 0, 0))
    out = lambda dtype: jax.ShapeDtypeStruct((experts, groups, width), dtype)
    return pl.pallas_call(
        functools.partial(experts_kernel, micros, blocks),
        grid=(experts, ff // chunk),
        in_specs=[by_expert(length // GROUP)] * micros
        + [whole(gates[0].shape)] * micros
        + [
            whole(cot.shape),
            pl.BlockSpec((1, width, chunk), lambda e, c: (e, 0, c)),
            pl.BlockSpec((1, chunk, width), lambda e, c: (e, c, 0)),
        ],
        out_specs=[by_expert(groups)] * 4,
        out_shape=[out(F32), out(F32), out(BF), out(BF)],
        scratch_shapes=[pltpu.VMEM((experts, groups, width), F32)],
        compiler_params=params(),
        name="experts",
    )(*mgs, *gates, cot, w_in, w_back)


def backward_call(packed, micro, x, cot, h, gate, eo, dmg, ob, lse, q, k, v, kt, start, g1, g2, wc,
                  wqt, wk, wv, wo, before):
    length, width = x.shape
    blocks = length // BLOCK
    rows = wc.shape[0]
    per = BLOCK // GROUP
    experts = rows // per
    heads = width // HEAD_DIM
    first = before is None
    back = lambda i: blocks - 1 - i
    row_block = pl.BlockSpec((BLOCK, width), lambda i: (back(i), 0))
    col_block = lambda n: pl.BlockSpec((n, BLOCK), lambda i: (0, back(i)))
    group_block = pl.BlockSpec((experts, per, width), lambda i: (0, micro * blocks + back(i), 0))
    sums = [(width, width), (width, 2 * width), (width, width), (rows + 16, width)]
    out = lambda shape, dtype: jax.ShapeDtypeStruct(shape, dtype)
    return pl.pallas_call(
        functools.partial(backward_kernel, packed, blocks, first),
        grid=(blocks,),
        in_specs=[
            row_block, row_block, row_block, col_block(rows), group_block, group_block,
            col_block(width), col_block(heads), row_block, whole(k.shape), whole(v.shape),
            whole(kt.shape), col_block(1), whole(g1.shape), whole(g2.shape), whole(wc.shape),
            whole(wqt.shape), whole(wk.shape), whole(wv.shape), whole(wo.shape),
        ] + ([] if first else [whole(s) for s in sums]),
        out_specs=[row_block, row_block] + [whole(s) for s in sums],
        out_shape=[out((length, width), BF), out((length, width), BF)] + [out(s, F32) for s in sums],
        scratch_shapes=[
            pltpu.VMEM((length, width), F32), pltpu.VMEM((length, width), F32),
            pltpu.VMEM((width, BLOCK), BF), pltpu.VMEM((BLOCK, width), BF),
            pltpu.VMEM((width, BLOCK), BF), pltpu.VMEM((heads, BLOCK), F32),
            pltpu.VMEM((length, BLOCK), F32),
        ],
        compiler_params=params(),
        name="attention_backward",
    )(x, cot, h, gate, eo, dmg, ob, lse, q, k, v, kt, start, g1, g2, wc, wqt, wk, wv, wo,
      *([] if first else before))


def swap(value, axis, size, distance, stride=1):
    n = lax.axis_size(axis)
    return lax.ppermute(value, axis, [(i, i ^ (distance * stride)) for i in range(n)])


def take(value, index, axis=0):
    return lax.dynamic_index_in_dim(value, index, axis, keepdims=False)


def trade(pieces, axis, size, me):
    got = lax.dynamic_update_index_in_dim(jnp.zeros_like(pieces), take(pieces, me), me, 0)
    for d in range(1, size):
        came = swap(take(pieces, me ^ d), axis, size, d)
        got = lax.dynamic_update_index_in_dim(got, came, me ^ d, 0)
    return got


def local(block_input, segment_ids, gain_one, w_query, w_key, w_value, w_out, gain_two, w_ctrl,
          w_in, w_back, cotangent):
    micros, seqs, rows, width = block_input.shape
    experts, _, ff = w_in.shape
    nb = lax.axis_size("blk")
    nd = lax.axis_size("dp")
    blk, dp = lax.axis_index("blk"), lax.axis_index("dp")
    length = nb * rows
    per = BLOCK // GROUP

    def to_sequences(a):
        return trade(a, "blk", nb, blk).reshape(length, -1)

    def to_blocks(a):
        return trade(a.reshape(nb, rows, width), "blk", nb, blk)

    seg = to_sequences(segment_ids).reshape(1, length)
    start = jnp.sum((seg.reshape(length, 1) < seg).astype(jnp.int32), axis=0, keepdims=True)
    g1, g2 = gain_one.reshape(1, width), gain_two.reshape(1, width)
    wqkv = jnp.concatenate([w_query, w_key, w_value], axis=1)
    wkvt = jnp.concatenate([w_key, w_value], axis=1).T
    wqt = w_query.T
    wc = jnp.repeat(w_ctrl.T, per, axis=0)

    xs = [to_sequences(block_input[m]) for m in range(micros)]
    fwd = [
        forward_call(m > 0, xs[m], start, g1, wqkv, wkvt, w_out, g2, wc) for m in range(micros)
    ]
    cots = jnp.stack([to_sequences(cotangent[m]) for m in range(micros)])
    eo, dmg, mgb, deob = experts_call([f[8] for f in fwd], [f[7] for f in fwd], cots, w_in, w_back)

    grads = None
    acts, gis = [], []
    for m in range(micros):
        q, k, v, kt, ob, lse, h, gate, _ = fwd[m]
        act, gi, *grads = backward_call(
            m > 0, m, xs[m], cots[m], h, gate, eo, dmg, ob, lse, q, k, v, kt, start, g1, g2, wc,
            wqt, w_key, w_value, w_out, grads,
        )
        acts.append(to_blocks(act))
        gis.append(to_blocks(gi))
    gqt, gkv, go, small = grads

    slices = nb
    e_mine = blk % experts
    pair = jnp.stack([mgb, deob])
    keep = take(pair, e_mine, 1)
    came = swap(take(pair, 1 - e_mine, 1), "blk", nb, 1)
    mine = jnp.stack([keep, came])
    sets = [mine]
    for far in (0, 1):
        for d in range(0, nb, 2):
            if far == 0 and d == 0:
                continue
            if far:
                moved = lax.ppermute(
                    mine, ("dp", "blk"),
                    [(i * nb + j, (i ^ 1) * nb + (j ^ d)) for i in range(nd) for j in range(nb)],
                )
            else:
                moved = swap(mine, "blk", nb, d)
            sets.append(moved)
    both = jnp.stack(sets)
    mg_all = both[:, :, 0].reshape(-1, width)
    deo_all = both[:, :, 1].reshape(-1, width)
    part = (dp % 2) * (nb // 2) + blk // 2
    cut = ff // slices
    win_cut = lax.dynamic_slice(w_in, (e_mine, 0, part * cut), (1, width, cut))[0]
    wback_cut = lax.dynamic_slice(w_back, (e_mine, part * cut, 0), (1, cut, width))[0]
    act, slope = gelu_both(nn(mg_all, win_cut))
    du = (slope * nt(deo_all, wback_cut)).astype(BF)
    g_in = tn(mg_all, du)
    g_back = tn(act.astype(BF), deo_all)
    planes = nd // 2
    plane = dp // 2

    def plane_swap(a, d):
        return lax.ppermute(a, "dp", [(i, i ^ (2 * d)) for i in range(nd)])

    ours = jnp.stack([g_in, g_back]).reshape(2, planes, width // planes, cut).astype(F32)
    total = take(ours, plane, 1)
    for d in range(1, planes):
        total = total + plane_swap(take(ours, plane ^ d, 1).astype(BF), d).astype(F32)
    got = jnp.zeros((planes,) + total.shape, BF)
    got = lax.dynamic_update_index_in_dim(got, total.astype(BF), plane, 0)
    for d in range(1, planes):
        got = lax.dynamic_update_index_in_dim(got, plane_swap(total.astype(BF), d), plane ^ d, 0)
    piece = jnp.transpose(got, (1, 0, 2, 3)).reshape(2, width, cut)
    full = jnp.zeros((2 * nb, 2, width, cut), BF)
    place = (dp % 2) * nb + blk
    full = lax.dynamic_update_index_in_dim(full, piece, place, 0)
    for far in (0, 1):
        for d in range(nb):
            if far == 0 and d == 0:
                continue
            moved = lax.ppermute(
                piece, ("dp", "blk"),
                [(i * nb + j, (i ^ far) * nb + (j ^ d)) for i in range(nd) for j in range(nb)],
            )
            full = lax.dynamic_update_index_in_dim(full, moved, ((dp % 2) ^ far) * nb + (blk ^ d), 0)
    full = full.reshape(2, nb // 2, 2, 2, width, cut).astype(F32)
    grad_in = jnp.transpose(full[:, :, :, 0], (2, 3, 0, 1, 4)).reshape(experts, width, ff)
    grad_back = jnp.transpose(full[:, :, :, 1], (2, 0, 1, 3, 4)).reshape(experts, ff, width)

    flat = jnp.concatenate([gqt, gkv[:, :width], gkv[:, width:], go], axis=0)
    def reduce_scatter(a, size, me, move):
        a = a.reshape(size, a.shape[0] // size, width)
        total = take(a, me)
        for d in range(1, size):
            total = total + move(take(a, me ^ d).astype(BF), d).astype(F32)
        return total

    def gather(a, size, me, move):
        got = jnp.zeros((size,) + a.shape, a.dtype)
        got = lax.dynamic_update_index_in_dim(got, a, me, 0)
        for d in range(1, size):
            got = lax.dynamic_update_index_in_dim(got, move(a, d), me ^ d, 0)
        return got.reshape(-1, width)

    def add_all(a, size, move):
        total = a
        for d in range(1, size):
            total = total + move(a, d)
        return total

    by_core = lambda a, d: swap(a, "blk", nb, d)
    def by_plane(a, d):
        far, d = d % 2, (d // 2) * 2
        return lax.ppermute(
            a, ("dp", "blk"),
            [(i * nb + j, (i ^ far) * nb + (j ^ d)) for i in range(nd) for j in range(nb)],
        )
    stages = [(2, blk % 2, by_core), (nb, (blk // 2) * 2 + dp % 2, by_plane), (planes, plane, plane_swap)]
    for s in stages:
        flat = reduce_scatter(flat, *s)
        small = add_all(small, s[0], s[2])
    flat = flat.astype(BF)
    for s in reversed(stages):
        flat = gather(flat, *s)
    flat = flat.astype(F32).reshape(4, width, width)
    ctrl = jnp.sum(small[: experts * per].reshape(experts, per, width), axis=1).T
    return (
        jnp.stack(acts), jnp.stack(gis), small[experts * per + 8], flat[0].T, flat[1], flat[2],
        flat[3], small[experts * per], ctrl, grad_in, grad_back,
    )


def solution(mesh):
    data = P(None, "dp", "blk", None)
    in_specs = (data, P("dp", "blk")) + (P(),) * 9 + (data,)
    out_specs = (data, data) + (P(),) * 9
    return jax.shard_map(local, mesh=mesh, in_specs=in_specs, out_specs=out_specs, check_vma=False)
```

time: 987 us -> 542 us (0.55)
  waiting for transfers between devices: 632 us -> 207 us
  matrix products: 162 us -> 5.93 us
  Pallas kernels: 0 us -> 136 us
  starting transfers between devices: 0.41 us -> 66.9 us
  blocking collectives: 47.6 us -> 0 us
  other arithmetic: 45 us -> 25.5 us
  local copies, waits for them, and re-layouts: 78.8 us -> 93.9 us
  between operations: 14.9 us -> 2.02 us
    psum x1 -> x0, waiting for transfers between devices: 275 us -> none  [local(): lax.psum((grad_gain_one, grad_query, grad_key, grad_value, grad_out, grad...]
    reduce_scatter x2 -> x0, waiting for transfers between devices: 256 us -> none  [the longest x1 186 us: local(): lax.psum_scatter(value_full.astype(jnp.bfloat16), 'blk', scatter_dimensio...]
    ppermute x0 -> x65, waiting for transfers between devices: none -> 207 us  [the longest x7 62.3 us: local(): lax.ppermute(piece, ('dp', 'blk'), [(i * nb + j, (i ^ far) * nb + (j ^ d)...]
    dot_general x34 -> x3, matrix products: 162 us -> 5.93 us  [dot(): lax.dot_general(a, b, (((ca,), (cb,)), ((), ())), preferred_element_type=...]
    pallas_call x0 -> x5, Pallas kernels: none -> 136 us  [the longest x2 70.1 us: backward_call(): pl.pallas_call(functools.partial(backward_kernel, packed, blocks, first),...]
    all_gather x2 -> x0, waiting for transfers between devices: 101 us -> none  [the longest x1 61.6 us: local(): value_piece = lax.all_gather(send[1], 'blk', axis=1, tiled=True)]
    ppermute x0 -> x65, starting transfers between devices: none -> 66.9 us  [the longest x15 27.2 us: plane_swap(): return lax.ppermute(a, 'dp', [(i, i ^ 2 * d) for i in range(nd)])]
    psum x1 -> x0, blocking collectives: 41.2 us -> none  [local(): lax.psum((grad_gain_one, grad_query, grad_key, grad_value, grad_out, grad...]
  transfers between devices with their start and end apart: 5 -> 65, of which waited for: 5 -> 23; matrix products, arithmetic and copies ran while one was open for 5% -> 20% of each run, Pallas kernels for 0% -> 10%
where the time goes in v1:
time: 542 us; the launch traced here: 538 us
  waiting for transfers between devices  207 us (38%)
  Pallas kernels  136 us (25%)
  local copies, waits for them, and re-layouts  93.9 us (17%)
  starting transfers between devices  66.9 us (12%)
  other arithmetic  25.5 us (5%)
  matrix products  5.93 us (1%)
    pallas_call x2, Pallas kernels, backward_call(): pl.pallas_call(functools.partial(backward_kernel, packed, blocks, first),...  70.1 us
    ppermute x7, waiting for transfers between devices, local(): lax.ppermute(piece, ('dp', 'blk'), [(i * nb + j, (i ^ far) * nb + (j ^ d)...  62.3 us
    pallas_call x2, Pallas kernels, forward_call(): pl.pallas_call(functools.partial(forward_kernel, packed, blocks), grid=(b...  54.9 us
    ppermute x32, waiting for transfers between devices, swap(): lax.ppermute(value, axis, [(i, i ^ distance * stride) for i in range(n)])  54.4 us
    ppermute x9, waiting for transfers between devices, by_plane(): lax.ppermute(a, ('dp', 'blk'), [(i * nb + j, (i ^ far) * nb + (j ^ d)) fo...  51 us
    ppermute x15, waiting for transfers between devices, plane_swap(): return lax.ppermute(a, 'dp', [(i, i ^ 2 * d) for i in range(nd)])  39.6 us
    ppermute x15, starting transfers between devices, plane_swap(): return lax.ppermute(a, 'dp', [(i, i ^ 2 * d) for i in range(nd)])  27.2 us
    ppermute x32, starting transfers between devices, swap(): lax.ppermute(value, axis, [(i, i ^ distance * stride) for i in range(n)])  20.6 us
  transfers between devices with their start and end apart: 65, of which 23 were waited for; matrix products, arithmetic and copies ran while one was open for 20% of the time, Pallas kernels for 10%

profile of v1, /device:TPU:0, one launch (start us, length us, event | category | flops | bytes accessed | tf_op | source)
XLA Modules:
  0.0 538.0 jit_solution(14973519690067202589)
XLA Ops:
  2.1 2.6 collective-permute-start.8
  4.8 2.8 fusion.77
  15.2 2.6 dynamic-slice_bitcast_fusion.21
  23.8 2.2 maximum_bitcast_fusion.wkvt_ref
  31.9 4.9 collective-permute-done.10
  40.8 7.2 %collective-permute-done.1 = bf16[256,512]{1,0:T(8,128)(2,1)} collective-permute-done((bf16[256,512]{1,0:T(8,128)(2,1)}, bf16[256,512]{1,0:T(8,128)(2,1)}, u32[]{:S(2)}, u32[]{:S(2)}) %collective-permute-start.1) | collective-permute-done | bytes 262176 | tf_op jit(solution)/shard_map/ppermute | solution.py:423
  52.0 7.1 %collective-permute-done.13 = bf16[256,512]{1,0:T(8,128)(2,1)S(1)} collective-permute-done((bf16[256,512]{1,0:T(8,128)(2,1)}, bf16[256,512]{1,0:T(8,128)(2,1)S(1)}, u32[]{:S(2)}, u32[]{:S(2)}) %collective-permute-start.13) | collective-permute-done | bytes 262176 | tf_op jit(solution)/shard_map/ppermute | solution.py:423
  60.1 28.7 %attention_forward.2 = (bf16[1024,512]{1,0:T(8,128)(2,1)}, bf16[1024,512]{1,0:T(8,128)(2,1)}, bf16[1024,512]{1,0:T(8,128)(2,1)}, bf16[512,1024]{1,0:T(8,128)(2,1...) custom-call(bf16[1024,512]{1,0:T(8,128)(2,1)} %bitcast.340, ...), custom_call_target="tpu_custom_call" | custom-call | tf_op jit(solution)/shard_map/attention_forward/pallas_call | solution.py:326
  88.8 26.2 %attention_forward.3 = (bf16[1024,512]{1,0:T(8,128)(2,1)}, bf16[1024,512]{1,0:T(8,128)(2,1)}, bf16[1024,512]{1,0:T(8,128)(2,1)}, bf16[512,1024]{1,0:T(8,128)(2,1...) custom-call(bf16[1024,512]{1,0:T(8,128)(2,1)} %bitcast.336, ...), custom_call_target="tpu_custom_call" | custom-call | tf_op jit(solution)/shard_map/attention_forward/pallas_call | solution.py:326
  116.5 2.7 pad_maximum_fusion.1.refs_4_
  119.2 11.4 %experts.1 = (f32[2,64,512]{2,1,0:T(8,128)}, f32[2,64,512]{2,1,0:T(8,128)}, bf16[2,64,512]{2,1,0:T(8,128)(2,1)}, bf16[2,64,512]{2,1,0:T(8,128)(2,1)}) custom-call(f32[2,32,512]{2,1,0:T(8,128)} %get-tuple-element.47.refs_0_, f32[2,32,512]{2,1,0:T(8,128)} %get-tuple-element.48.refs_1_, f32[16,1024]{1,0:T(8,128)} %get-tuple-element.46.refs_2_.gate_ref, ...), custom_call_target="tpu_custom_call" | custom-call | tf_op jit(solution)/shard_map/experts/pallas_call | solution.py:365
  130.6 35.5 %attention_backward.2 = (bf16[1024,512]{1,0:T(8,128)(2,1)}, bf16[1024,512]{1,0:T(8,128)(2,1)}, f32[512,512]{1,0:T(8,128)}, f32[512,1024]{1,0:T(8,128)}, f32[512,512]{1,0:T(8,128)}, /*index=5*/f32[32,512]{1,0:T(8,128)}) custom-call(bf16[1024,512]{1,0:T(8,128)(2,1)} %bitcast.341, bf16[1024,512]{1,0:T(8,128)(2,1)} %bitcast.15.cot_ref, ...), custom_call_target="tpu_custom_call" | custom-call | tf_op jit(solution)/shard_map/attention_backward/pallas_call | solution.py:398
  172.2 34.6 %attention_backward.3 = (bf16[1024,512]{1,0:T(8,128)(2,1)}, bf16[1024,512]{1,0:T(8,128)(2,1)}, f32[512,512]{1,0:T(8,128)}, f32[512,1024]{1,0:T(8,128)}, f32[512,512]{1,0:T(8,128)}, /*index=5*/f32[32,512]{1,0:T(8,128)}) custom-call(bf16[1024,512]{1,0:T(8,128)(2,1)} %bitcast.337, bf16[1024,512]{1,0:T(8,128)(2,1)} %bitcast.339, ...), custom_call_target="tpu_custom_call" | custom-call | tf_op jit(solution)/shard_map/attention_backward/pallas_call | solution.py:398
  213.7 2.7 collective-permute-start.30
  221.8 3.5 collective-permute-start.33
  226.3 2.3 collective-permute-done.33
  228.6 2.4 collective-permute-done.32
  236.3 8.8 %collective-permute-done.19 = bf16[256,512]{1,0:T(8,128)(2,1)S(1)} collective-permute-done((bf16[256,512]{1,0:T(8,128)(2,1)S(1)}, bf16[256,512]{1,0:T(8,128)(2,1)S(1)}, u32[]{:S(2)}, u32[]{:S(2)}) %collective-permute-start.19) | collective-permute-done | bytes 262176 | tf_op jit(solution)/shard_map/ppermute | solution.py:423
  247.3 9.1 %collective-permute-done.16 = bf16[256,512]{1,0:T(8,128)(2,1)S(1)} collective-permute-done((bf16[256,512]{1,0:T(8,128)(2,1)S(1)}, bf16[256,512]{1,0:T(8,128)(2,1)S(1)}, u32[]{:S(2)}, u32[]{:S(2)}) %collective-permute-start.16) | collective-permute-done | bytes 262176 | tf_op jit(solution)/shard_map/ppermute | solution.py:423
  258.7 9.0 %collective-permute-done.22 = bf16[256,512]{1,0:T(8,128)(2,1)S(1)} collective-permute-done((bf16[256,512]{1,0:T(8,128)(2,1)S(1)}, bf16[256,512]{1,0:T(8,128)(2,1)S(1)}, u32[]{:S(2)}, u32[]{:S(2)}) %collective-permute-start.22) | collective-permute-done | bytes 262176 | tf_op jit(solution)/shard_map/ppermute | solution.py:423
  270.7 8.2 %collective-permute-done.49 = bf16[2,2,64,512]{3,2,1,0:T(8,128)(2,1)S(1)} collective-permute-done((bf16[2,2,64,512]{3,2,1,0:T(8,128)(2,1)S(1)}, bf16[2,2,64,512]{3,2,1,0:T(8,128)(2,1)S(1)}, u32[]{:S(2)}, u32[]{:S(2)}) %collective-permute-start.49) | collective-permute-done | bytes 262176 | tf_op jit(solution)/shard_map/ppermute | solution.py:423
  280.1 2.6 fusion.16
  282.7 2.5 copy.80
  285.7 2.9 convolution_bitcast_fusion.1
  290.9 2.3 collective-permute-start.54
  293.2 2.2 bitcast_add_fusion
  297.5 4.7 collective-permute-done.52
  304.1 6.1 %collective-permute-done.53 = bf16[2,128,512]{2,1,0:T(8,128)(2,1)S(1)} collective-permute-done((bf16[2,128,512]{2,1,0:T(8,128)(2,1)S(1)}, bf16[2,128,512]{2,1,0:T(8,128)(2,1)S(1)}, u32[]{:S(2)}, u32[]{:S(2)}) %collective-permute-start.53) | collective-permute-done | bytes 262176 | tf_op jit(solution)/shard_map/ppermute | solution.py:515
  310.5 6.2 %collective-permute-start.56 = (bf16[2,128,512]{2,1,0:T(8,128)(2,1)S(1)}, bf16[2,128,512]{2,1,0:T(8,128)(2,1)S(1)}, u32[]{:S(2)}, u32[]{:S(2)}) collective-permute-start(bf16[2,128,512]{2,1,0:T(8,128)(2,1)S(1)} %get-tuple-element.124), channel_id=1, source_target_pairs={{0,16},{4,20},{8,24},{12,28},{16,0},{20,4},{24,8},{28,12},{1,17},{... | collective-permute-start | bytes 786440 | tf_op jit(solution)/shard_map/ppermute | solution.py:515
  319.6 2.3 collective-permute-start.40
  321.9 7.1 %collective-permute-done.55 = bf16[2,128,512]{2,1,0:T(8,128)(2,1)S(1)} collective-permute-done((bf16[2,128,512]{2,1,0:T(8,128)(2,1)S(1)}, bf16[2,128,512]{2,1,0:T(8,128)(2,1)S(1)}, u32[]{:S(2)}, u32[]{:S(2)}) %collective-permute-start.55) | collective-permute-done | bytes 262176 | tf_op jit(solution)/shard_map/ppermute | solution.py:515
  329.1 2.6 collective-permute-start.39
  331.7 3.9 collective-permute-done.38
  335.6 3.0 collective-permute-done.40
  338.6 6.0 %collective-permute-done.39 = bf16[64,512]{1,0:T(8,128)(2,1)S(1)} collective-permute-done((bf16[64,512]{1,0:T(8,128)(2,1)S(1)}, bf16[64,512]{1,0:T(8,128)(2,1)S(1)}, u32[]{:S(2)}, u32[]{:S(2)}) %collective-permute-start.39) | collective-permute-done | bytes 65568 | tf_op jit(solution)/shard_map/ppermute | solution.py:515
  344.8 2.4 collective-permute-start.42
  350.8 2.6 collective-permute-done.43
  356.8 4.2 broadcast_in_dim.189
  362.8 2.4 collective-permute-start.46
  365.2 49.3 %collective-permute-done.45 = bf16[256,512]{1,0:T(8,128)(2,1)S(1)} collective-permute-done((bf16[256,512]{1,0:T(8,128)(2,1)S(1)}, bf16[256,512]{1,0:T(8,128)(2,1)S(1)}, u32[]{:S(2)}, u32[]{:S(2)}) %collective-permute-start.45) | collective-permute-done | bytes 262176 | tf_op jit(solution)/shard_map/ppermute | solution.py:566
  420.6 19.3 %collective-permute-done.60 = bf16[2,512,512]{2,1,0:T(8,128)(2,1)S(1)} collective-permute-done((bf16[2,512,512]{2,1,0:T(8,128)(2,1)S(1)}, bf16[2,512,512]{2,1,0:T(8,128)(2,1)S(1)}, u32[]{:S(2)}, u32[]{:S(2)}) %collective-permute-start.60) | collective-permute-done | bytes 1048608 | tf_op jit(solution)/shard_map/ppermute | solution.py:533
  442.0 20.0 %collective-permute-done.62 = bf16[2,512,512]{2,1,0:T(8,128)(2,1)S(1)} collective-permute-done((bf16[2,512,512]{2,1,0:T(8,128)(2,1)S(1)}, bf16[2,512,512]{2,1,0:T(8,128)(2,1)S(1)}, u32[]{:S(2)}, u32[]{:S(2)}) %collective-permute-start.62) | collective-permute-done | bytes 1048608 | tf_op jit(solution)/shard_map/ppermute | solution.py:533
  463.1 23.0 %collective-permute-done.63 = bf16[2,512,512]{2,1,0:T(8,128)(2,1)S(1)} collective-permute-done((bf16[2,512,512]{2,1,0:T(8,128)(2,1)S(1)}, bf16[2,512,512]{2,1,0:T(8,128)(2,1)S(1)}, u32[]{:S(2)}, u32[]{:S(2)}) %collective-permute-start.63) | collective-permute-done | bytes 1048608 | tf_op jit(solution)/shard_map/ppermute | solution.py:533
  488.2 11.7 %convert.3 = f32[2,2,2,2,512,512]{5,4,3,2,1,0:T(8,128)} convert(bf16[2,2,2,2,512,512]{5,4,3,2,1,0:T(8,128)(2,1)} %bitcast.159) | non-fusion elementwise | flops 4194304 | bytes 25165824 | tf_op jit(solution)/shard_map/convert_element_type | solution.py:538
  499.9 9.6 %slice_bitcast_fusion = (f32[2,2,2,512,512]{4,3,0,2,1:T(8,128)S(1)}, f32[2,512,2,2,512]{4,1,0,3,2:T(8,128)}) fusion(f32[2,2,2,2,512,512]{5,4,3,2,1,0:T(8,128)} %convert.3), kind=kLoop, calls=%fused_computation | loop fusion | bytes 33554432 | tf_op jit(solution)/shard_map/transpose | solution.py:540
  509.5 4.5 copy.89
  514.0 10.0 %copy.88 = f32[2,512,2,2,512]{1,4,3,2,0:T(8,128)} copy(f32[2,512,2,2,512]{4,1,0,3,2:T(8,128)} %get-tuple-element.128) | data formatting | bytes 16777216 | tf_op jit(solution)/shard_map/transpose | solution.py:539
  523.9 8.7 %copy.91 = f32[2,512,2048]{2,1,0:T(8,128)} copy(f32[2,512,2048]{1,2,0:T(8,128)} %bitcast.333) | data formatting | bytes 16777216
  (267 shorter events, 99.4 us)
Async XLA Ops:
  1.6 25.6 %collective-permute-start.6 = (s32[256]{0:T(256)S(1)}, s32[256]{0:T(256)S(1)}, u32[]{:S(2)}, u32[]{:S(2)}) collective-permute-start(s32[256]{0:T(256)S(1)} %bitcast.405), channel_id=1, source_target_pairs={{0,1},{1,0},{2,3},{3,2},{4,5},{5,4},{6,7},{7,6},{8,9},{9,8},{10,11... | collective-permute-start | bytes 3080 | tf_op jit(solution)/shard_map/ppermute | solution.py:423
  2.1 26.7 %collective-permute-start.8 = (s32[256]{0:T(256)S(1)}, s32[256]{0:T(256)S(1)}, u32[]{:S(2)}, u32[]{:S(2)}) collective-permute-start(s32[256]{0:T(256)S(1)} %bitcast.401), channel_id=1, source_target_pairs={{0,3},{1,2},{2,1},{3,0},{4,7},{5,6},{6,5},{7,4},{8,11},{9,10},{10,... | collective-permute-start | bytes 3080 | tf_op jit(solution)/shard_map/ppermute | solution.py:423
  4.7 22.7 %collective-permute-start.7 = (s32[256]{0:T(256)S(1)}, s32[256]{0:T(256)S(1)}, u32[]{:S(2)}, u32[]{:S(2)}) collective-permute-start(s32[256]{0:T(256)S(1)} %bitcast.402), channel_id=1, source_target_pairs={{0,2},{1,3},{2,0},{3,1},{4,6},{5,7},{6,4},{7,5},{8,10},{9,11},{10,... | collective-permute-start | bytes 3080 | tf_op jit(solution)/shard_map/ppermute | solution.py:423
  9.3 28.4 %collective-permute-start.11 = (bf16[256,512]{1,0:T(8,128)(2,1)S(1)}, bf16[256,512]{1,0:T(8,128)(2,1)}, u32[]{:S(2)}, u32[]{:S(2)}) collective-permute-start(bf16[256,512]{1,0:T(8,128)(2,1)S(1)} %get-tuple-element.168), channel_id=1, source_target_pairs={{0,3},{1,2},{2,1},{3,0},{4,7},{5,6},{6,5},{7,4},{8,11},{9,10},{10,... | collective-permute-start | bytes 786440 | tf_op jit(solution)/shard_map/ppermute | solution.py:423
  10.6 20.2 %collective-permute-start.9 = (bf16[256,512]{1,0:T(8,128)(2,1)}, bf16[256,512]{1,0:T(8,128)(2,1)}, u32[]{:S(2)}, u32[]{:S(2)}) collective-permute-start(bf16[256,512]{1,0:T(8,128)(2,1)} %get-tuple-element.170), channel_id=1, source_target_pairs={{0,1},{1,0},{2,3},{3,2},{4,5},{5,4},{6,7},{7,6},{8,9},{9,8},{10,11... | collective-permute-start | bytes 786440 | tf_op jit(solution)/shard_map/ppermute | solution.py:423
  27.4 21.5 %collective-permute-start.2 = (bf16[256,512]{1,0:T(8,128)(2,1)}, bf16[256,512]{1,0:T(8,128)(2,1)}, u32[]{:S(2)}, u32[]{:S(2)}) collective-permute-start(bf16[256,512]{1,0:T(8,128)(2,1)} %get-tuple-element.162), channel_id=1, source_target_pairs={{0,3},{1,2},{2,1},{3,0},{4,7},{5,6},{6,5},{7,4},{8,11},{9,10},{10,... | collective-permute-start | bytes 786440 | tf_op jit(solution)/shard_map/ppermute | solution.py:423
  28.8 19.2 %collective-permute-start.1 = (bf16[256,512]{1,0:T(8,128)(2,1)}, bf16[256,512]{1,0:T(8,128)(2,1)}, u32[]{:S(2)}, u32[]{:S(2)}) collective-permute-start(bf16[256,512]{1,0:T(8,128)(2,1)} %get-tuple-element.163), channel_id=1, source_target_pairs={{0,2},{1,3},{2,0},{3,1},{4,6},{5,7},{6,4},{7,5},{8,10},{9,11},{10,... | collective-permute-start | bytes 786440 | tf_op jit(solution)/shard_map/ppermute | solution.py:423
  36.8 22.4 %collective-permute-start.14 = (bf16[256,512]{1,0:T(8,128)(2,1)}, bf16[256,512]{1,0:T(8,128)(2,1)S(1)}, u32[]{:S(2)}, u32[]{:S(2)}) collective-permute-start(bf16[256,512]{1,0:T(8,128)(2,1)} %get-tuple-element.165), channel_id=1, source_target_pairs={{0,3},{1,2},{2,1},{3,0},{4,7},{5,6},{6,5},{7,4},{8,11},{9,10},{10,... | collective-permute-start | bytes 786440 | tf_op jit(solution)/shard_map/ppermute | solution.py:423
  37.7 21.4 %collective-permute-start.13 = (bf16[256,512]{1,0:T(8,128)(2,1)}, bf16[256,512]{1,0:T(8,128)(2,1)S(1)}, u32[]{:S(2)}, u32[]{:S(2)}) collective-permute-start(bf16[256,512]{1,0:T(8,128)(2,1)} %get-tuple-element.166), channel_id=1, source_target_pairs={{0,2},{1,3},{2,0},{3,1},{4,6},{5,7},{6,4},{7,5},{8,10},{9,11},{10,... | collective-permute-start | bytes 786440 | tf_op jit(solution)/shard_map/ppermute | solution.py:423
  38.9 11.2 %collective-permute-start.12 = (bf16[256,512]{1,0:T(8,128)(2,1)}, bf16[256,512]{1,0:T(8,128)(2,1)S(1)}, u32[]{:S(2)}, u32[]{:S(2)}) collective-permute-start(bf16[256,512]{1,0:T(8,128)(2,1)} %get-tuple-element.167), channel_id=1, source_target_pairs={{0,1},{1,0},{2,3},{3,2},{4,5},{5,4},{6,7},{7,6},{8,9},{9,8},{10,11... | collective-permute-start | bytes 786440 | tf_op jit(solution)/shard_map/ppermute | solution.py:423
  48.0 67.7 %collective-permute-start.5 = (bf16[256,512]{1,0:T(8,128)(2,1)}, bf16[256,512]{1,0:T(8,128)(2,1)S(1)}, u32[]{:S(2)}, u32[]{:S(2)}) collective-permute-start(bf16[256,512]{1,0:T(8,128)(2,1)} %get-tuple-element.159), channel_id=1, source_target_pairs={{0,3},{1,2},{2,1},{3,0},{4,7},{5,6},{6,5},{7,4},{8,11},{9,10},{10,... | collective-permute-start | bytes 786440 | tf_op jit(solution)/shard_map/ppermute | solution.py:423
  49.0 66.0 %collective-permute-start.4 = (bf16[256,512]{1,0:T(8,128)(2,1)}, bf16[256,512]{1,0:T(8,128)(2,1)S(1)}, u32[]{:S(2)}, u32[]{:S(2)}) collective-permute-start(bf16[256,512]{1,0:T(8,128)(2,1)} %get-tuple-element.160), channel_id=1, source_target_pairs={{0,2},{1,3},{2,0},{3,1},{4,6},{5,7},{6,4},{7,5},{8,10},{9,11},{10,... | collective-permute-start | bytes 786440 | tf_op jit(solution)/shard_map/ppermute | solution.py:423
  209.6 15.7 %collective-permute-start.48 = (bf16[2,64,512]{2,1,0:T(8,128)(2,1)S(1)}, bf16[2,64,512]{2,1,0:T(8,128)(2,1)S(1)}, u32[]{:S(2)}, u32[]{:S(2)}) collective-permute-start(bf16[2,64,512]{2,1,0:T(8,128)(2,1)S(1)} %get-tuple-element.177), channel_id=1, source_target_pairs={{0,1},{1,0},{2,3},{3,2},{4,5},{5,4},{6,7},{7,6},{8,9},{9,8},{10,11... | collective-permute-start | bytes 393224 | tf_op jit(solution)/shard_map/ppermute | solution.py:423
  210.2 24.5 %collective-permute-start.26 = (bf16[256,512]{1,0:T(8,128)(2,1)S(1)}, bf16[256,512]{1,0:T(8,128)(2,1)S(1)}, u32[]{:S(2)}, u32[]{:S(2)}) collective-permute-start(bf16[256,512]{1,0:T(8,128)(2,1)S(1)} %get-tuple-element.150), channel_id=1, source_target_pairs={{0,3},{1,2},{2,1},{3,0},{4,7},{5,6},{6,5},{7,4},{8,11},{9,10},{10,... | collective-permute-start | bytes 786440 | tf_op jit(solution)/shard_map/ppermute | solution.py:423
  219.2 14.9 %collective-permute-start.25 = (bf16[256,512]{1,0:T(8,128)(2,1)S(1)}, bf16[256,512]{1,0:T(8,128)(2,1)S(1)}, u32[]{:S(2)}, u32[]{:S(2)}) collective-permute-start(bf16[256,512]{1,0:T(8,128)(2,1)S(1)} %get-tuple-element.151), channel_id=1, source_target_pairs={{0,2},{1,3},{2,0},{3,1},{4,6},{5,7},{6,4},{7,5},{8,10},{9,11},{10,... | collective-permute-start | bytes 786440 | tf_op jit(solution)/shard_map/ppermute | solution.py:423
  231.0 14.5 %collective-permute-start.20 = (bf16[256,512]{1,0:T(8,128)(2,1)S(1)}, bf16[256,512]{1,0:T(8,128)(2,1)S(1)}, u32[]{:S(2)}, u32[]{:S(2)}) collective-permute-start(bf16[256,512]{1,0:T(8,128)(2,1)S(1)} %get-tuple-element.156), channel_id=1, source_target_pairs={{0,3},{1,2},{2,1},{3,0},{4,7},{5,6},{6,5},{7,4},{8,11},{9,10},{10,... | collective-permute-start | bytes 786440 | tf_op jit(solution)/shard_map/ppermute | solution.py:423
  231.0 14.1 %collective-permute-start.19 = (bf16[256,512]{1,0:T(8,128)(2,1)S(1)}, bf16[256,512]{1,0:T(8,128)(2,1)S(1)}, u32[]{:S(2)}, u32[]{:S(2)}) collective-permute-start(bf16[256,512]{1,0:T(8,128)(2,1)S(1)} %get-tuple-element.157), channel_id=1, source_target_pairs={{0,2},{1,3},{2,0},{3,1},{4,6},{5,7},{6,4},{7,5},{8,10},{9,11},{10,... | collective-permute-start | bytes 786440 | tf_op jit(solution)/shard_map/ppermute | solution.py:423
  234.1 22.4 %collective-permute-start.17 = (bf16[256,512]{1,0:T(8,128)(2,1)S(1)}, bf16[256,512]{1,0:T(8,128)(2,1)S(1)}, u32[]{:S(2)}, u32[]{:S(2)}) collective-permute-start(bf16[256,512]{1,0:T(8,128)(2,1)S(1)} %copy-done.21), channel_id=1, source_target_pairs={{0,3},{1,2},{2,1},{3,0},{4,7},{5,6},{6,5},{7,4},{8,11},{9,10},{10,... | collective-permute-start | bytes 786440 | tf_op jit(solution)/shard_map/ppermute | solution.py:423
  234.7 21.7 %collective-permute-start.16 = (bf16[256,512]{1,0:T(8,128)(2,1)S(1)}, bf16[256,512]{1,0:T(8,128)(2,1)S(1)}, u32[]{:S(2)}, u32[]{:S(2)}) collective-permute-start(bf16[256,512]{1,0:T(8,128)(2,1)S(1)} %copy-done.22), channel_id=1, source_target_pairs={{0,2},{1,3},{2,0},{3,1},{4,6},{5,7},{6,4},{7,5},{8,10},{9,11},{10,... | collective-permute-start | bytes 786440 | tf_op jit(solution)/shard_map/ppermute | solution.py:423
  245.1 25.5 %collective-permute-start.23 = (bf16[256,512]{1,0:T(8,128)(2,1)S(1)}, bf16[256,512]{1,0:T(8,128)(2,1)S(1)}, u32[]{:S(2)}, u32[]{:S(2)}) collective-permute-start(bf16[256,512]{1,0:T(8,128)(2,1)S(1)} %get-tuple-element.147), channel_id=1, source_target_pairs={{0,3},{1,2},{2,1},{3,0},{4,7},{5,6},{6,5},{7,4},{8,11},{9,10},{10,... | collective-permute-start | bytes 786440 | tf_op jit(solution)/shard_map/ppermute | solution.py:423
  245.5 22.1 %collective-permute-start.22 = (bf16[256,512]{1,0:T(8,128)(2,1)S(1)}, bf16[256,512]{1,0:T(8,128)(2,1)S(1)}, u32[]{:S(2)}, u32[]{:S(2)}) collective-permute-start(bf16[256,512]{1,0:T(8,128)(2,1)S(1)} %copy-done.19), channel_id=1, source_target_pairs={{0,2},{1,3},{2,0},{3,1},{4,6},{5,7},{6,4},{7,5},{8,10},{9,11},{10,... | collective-permute-start | bytes 786440 | tf_op jit(solution)/shard_map/ppermute | solution.py:423
  247.0 11.0 %collective-permute-start.21 = (bf16[256,512]{1,0:T(8,128)(2,1)S(1)}, bf16[256,512]{1,0:T(8,128)(2,1)S(1)}, u32[]{:S(2)}, u32[]{:S(2)}) collective-permute-start(bf16[256,512]{1,0:T(8,128)(2,1)S(1)} %copy-done.20), channel_id=1, source_target_pairs={{0,1},{1,0},{2,3},{3,2},{4,5},{5,4},{6,7},{7,6},{8,9},{9,8},{10,11... | collective-permute-start | bytes 786440 | tf_op jit(solution)/shard_map/ppermute | solution.py:423
  256.4 36.8 %collective-permute-start.34 = (bf16[1024,512]{1,0:T(8,128)(2,1)}, bf16[1024,512]{1,0:T(8,128)(2,1)}, u32[]{:S(2)}, u32[]{:S(2)}) collective-permute-start(bf16[1024,512]{1,0:T(8,128)(2,1)} %fusion.17), channel_id=1, source_target_pairs={{0,1},{1,0},{2,3},{3,2},{4,5},{5,4},{6,7},{7,6},{8,9},{9,8},{10,11... | collective-permute-start | bytes 3145736 | tf_op jit(solution)/shard_map/ppermute | solution.py:423
  256.5 14.1 %collective-permute-start.50 = (bf16[2,2,64,512]{3,2,1,0:T(8,128)(2,1)S(1)}, bf16[2,2,64,512]{3,2,1,0:T(8,128)(2,1)S(1)}, u32[]{:S(2)}, u32[]{:S(2)}) collective-permute-start(bf16[2,2,64,512]{3,2,1,0:T(8,128)(2,1)S(1)} %get-tuple-element.175), channel_id=1, source_target_pairs={{0,4},{1,5},{2,6},{3,7},{4,0},{5,1},{6,2},{7,3},{8,12},{9,13},{10,... | collective-permute-start | bytes 786440 | tf_op jit(solution)/shard_map/ppermute | solution.py:493
  258.1 20.8 %collective-permute-start.49 = (bf16[2,2,64,512]{3,2,1,0:T(8,128)(2,1)S(1)}, bf16[2,2,64,512]{3,2,1,0:T(8,128)(2,1)S(1)}, u32[]{:S(2)}, u32[]{:S(2)}) collective-permute-start(bf16[2,2,64,512]{3,2,1,0:T(8,128)(2,1)S(1)} %get-tuple-element.175), channel_id=1, source_target_pairs={{0,2},{1,3},{2,0},{3,1},{4,6},{5,7},{6,4},{7,5},{8,10},{9,11},{10,... | collective-permute-start | bytes 786440 | tf_op jit(solution)/shard_map/ppermute | solution.py:423
  267.6 11.2 %collective-permute-start.51 = (bf16[2,2,64,512]{3,2,1,0:T(8,128)(2,1)S(1)}, bf16[2,2,64,512]{3,2,1,0:T(8,128)(2,1)S(1)}, u32[]{:S(2)}, u32[]{:S(2)}) collective-permute-start(bf16[2,2,64,512]{3,2,1,0:T(8,128)(2,1)S(1)} %get-tuple-element.175), channel_id=1, source_target_pairs={{0,6},{1,7},{2,4},{3,5},{4,2},{5,3},{6,0},{7,1},{8,14},{9,15},{10,... | collective-permute-start | bytes 786440 | tf_op jit(solution)/shard_map/ppermute | solution.py:493
  288.7 13.4 %collective-permute-start.52 = (bf16[2,128,512]{2,1,0:T(8,128)(2,1)S(1)}, bf16[2,128,512]{2,1,0:T(8,128)(2,1)S(1)}, u32[]{:S(2)}, u32[]{:S(2)}) collective-permute-start(bf16[2,128,512]{2,1,0:T(8,128)(2,1)S(1)} %get-tuple-element.133), channel_id=1, source_target_pairs={{0,8},{4,12},{8,0},{12,4},{16,24},{20,28},{24,16},{28,20},{1,9},{5... | collective-permute-start | bytes 786440 | tf_op jit(solution)/shard_map/ppermute | solution.py:515
  288.8 21.4 %collective-permute-start.53 = (bf16[2,128,512]{2,1,0:T(8,128)(2,1)S(1)}, bf16[2,128,512]{2,1,0:T(8,128)(2,1)S(1)}, u32[]{:S(2)}, u32[]{:S(2)}) collective-permute-start(bf16[2,128,512]{2,1,0:T(8,128)(2,1)S(1)} %get-tuple-element.134), channel_id=1, source_target_pairs={{0,16},{4,20},{8,24},{12,28},{16,0},{20,4},{24,8},{28,12},{1,17},{... | collective-permute-start | bytes 786440 | tf_op jit(solution)/shard_map/ppermute | solution.py:515
  290.9 19.3 %collective-permute-start.54 = (bf16[2,128,512]{2,1,0:T(8,128)(2,1)S(1)}, bf16[2,128,512]{2,1,0:T(8,128)(2,1)S(1)}, u32[]{:S(2)}, u32[]{:S(2)}) collective-permute-start(bf16[2,128,512]{2,1,0:T(8,128)(2,1)S(1)} %get-tuple-element.135), channel_id=1, source_target_pairs={{0,24},{4,28},{8,16},{12,20},{16,8},{20,12},{24,0},{28,4},{1,25},{... | collective-permute-start | bytes 786440 | tf_op jit(solution)/shard_map/ppermute | solution.py:515
  295.5 21.2 %collective-permute-start.35 = (bf16[256,512]{1,0:T(8,128)(2,1)S(1)}, bf16[256,512]{1,0:T(8,128)(2,1)S(1)}, u32[]{:S(2)}, u32[]{:S(2)}) collective-permute-start(bf16[256,512]{1,0:T(8,128)(2,1)S(1)} %get-tuple-element.136), channel_id=1, source_target_pairs={{0,4},{1,5},{2,6},{3,7},{4,0},{5,1},{6,2},{7,3},{8,12},{9,13},{10,... | collective-permute-start | bytes 786440 | tf_op jit(solution)/shard_map/ppermute | solution.py:566
  297.1 21.2 %collective-permute-start.37 = (bf16[256,512]{1,0:T(8,128)(2,1)S(1)}, bf16[256,512]{1,0:T(8,128)(2,1)S(1)}, u32[]{:S(2)}, u32[]{:S(2)}) collective-permute-start(bf16[256,512]{1,0:T(8,128)(2,1)S(1)} %get-tuple-element.137), channel_id=1, source_target_pairs={{0,6},{1,7},{2,4},{3,5},{4,2},{5,3},{6,0},{7,1},{8,14},{9,15},{10,... | collective-permute-start | bytes 786440 | tf_op jit(solution)/shard_map/ppermute | solution.py:566
  302.1 16.1 %collective-permute-start.36 = (bf16[256,512]{1,0:T(8,128)(2,1)S(1)}, bf16[256,512]{1,0:T(8,128)(2,1)S(1)}, u32[]{:S(2)}, u32[]{:S(2)}) collective-permute-start(bf16[256,512]{1,0:T(8,128)(2,1)S(1)} %get-tuple-element.138), channel_id=1, source_target_pairs={{0,2},{1,3},{2,0},{3,1},{4,6},{5,7},{6,4},{7,5},{8,10},{9,11},{10,... | collective-permute-start | bytes 786440 | tf_op jit(solution)/shard_map/ppermute | solution.py:566
  310.5 34.3 %collective-permute-start.56 = (bf16[2,128,512]{2,1,0:T(8,128)(2,1)S(1)}, bf16[2,128,512]{2,1,0:T(8,128)(2,1)S(1)}, u32[]{:S(2)}, u32[]{:S(2)}) collective-permute-start(bf16[2,128,512]{2,1,0:T(8,128)(2,1)S(1)} %get-tuple-element.124), channel_id=1, source_target_pairs={{0,16},{4,20},{8,24},{12,28},{16,0},{20,4},{24,8},{28,12},{1,17},{... | collective-permute-start | bytes 786440 | tf_op jit(solution)/shard_map/ppermute | solution.py:515
  316.7 12.4 %collective-permute-start.55 = (bf16[2,128,512]{2,1,0:T(8,128)(2,1)S(1)}, bf16[2,128,512]{2,1,0:T(8,128)(2,1)S(1)}, u32[]{:S(2)}, u32[]{:S(2)}) collective-permute-start(bf16[2,128,512]{2,1,0:T(8,128)(2,1)S(1)} %get-tuple-element.124), channel_id=1, source_target_pairs={{0,8},{4,12},{8,0},{12,4},{16,24},{20,28},{24,16},{28,20},{1,9},{5... | collective-permute-start | bytes 786440 | tf_op jit(solution)/shard_map/ppermute | solution.py:515
  316.7 38.1 %collective-permute-start.57 = (bf16[2,128,512]{2,1,0:T(8,128)(2,1)S(1)}, bf16[2,128,512]{2,1,0:T(8,128)(2,1)S(1)}, u32[]{:S(2)}, u32[]{:S(2)}) collective-permute-start(bf16[2,128,512]{2,1,0:T(8,128)(2,1)S(1)} %get-tuple-element.124), channel_id=1, source_target_pairs={{0,24},{4,28},{8,16},{12,20},{16,8},{20,12},{24,0},{28,4},{1,25},{... | collective-permute-start | bytes 786440 | tf_op jit(solution)/shard_map/ppermute | solution.py:515
  318.5 17.1 %collective-permute-start.38 = (bf16[64,512]{1,0:T(8,128)(2,1)S(1)}, bf16[64,512]{1,0:T(8,128)(2,1)S(1)}, u32[]{:S(2)}, u32[]{:S(2)}) collective-permute-start(bf16[64,512]{1,0:T(8,128)(2,1)S(1)} %get-tuple-element.171), channel_id=1, source_target_pairs={{0,8},{4,12},{8,0},{12,4},{16,24},{20,28},{24,16},{28,20},{1,9},{5... | collective-permute-start | bytes 196616 | tf_op jit(solution)/shard_map/ppermute | solution.py:515
  319.6 18.9 %collective-permute-start.40 = (bf16[64,512]{1,0:T(8,128)(2,1)S(1)}, bf16[64,512]{1,0:T(8,128)(2,1)S(1)}, u32[]{:S(2)}, u32[]{:S(2)}) collective-permute-start(bf16[64,512]{1,0:T(8,128)(2,1)S(1)} %get-tuple-element.172), channel_id=1, source_target_pairs={{0,24},{4,28},{8,16},{12,20},{16,8},{20,12},{24,0},{28,4},{1,25},{... | collective-permute-start | bytes 196616 | tf_op jit(solution)/shard_map/ppermute | solution.py:515
  329.1 15.6 %collective-permute-start.39 = (bf16[64,512]{1,0:T(8,128)(2,1)S(1)}, bf16[64,512]{1,0:T(8,128)(2,1)S(1)}, u32[]{:S(2)}, u32[]{:S(2)}) collective-permute-start(bf16[64,512]{1,0:T(8,128)(2,1)S(1)} %get-tuple-element.173), channel_id=1, source_target_pairs={{0,16},{4,20},{8,24},{12,28},{16,0},{20,4},{24,8},{28,12},{1,17},{... | collective-permute-start | bytes 196616 | tf_op jit(solution)/shard_map/ppermute | solution.py:515
  354.8 132.3 %collective-permute-start.64 = (bf16[2,512,512]{2,1,0:T(8,128)(2,1)S(1)}, bf16[2,512,512]{2,1,0:T(8,128)(2,1)S(1)}, u32[]{:S(2)}, u32[]{:S(2)}) collective-permute-start(bf16[2,512,512]{2,1,0:T(8,128)(2,1)S(1)} %bitcast.347), channel_id=1, source_target_pairs={{0,7},{1,6},{2,5},{3,4},{4,3},{5,2},{6,1},{7,0},{8,15},{9,14},{10,... | collective-permute-start | bytes 3145736 | tf_op jit(solution)/shard_map/ppermute | solution.py:533
  354.9 62.9 %collective-permute-start.59 = (bf16[2,512,512]{2,1,0:T(8,128)(2,1)S(1)}, bf16[2,512,512]{2,1,0:T(8,128)(2,1)S(1)}, u32[]{:S(2)}, u32[]{:S(2)}) collective-permute-start(bf16[2,512,512]{2,1,0:T(8,128)(2,1)S(1)} %bitcast.348), channel_id=1, source_target_pairs={{0,2},{1,3},{2,0},{3,1},{4,6},{5,7},{6,4},{7,5},{8,10},{9,11},{10,... | collective-permute-start | bytes 3145736 | tf_op jit(solution)/shard_map/ppermute | solution.py:533
  355.5 60.2 %collective-permute-start.58 = (bf16[2,512,512]{2,1,0:T(8,128)(2,1)S(1)}, bf16[2,512,512]{2,1,0:T(8,128)(2,1)S(1)}, u32[]{:S(2)}, u32[]{:S(2)}) collective-permute-start(bf16[2,512,512]{2,1,0:T(8,128)(2,1)S(1)} %bitcast.349), channel_id=1, source_target_pairs={{0,1},{1,0},{2,3},{3,2},{4,5},{5,4},{6,7},{7,6},{8,9},{9,8},{10,11... | collective-permute-start | bytes 3145736 | tf_op jit(solution)/shard_map/ppermute | solution.py:533
  362.1 52.4 %collective-permute-start.45 = (bf16[256,512]{1,0:T(8,128)(2,1)S(1)}, bf16[256,512]{1,0:T(8,128)(2,1)S(1)}, u32[]{:S(2)}, u32[]{:S(2)}) collective-permute-start(bf16[256,512]{1,0:T(8,128)(2,1)S(1)} %bitcast.372), channel_id=1, source_target_pairs={{0,2},{1,3},{2,0},{3,1},{4,6},{5,7},{6,4},{7,5},{8,10},{9,11},{10,... | collective-permute-start | bytes 786440 | tf_op jit(solution)/shard_map/ppermute | solution.py:566
  362.8 51.9 %collective-permute-start.46 = (bf16[256,512]{1,0:T(8,128)(2,1)S(1)}, bf16[256,512]{1,0:T(8,128)(2,1)S(1)}, u32[]{:S(2)}, u32[]{:S(2)}) collective-permute-start(bf16[256,512]{1,0:T(8,128)(2,1)S(1)} %bitcast.374), channel_id=1, source_target_pairs={{0,6},{1,7},{2,4},{3,5},{4,2},{5,3},{6,0},{7,1},{8,14},{9,15},{10,... | collective-permute-start | bytes 786440 | tf_op jit(solution)/shard_map/ppermute | solution.py:566
  414.4 25.4 %collective-permute-start.60 = (bf16[2,512,512]{2,1,0:T(8,128)(2,1)S(1)}, bf16[2,512,512]{2,1,0:T(8,128)(2,1)S(1)}, u32[]{:S(2)}, u32[]{:S(2)}) collective-permute-start(bf16[2,512,512]{2,1,0:T(8,128)(2,1)S(1)} %bitcast.351), channel_id=1, source_target_pairs={{0,3},{1,2},{2,1},{3,0},{4,7},{5,6},{6,5},{7,4},{8,11},{9,10},{10,... | collective-permute-start | bytes 3145736 | tf_op jit(solution)/shard_map/ppermute | solution.py:533
  414.7 26.3 %collective-permute-start.61 = (bf16[2,512,512]{2,1,0:T(8,128)(2,1)S(1)}, bf16[2,512,512]{2,1,0:T(8,128)(2,1)S(1)}, u32[]{:S(2)}, u32[]{:S(2)}) collective-permute-start(bf16[2,512,512]{2,1,0:T(8,128)(2,1)S(1)} %bitcast.352), channel_id=1, source_target_pairs={{0,4},{1,5},{2,6},{3,7},{4,0},{5,1},{6,2},{7,3},{8,12},{9,13},{10,... | collective-permute-start | bytes 3145736 | tf_op jit(solution)/shard_map/ppermute | solution.py:533
  415.7 46.3 %collective-permute-start.62 = (bf16[2,512,512]{2,1,0:T(8,128)(2,1)S(1)}, bf16[2,512,512]{2,1,0:T(8,128)(2,1)S(1)}, u32[]{:S(2)}, u32[]{:S(2)}) collective-permute-start(bf16[2,512,512]{2,1,0:T(8,128)(2,1)S(1)} %bitcast.353), channel_id=1, source_target_pairs={{0,5},{1,4},{2,7},{3,6},{4,1},{5,0},{6,3},{7,2},{8,13},{9,12},{10,... | collective-permute-start | bytes 3145736 | tf_op jit(solution)/shard_map/ppermute | solution.py:533
  417.9 68.2 %collective-permute-start.63 = (bf16[2,512,512]{2,1,0:T(8,128)(2,1)S(1)}, bf16[2,512,512]{2,1,0:T(8,128)(2,1)S(1)}, u32[]{:S(2)}, u32[]{:S(2)}) collective-permute-start(bf16[2,512,512]{2,1,0:T(8,128)(2,1)S(1)} %bitcast.354), channel_id=1, source_target_pairs={{0,6},{1,7},{2,4},{3,5},{4,2},{5,3},{6,0},{7,1},{8,14},{9,15},{10,... | collective-permute-start | bytes 3145736 | tf_op jit(solution)/shard_map/ppermute | solution.py:533
  439.9 92.7 %collective-permute-start.47 = (bf16[1024,512]{1,0:T(8,128)(2,1)S(1)}, bf16[1024,512]{1,0:T(8,128)(2,1)}, u32[]{:S(2)}, u32[]{:S(2)}) collective-permute-start(bf16[1024,512]{1,0:T(8,128)(2,1)S(1)} %bitcast.356), channel_id=1, source_target_pairs={{0,1},{1,0},{2,3},{3,2},{4,5},{5,4},{6,7},{7,6},{8,9},{9,8},{10,11... | collective-permute-start | bytes 3145736 | tf_op jit(solution)/shard_map/ppermute | solution.py:423
  (44 other events, 596.1 us)

commit v2 on v1

v2 whole, which is shorter than its diff:
```python
import functools

import jax
import jax.numpy as jnp
from jax import lax
from jax.experimental import pallas as pl
from jax.experimental.pallas import tpu as pltpu
from jax.sharding import PartitionSpec as P

HEAD_DIM = 64
GROUP = 32
EPSILON = 1e-05
BLOCK = 256
CHUNK = 512
SCALE = 0.125
MASKED = -1e30
VMEM_LIMIT = 60 * 1024 * 1024
BF = jnp.bfloat16
F32 = jnp.float32
MESH = pl.DeviceIdType.MESH


def dot(a, b, ca, cb):
    return lax.dot_general(a, b, (((ca,), (cb,)), ((), ())), preferred_element_type=F32)


def nn(a, b):
    return dot(a, b, 1, 0)


def nt(a, b):
    return dot(a, b, 1, 1)


def tn(a, b):
    return dot(a, b, 0, 0)


def key_range(packed, i):
    low = max(0, i * BLOCK - BLOCK - BLOCK // 2) if packed else 0
    return low, (i + 1) * BLOCK - low


def head_masks():
    lane = lax.broadcasted_iota(jnp.int32, (1, 2 * HEAD_DIM), 1)
    first = (lane < HEAD_DIM).astype(F32).astype(BF)
    return first, (lane >= HEAD_DIM).astype(F32).astype(BF)


def group_match(rows, tokens):
    row = lax.broadcasted_iota(jnp.int32, (rows, tokens), 0)
    col = lax.broadcasted_iota(jnp.int32, (rows, tokens), 1)
    return (row % (tokens // GROUP)) == (col // GROUP)


def fill_bias(bias_ref, start_ref, packed, i):
    low, count = key_range(packed, i)
    q_pos = i * BLOCK + lax.broadcasted_iota(jnp.int32, (1, BLOCK), 1)
    if packed:
        k_pos = low + lax.broadcasted_iota(jnp.int32, (count, BLOCK), 0)
        allowed = (k_pos <= q_pos) & (k_pos >= start_ref[...])
        bias_ref[0:count, :] = jnp.where(allowed, 0.0, MASKED)
    else:
        k_pos = i * BLOCK + lax.broadcasted_iota(jnp.int32, (BLOCK, BLOCK), 0)
        bias_ref[0:BLOCK, :] = jnp.where(k_pos <= q_pos, 0.0, MASKED)


def add_bias(scores, bias_ref, packed, count):
    if packed:
        return scores + bias_ref[0:count, :]
    last = scores[count - BLOCK :, :] + bias_ref[0:BLOCK, :]
    if count == BLOCK:
        return last
    return jnp.concatenate([scores[: count - BLOCK, :], last], axis=0)


def rms(values):
    return lax.rsqrt(jnp.mean(values * values, axis=-1, keepdims=True) + EPSILON)


def peer(axis, me, d):
    return {axis: me ^ d}


def arrive(partners):
    barrier = pltpu.get_barrier_semaphore()
    for p in partners:
        pl.semaphore_signal(barrier, inc=1, device_id=p, device_id_type=MESH)
    pl.semaphore_wait(barrier, len(partners))


def remote(src, dst, sems, k, where):
    return pltpu.make_async_remote_copy(
        src_ref=src, dst_ref=dst, send_sem=sems[0].at[k], recv_sem=sems[1].at[k],
        device_id=where, device_id_type=MESH,
    )


class Exchange:
    def __init__(self, nb, src, dst, own, sems, base):
        self.nb, self.src, self.dst, self.own, self.sems, self.base = nb, src, dst, own, sems, base
        self.me = lax.axis_index("blk")

    def local(self):
        return pltpu.make_async_copy(
            self.src.at[self.me], self.dst.at[self.me], self.own.at[self.base]
        )

    def copy(self, d):
        return remote(
            self.src.at[self.me ^ d], self.dst.at[self.me], self.sems,
            self.base * (self.nb - 1) + d - 1, peer("blk", self.me, d),
        )

    def start(self):
        self.local().start()
        for d in range(1, self.nb):
            self.copy(d).start()

    def wait(self):
        self.local().wait()
        for d in range(1, self.nb):
            self.copy(d).wait()


def forward_kernel(packed, blocks, nb, moves, *refs):
    if packed:
        x_ref, refs = refs[0], refs[1:]
    else:
        x_src, refs = refs[0], refs[1:]
    start_ref, g1_ref, wqkv_ref, wkvt_ref, wo_ref, g2_ref, wc_ref = refs[:7]
    srcs, refs = refs[7 : 7 + moves], refs[7 + moves :]
    q_ref, k_ref, v_ref, kt_ref, ob_ref, lse_ref, h_ref, gate_ref, mg_ref = refs[:9]
    dsts, refs = refs[9 : 9 + moves], refs[9 + moves :]
    if not packed:
        x_out, refs = refs[0], refs[1:]
    vt_all, bias, own, send_sem, recv_sem = refs[:5]
    sems = (send_sem, recv_sem)
    step = pl.program_id(0)
    width = q_ref.shape[1]
    pairs = width // (2 * HEAD_DIM)
    me = lax.axis_index("blk")
    later = [Exchange(nb, s, t, own, sems, n) for n, (s, t) in enumerate(zip(srcs, dsts))]
    if not packed:
        x_all = refs[5]
        first = Exchange(nb, x_src, x_all, own, sems, moves)
        keep = pltpu.make_async_copy(x_all, x_out, own.at[moves + 1])

    @pl.when(step == 0)
    def _():
        if not packed:
            first.local().start()
        arrive([peer("blk", me, d) for d in range(1, nb)])
        for d in range(1, nb):
            if not packed:
                first.copy(d).start()
        if packed:
            for x in later:
                x.start()

    @pl.when(step < blocks)
    def _():
        if packed:
            block = step
            x = x_ref[pl.ds(pl.multiple_of(block * BLOCK, BLOCK), BLOCK), :]
        else:
            block = me ^ step
            pl.when(step == 0)(first.local().wait)
            for d in range(1, nb):
                pl.when(step == d)(first.copy(d).wait_recv)
            x = x_all[block]
        x = x.astype(F32)
        n1 = (x * rms(x) * g1_ref[...]).astype(BF)
        qkv = nn(n1, wqkv_ref[...]).astype(BF)
        at = pl.ds(pl.multiple_of(block * BLOCK, BLOCK), BLOCK)
        q_ref[at, :] = qkv[:, :width]
        k_ref[at, :] = qkv[:, width : 2 * width]
        v_ref[at, :] = qkv[:, 2 * width :]
        kvt = nt(wkvt_ref[...], n1).astype(BF)
        kt_ref[:, at] = kvt[:width]
        vt_all[:, at] = kvt[width:]

    if not packed:
        @pl.when(step == nb - 1)
        def _():
            for x in later:
                x.start()
            keep.start()

    masks = head_masks()

    def attend(i):
        low, count = key_range(packed, i)
        fill_bias(bias, start_ref, packed, i)

        def pair(hp, carry):
            lanes = pl.ds(pl.multiple_of(hp * 2 * HEAD_DIM, 2 * HEAD_DIM), 2 * HEAD_DIM)
            q_pair = q_ref[i * BLOCK : (i + 1) * BLOCK, lanes]
            k_pair = k_ref[low : low + count, lanes]
            for h in range(2):
                scores = add_bias(nt(k_pair, q_pair * masks[h]), bias, packed, count)
                top = jnp.max(scores, axis=0, keepdims=True)
                p = jnp.exp((scores - top) * SCALE)
                total = jnp.sum(p, axis=0, keepdims=True)
                rows = pl.ds(pl.multiple_of(hp * 2 * HEAD_DIM + h * HEAD_DIM, HEAD_DIM), HEAD_DIM)
                o = nn(vt_all[rows, low : low + count], p.astype(BF))
                ob_ref[rows, :] = (o * (1.0 / total)).astype(BF)
                lse_ref[pl.ds(hp * 2 + h, 1), :] = top * SCALE + jnp.log(total)
            return carry

        lax.fori_loop(0, pairs, pair, 0)

    for i in range(blocks):
        pl.when(step == blocks + i)(functools.partial(attend, i))

    @pl.when(step >= blocks)
    def _():
        if packed:
            x = x_ref[pl.ds(pl.multiple_of((step - blocks) * BLOCK, BLOCK), BLOCK), :]
        else:
            x = x_all[step - blocks]
        h = x.astype(F32) + tn(ob_ref[...], wo_ref[...])
        h_ref[...] = h
        n2 = (h * rms(h) * g2_ref[...]).astype(BF)
        logits = nt(wc_ref[...], n2)
        rows = logits.shape[0]
        match = group_match(rows, BLOCK)
        logits = jnp.where(match, logits, MASKED)
        e = jnp.where(match, jnp.exp(logits - jnp.max(logits, axis=1, keepdims=True)), 0.0)
        gate = e / jnp.sum(e, axis=1, keepdims=True)
        gate_ref[...] = gate
        mg = nn(gate.astype(BF), n2).astype(BF).astype(F32)
        half = rows // mg_ref.shape[0]
        for j in range(mg_ref.shape[0]):
            mg_ref[j] = mg[j * half : (j + 1) * half]

    @pl.when(step == 2 * blocks - 1)
    def _():
        if not packed:
            keep.wait()
            for d in range(1, nb):
                first.copy(d).wait_send()
        for x in later:
            x.wait()


def gelu_both(u):
    c = 0.7978845608028654
    t = jnp.tanh(c * (u + 0.044715 * (u * u * u)))
    act = 0.5 * u * (1.0 + t)
    slope = 0.5 * (1.0 + t) + 0.5 * u * (1.0 - t * t) * (c * (1.0 + 3 * 0.044715 * (u * u)))
    return act, slope


def same_plane(far, d):
    return {"dp": lax.axis_index("dp") ^ far, "blk": lax.axis_index("blk") ^ d}


def plane_steps(nb):
    return [(far, d) for far in (0, 1) for d in range(0, nb, 2) if far or d]


def experts_kernel(micros, blocks, nb, *refs):
    mgs, gates = refs[:micros], refs[micros : 2 * micros]
    cot_ref, win_ref, wback_ref = refs[2 * micros : 2 * micros + 3]
    eo_ref, dmg_ref, all_ref, factors, mine, gathered, send_sem, recv_sem = refs[2 * micros + 3 :]
    sems = (send_sem, recv_sem)
    e, c = pl.program_id(0), pl.program_id(1)
    at = e * pl.num_programs(1) + c
    last = pl.num_programs(0) * pl.num_programs(1) - 1
    per = BLOCK // GROUP
    n_exp = factors.shape[0]
    groups = micros * blocks * per
    blk = lax.axis_index("blk")
    kind = blk % n_exp
    steps = plane_steps(nb)

    def core_copy():
        return remote(factors.at[1 - kind], mine.at[1], sems, 0, peer("blk", blk, 1))

    def plane_copy(n):
        return remote(mine, gathered.at[n], sems, 1 + n, same_plane(*steps[n]))

    @pl.when(at == 0)
    def _():
        for j in range(n_exp):
            factors[j, 0] = jnp.concatenate([r[j] for r in mgs], axis=0).astype(BF)
            parts = []
            for m in range(micros):
                for i in range(blocks):
                    part = gates[m][:, i * BLOCK : (i + 1) * BLOCK].astype(BF)
                    d = nn(part, cot_ref[m, i * BLOCK : (i + 1) * BLOCK, :])
                    parts.append(d[j * per : (j + 1) * per])
            factors[j, 1] = jnp.concatenate(parts, axis=0).astype(BF)
        arrive([peer("blk", blk, 1)] + [same_plane(*s) for s in steps])
        core_copy().start()
        mine[0] = factors[kind]

    mg, deo = factors[e, 0], factors[e, 1]
    act, slope = gelu_both(nn(mg, win_ref[0]))
    eo_part = nn(act.astype(BF), wback_ref[0])
    du = (slope * nt(deo, wback_ref[0])).astype(BF)
    dmg_part = nt(du, win_ref[0])

    @pl.when(c == 0)
    def _():
        eo_ref[0] = eo_part
        dmg_ref[0] = dmg_part

    @pl.when(c > 0)
    def _():
        eo_ref[0] += eo_part
        dmg_ref[0] += dmg_part

    @pl.when(at == 2)
    def _():
        core_copy().wait()
        for n in range(len(steps)):
            plane_copy(n).start()

    @pl.when(at == last)
    def _():
        for n in range(len(steps)):
            plane_copy(n).wait()
        for n in range(len(steps) + 1):
            piece = mine[...] if n == 0 else gathered[n - 1]
            for f in range(2):
                for j in range(2):
                    rows = slice((2 * n + j) * groups, (2 * n + j + 1) * groups)
                    all_ref[f, rows, :] = piece[j, f]


class Return:
    def __init__(self, nb, buf, out, own, sems, base):
        self.nb, self.buf, self.out, self.own, self.sems, self.base = nb, buf, out, own, sems, base
        self.me = lax.axis_index("blk")

    def local(self):
        return pltpu.make_async_copy(
            self.buf.at[self.me], self.out.at[self.me], self.own.at[self.base]
        )

    def copy(self, d):
        return remote(
            self.buf.at[self.me ^ d], self.out.at[self.me], self.sems,
            self.base * (self.nb - 1) + d - 1, peer("blk", self.me, d),
        )

    def start(self, i):
        pl.when(i == self.me)(self.local().start)
        for d in range(1, self.nb):
            pl.when(i == (self.me ^ d))(self.copy(d).start)

    def wait(self):
        self.local().wait()
        for d in range(1, self.nb):
            self.copy(d).wait()


def other_plane(d):
    return {"dp": lax.axis_index("dp") ^ (2 * d)}


def pair_sum(parts):
    while len(parts) > 1:
        parts = [parts[n] + parts[n + 1] for n in range(0, len(parts), 2)]
    return parts[0]


def my_part():
    return lax.axis_index("blk") // 2 + (lax.axis_size("blk") // 2) * (lax.axis_index("dp") % 2)


def backward_kernel(packed, blocks, nb, planes, first, x_ref, cot_ref, h_ref, gate_ref, eo_ref, dmg_ref,
                    ob_ref, lse_ref, q_ref, k_ref, v_ref, kt_ref, start_ref, g1_ref, g2_ref, wc_ref,
                    wqt_ref, wk_ref, wv_ref, wo_ref, *refs):
    if first:
        (factors, win_hbm, wback_hbm), refs = refs[:3], refs[3:]
        (act_ref, gi_ref, gall_ref, small_ref, piece_ref), refs = refs[:5], refs[5:]
    else:
        before, refs = refs[:2], refs[2:]
        (act_ref, gi_ref, gall_ref, small_ref), refs = refs[:4], refs[4:]
    dk_acc, dv_acc, dqt, dob, dobt, delta, bias, act_buf, gi_buf, own, send_sem, recv_sem = refs[:12]
    sems = (send_sem, recv_sem)
    step = pl.program_id(0)
    block = blocks - 1 - step
    width = x_ref.shape[1]
    pairs = width // (2 * HEAD_DIM)
    heads = width // HEAD_DIM
    me = lax.axis_index("blk")
    act_out = Return(nb, act_buf, act_ref, own, sems, 0)
    gi_out = Return(nb, gi_buf, gi_ref, own, sems, 1)
    if first:
        win, wback, ours, theirs, load_sem, send_z, recv_z = refs[12:]
        kind, part, plane = me % 2, my_part(), lax.axis_index("dp") // 2
        cut = win.shape[1]
        columns = pl.ds(pl.multiple_of(part * cut, cut), cut)
        loads = [
            pltpu.make_async_copy(win_hbm.at[kind, :, columns], win, load_sem.at[0]),
            pltpu.make_async_copy(wback_hbm.at[kind, columns, :], wback, load_sem.at[1]),
        ]

        def plane_copy(d):
            return remote(ours.at[plane ^ d], theirs.at[d - 1], (send_z, recv_z), d - 1, other_plane(d))

    @pl.when(step == 0)
    def _():
        partners = [peer("blk", me, d) for d in range(1, nb)]
        if first:
            partners += [other_plane(d) for d in range(1, planes)]
            for c in loads:
                c.start()
        arrive(partners)
        dk_acc[...] = jnp.zeros_like(dk_acc)
        dv_acc[...] = jnp.zeros_like(dv_acc)
        if first:
            gall_ref[...] = jnp.zeros_like(gall_ref)
            small_ref[...] = jnp.zeros_like(small_ref)
            for c in loads:
                c.wait()
            mg, deo = factors[0], factors[1]
            act, slope = gelu_both(nn(mg, win[...]))
            du = (slope * nt(deo, wback[...])).astype(BF)
            rows = width // planes
            g_in = tn(mg, du).astype(BF)
            for n in range(planes):
                ours[n, 0] = g_in[n * rows : (n + 1) * rows]
            rows = cut // planes
            g_back = tn(act.astype(BF), deo).astype(BF)
            for n in range(planes):
                ours[n, 1] = g_back[n * rows : (n + 1) * rows]
            for d in range(1, planes):
                plane_copy(d).start()
        else:
            gall_ref[...] = before[0][...]
            small_ref[...] = before[1][...]

    h = h_ref[...]
    cot_b = cot_ref[...]
    dout = cot_b.astype(F32)
    r2 = rms(h)
    z = h * r2
    n2 = (z * g2_ref[...]).astype(BF)
    gate = gate_ref[...]
    rows = gate.shape[0]
    gate_b = gate.astype(BF)
    gate_low = (gate - gate_b.astype(F32)).astype(BF)
    eo = jnp.concatenate([eo_ref[j] for j in range(eo_ref.shape[0])], axis=0)
    dmg = jnp.concatenate([dmg_ref[j] for j in range(dmg_ref.shape[0])], axis=0).astype(BF)
    eo_b = eo.astype(BF)
    eo_low = (eo - eo_b.astype(F32)).astype(BF)
    mixed = tn(
        jnp.concatenate([gate_b, gate_low, gate_b], axis=0),
        jnp.concatenate([eo_b, eo_b, eo_low], axis=0),
    )
    act_buf[block] = (h + mixed).astype(BF)
    act_out.start(block)
    dw2 = nt(jnp.concatenate([eo_b, eo_low], axis=0), cot_b)
    dw = dw2[:rows] + dw2[rows:] + nt(dmg, n2)
    wdw = gate * dw
    dlog = (wdw - gate * jnp.sum(wdw, axis=1, keepdims=True)).astype(BF)
    dn2 = tn(
        jnp.concatenate([gate_b, dlog], axis=0),
        jnp.concatenate([dmg, wc_ref[...]], axis=0),
    )
    small_ref[0:rows, :] += nn(dlog, n2)
    dg2 = dn2 * z
    small_ref[rows : rows + 1, :] += jnp.sum(dg2, axis=0, keepdims=True)
    a = dn2 * g2_ref[...]
    dh = dout + r2 * (a - z * jnp.mean(a * z, axis=-1, keepdims=True))
    da = dh.astype(BF)
    dob[...] = nt(da, wo_ref[...]).astype(BF)
    dobt[...] = nt(wo_ref[...], da).astype(BF)
    gall_ref[3 * width :, :] += nn(ob_ref[...], da)
    prod = dobt[...].astype(F32) * ob_ref[...].astype(F32)
    for hd in range(heads):
        delta[hd : hd + 1, :] = jnp.sum(
            prod[hd * HEAD_DIM : (hd + 1) * HEAD_DIM], axis=0, keepdims=True
        )
    masks = head_masks()

    def attend(i):
        low, count = key_range(packed, i)
        fill_bias(bias, start_ref, packed, i)
        keys = slice(low, low + count)

        def pair(hp, carry):
            lanes = pl.ds(pl.multiple_of(hp * 2 * HEAD_DIM, 2 * HEAD_DIM), 2 * HEAD_DIM)
            q_pair, dob_pair = q_ref[:, lanes], dob[:, lanes]
            k_pair, v_pair = k_ref[keys, lanes], v_ref[keys, lanes]
            dk_sum = dv_sum = None
            for h in range(2):
                qm, dm = q_pair * masks[h], dob_pair * masks[h]
                scores = add_bias(nt(k_pair, qm), bias, packed, count)
                p = jnp.exp(scores * SCALE - lse_ref[pl.ds(hp * 2 + h, 1), :])
                dp = nt(v_pair, dm)
                ds = (p * (dp - delta[pl.ds(hp * 2 + h, 1), :])).astype(BF)
                rows_h = pl.ds(pl.multiple_of(hp * 2 * HEAD_DIM + h * HEAD_DIM, HEAD_DIM), HEAD_DIM)
                dqt[rows_h, :] = (nn(kt_ref[rows_h, keys], ds) * SCALE).astype(BF)
                dk_part, dv_part = nn(ds, qm), nn(p.astype(BF), dm)
                dk_sum = dk_part if dk_sum is None else dk_sum + dk_part
                dv_sum = dv_part if dv_sum is None else dv_sum + dv_part
            dk_acc[keys, lanes] += dk_sum
            dv_acc[keys, lanes] += dv_sum
            return carry

        lax.fori_loop(0, pairs, pair, 0)

    for i in range(blocks):
        pl.when(step == blocks - 1 - i)(functools.partial(attend, i))

    at = pl.ds(pl.multiple_of(block * BLOCK, BLOCK), BLOCK)
    dk = (dk_acc[at, :] * SCALE).astype(BF)
    dv = dv_acc[at, :].astype(BF)
    x = x_ref[...].astype(F32)
    r1 = rms(x)
    z1 = x * r1
    n1 = (z1 * g1_ref[...]).astype(BF)
    dq_t = dqt[...]
    dn1 = tn(dq_t, wqt_ref[...]) + nt(dk, wk_ref[...]) + nt(dv, wv_ref[...])
    small_ref[rows + 8 : rows + 9, :] += jnp.sum(dn1 * z1, axis=0, keepdims=True)
    b = dn1 * g1_ref[...]
    gi = dh + r1 * (b - z1 * jnp.mean(b * z1, axis=-1, keepdims=True))
    gi_buf[block] = gi.astype(BF)
    gi_out.start(block)
    gall_ref[:width, :] += nn(dq_t, n1)
    gkv = tn(n1, jnp.concatenate([dk, dv], axis=1))
    gall_ref[width : 2 * width, :] += gkv[:, :width]
    gall_ref[2 * width : 3 * width, :] += gkv[:, width:]

    @pl.when(step == blocks - 1)
    def _():
        act_out.wait()
        gi_out.wait()
        if first:
            for d in range(1, planes):
                plane_copy(d).wait()
            parts = [ours[plane].astype(F32)] + [theirs[d].astype(F32) for d in range(planes - 1)]
            piece_ref[...] = pair_sum(parts).astype(BF)


def tail_kernel(nb, planes, gall, small, piece, flat, small_out, gin, gback, s1, r1, s2, r2, s3, r3,
                fl, acc, rs, small_acc, own, send_sem, recv_sem):
    sems = (send_sem, recv_sem)
    blk, dp = lax.axis_index("blk"), lax.axis_index("dp")
    kind, part, plane = blk % 2, my_part(), dp // 2
    width = gall.shape[1]
    total = gall.shape[0]
    steps = plane_steps(nb)
    members = len(steps) + 1
    core = peer("blk", blk, 1)
    half, quarter = total // 2, total // 2 // members
    share = quarter // planes
    cut = gin.shape[2] // members
    rows = piece.shape[1]
    counter = iter(range(10000))
    waits = []

    def send(src, dst, where):
        c = remote(src, dst, sems, next(counter), where)
        c.start()
        return c

    def done(copies):
        for c in copies:
            c.wait_recv()
        waits.extend(copies)

    def part_of(far, d):
        return ((blk ^ d) // 2) + (nb // 2) * ((dp % 2) ^ far)

    arrive([core] + [same_plane(*s) for s in steps] + [other_plane(d) for d in range(1, planes)])

    def rows_of(n, size):
        return pl.ds(pl.multiple_of(n * size, size), size)

    s1[...] = gall[rows_of(1 - kind, half), :].astype(BF)
    c1 = [send(s1, r1, core), send(small, rs.at[0], core)]
    windows = lambda e, p, z: (
        (e, rows_of(z, rows), pl.ds(pl.multiple_of(p * cut, cut), cut)),
        (e, pl.ds(pl.multiple_of(p * cut + z * rows, rows), rows), slice(None)),
    )
    w_in, w_back = windows(kind, part, plane)
    locals_ = [
        pltpu.make_async_copy(piece.at[0], gin.at[w_in], own.at[0]),
        pltpu.make_async_copy(piece.at[1], gback.at[w_back], own.at[1]),
    ]
    for c in locals_:
        c.start()
    cz = []
    for d in range(1, planes):
        cz.append(send(piece.at[0], gin.at[w_in], other_plane(d)))
        cz.append(send(piece.at[1], gback.at[w_back], other_plane(d)))

    done(c1)
    acc[...] = gall[rows_of(kind, half), :] + r1[...].astype(F32)
    small_acc[0] = small[...] + rs[0]
    c2 = []
    for n, (far, d) in enumerate(steps):
        p = part_of(far, d)
        s2[n] = acc[rows_of(p, quarter), :].astype(BF)
        c2.append(send(s2.at[n], r2.at[n], same_plane(far, d)))
        c2.append(send(small_acc.at[0], rs.at[1 + n], same_plane(far, d)))
    done(cz)
    for c in locals_:
        c.wait()
    columns = pl.ds(pl.multiple_of(part * cut, cut), cut)
    w_in, w_back = (kind, slice(None), columns), (kind, columns, slice(None))
    cp = []
    done(c2)
    mine = pair_sum([acc[rows_of(part, quarter), :]] + [r2[n].astype(F32) for n in range(members - 1)])
    small_acc[1] = pair_sum([small_acc[0]] + [rs[1 + n] for n in range(members - 1)])
    c3 = []
    acc[0:quarter, :] = mine
    s3[...] = mine.astype(BF)
    for d in range(1, planes):
        c3.append(send(s3.at[rows_of(plane ^ d, share), :], r3.at[d - 1], other_plane(d)))
        c3.append(send(small_acc.at[1], rs.at[members + d - 1], other_plane(d)))
    for far, d in steps:
        cp.append(send(gin.at[w_in], gin.at[w_in], same_plane(far, d)))
        cp.append(send(gback.at[w_back], gback.at[w_back], same_plane(far, d)))
    done(c3)
    mine = pair_sum([acc[rows_of(plane, share), :]] + [r3[d].astype(F32) for d in range(planes - 1)])
    small_out[...] = pair_sum([small_acc[1]] + [rs[members + d] for d in range(planes - 1)])
    at = pl.multiple_of(kind * half + part * quarter + plane * share, share)
    fl[pl.ds(at, share), :] = mine.astype(BF)
    w = fl.at[pl.ds(at, share), :]
    c4 = [send(w, w, other_plane(d)) for d in range(1, planes)]
    done(c4)
    at = pl.multiple_of(kind * half + part * quarter, quarter)
    w = fl.at[pl.ds(at, quarter), :]
    c5 = [send(w, w, same_plane(far, d)) for far, d in steps]
    done(c5)
    w = fl.at[rows_of(kind, half), :]
    c6 = [send(w, w, core)]
    done(cp)
    c7 = [send(gin.at[kind], gin.at[kind], core), send(gback.at[kind], gback.at[kind], core)]
    done(c6)
    flat[...] = fl[...]
    done(c7)
    for c in waits:
        c.wait_send()


def whole(shape):
    return pl.BlockSpec(shape, lambda *_: (0,) * len(shape))


def held(shape):
    return pl.BlockSpec(shape, lambda *_: (0,) * len(shape), pipeline_mode=pl.Buffered(1))


ANY = pl.BlockSpec(memory_space=pl.ANY)
DMA = pltpu.SemaphoreType.DMA


def shaped(shape, dtype):
    return jax.ShapeDtypeStruct(shape, dtype)


def params(number):
    return pltpu.CompilerParams(
        vmem_limit_bytes=VMEM_LIMIT, collective_id=number, has_side_effects=True
    )


def forward_call(packed, x, start, g1, wqkv, wkvt, wo, g2, wc, srcs):
    nb = lax.axis_size("blk")
    width = wo.shape[0]
    length = nb * BLOCK
    blocks = length // BLOCK
    rows = wc.shape[0]
    per = BLOCK // GROUP
    experts = rows // per
    phase = lambda i: jnp.maximum(i - blocks, 0)
    col_block = lambda n: pl.BlockSpec((n, BLOCK), lambda i: (0, phase(i)))
    moves = len(srcs)
    copies = moves + (not packed)
    return pl.pallas_call(
        functools.partial(forward_kernel, packed, blocks, nb, moves),
        grid=(2 * blocks,),
        in_specs=[
            held(x.shape) if packed else ANY, col_block(1), held(g1.shape), held(wqkv.shape),
            held(wkvt.shape), held(wo.shape), held(g2.shape), held(wc.shape),
        ] + [ANY] * moves,
        out_specs=[
            whole((length, width)), whole((length, width)), whole((length, width)),
            whole((width, length)), col_block(width), col_block(width // HEAD_DIM),
            pl.BlockSpec((BLOCK, width), lambda i: (phase(i), 0)),
            col_block(rows),
            pl.BlockSpec((experts, per, width), lambda i: (0, phase(i), 0)),
        ] + [ANY] * copies,
        out_shape=[
            shaped((length, width), BF), shaped((length, width), BF), shaped((length, width), BF),
            shaped((width, length), BF), shaped((width, length), BF),
            shaped((width // HEAD_DIM, length), F32),
            shaped((length, width), F32),
            shaped((rows, length), F32),
            shaped((experts, length // GROUP, width), F32),
        ] + [shaped(a.shape, a.dtype) for a in srcs]
        + ([] if packed else [shaped((nb, BLOCK, width), BF)]),
        scratch_shapes=[
            pltpu.VMEM((width, length), BF), pltpu.VMEM((length, BLOCK), F32),
            DMA((copies + 1,)), DMA((copies * (nb - 1),)), DMA((copies * (nb - 1),)),
        ] + ([] if packed else [pltpu.VMEM((nb, BLOCK, width), BF)]),
        compiler_params=params(2 if packed else 1),
        name="attention_forward",
    )(x, start, g1, wqkv, wkvt, wo, g2, wc, *srcs)


def experts_call(mgs, gates, cot, w_in, w_back):
    micros, length, width = cot.shape
    experts, _, ff = w_in.shape
    nb = lax.axis_size("blk")
    blocks = length // BLOCK
    groups = micros * length // GROUP
    chunk = min(CHUNK, ff)
    by_expert = lambda n: pl.BlockSpec((1, n, width), lambda e, c: (e, 0, 0))
    members = len(plane_steps(nb))
    return pl.pallas_call(
        functools.partial(experts_kernel, micros, blocks, nb),
        grid=(experts, ff // chunk),
        in_specs=[held(a.shape) for a in mgs] + [held(a.shape) for a in gates]
        + [
            held(cot.shape),
            pl.BlockSpec((1, width, chunk), lambda e, c: (e, 0, c)),
            pl.BlockSpec((1, chunk, width), lambda e, c: (e, c, 0)),
        ],
        out_specs=[by_expert(groups)] * 2 + [whole((2, 2 * (members + 1) * groups, width))],
        out_shape=[shaped((experts, groups, width), F32)] * 2
        + [shaped((2, 2 * (members + 1) * groups, width), BF)],
        scratch_shapes=[
            pltpu.VMEM((experts, 2, groups, width), BF), pltpu.VMEM((2, 2, groups, width), BF),
            pltpu.VMEM((members, 2, 2, groups, width), BF), DMA((members + 1,)), DMA((members + 1,)),
        ],
        compiler_params=params(3),
        name="experts",
    )(*mgs, *gates, cot, w_in, w_back)


def backward_call(packed, micro, x, cot, h, gate, eo, dmg, ob, lse, q, k, v, kt, start, g1, g2, wc,
                  wqt, wk, wv, wo, extra, first):
    nb = lax.axis_size("blk")
    planes = lax.axis_size("dp") // 2
    length, width = x.shape
    blocks = length // BLOCK
    rows = wc.shape[0]
    per = BLOCK // GROUP
    experts = rows // per
    heads = width // HEAD_DIM
    back = lambda i: blocks - 1 - i
    row_block = pl.BlockSpec((BLOCK, width), lambda i: (back(i), 0))
    col_block = lambda n: pl.BlockSpec((n, BLOCK), lambda i: (0, back(i)))
    group_block = pl.BlockSpec((experts, per, width), lambda i: (0, micro * blocks + back(i), 0))
    sums = [(4 * width, width), (rows + 16, width)]
    blocked = shaped((nb, BLOCK, width), BF)
    scratch = [
        pltpu.VMEM((length, width), F32), pltpu.VMEM((length, width), F32),
        pltpu.VMEM((width, BLOCK), BF), pltpu.VMEM((BLOCK, width), BF),
        pltpu.VMEM((width, BLOCK), BF), pltpu.VMEM((heads, BLOCK), F32),
        pltpu.VMEM((length, BLOCK), F32),
        pltpu.VMEM((nb, BLOCK, width), BF), pltpu.VMEM((nb, BLOCK, width), BF),
        DMA((2,)), DMA((2 * (nb - 1),)), DMA((2 * (nb - 1),)),
    ]
    out_specs = [ANY, ANY] + [whole(s) for s in sums]
    out_shape = [blocked, blocked] + [shaped(s, F32) for s in sums]
    if first:
        factors, w_in, w_back = extra
        cut = w_in.shape[2] // nb
        assert cut == width
        piece = (2, width // planes, cut)
        extra_specs = [held(factors.shape), ANY, ANY]
        out_specs.append(whole(piece))
        out_shape.append(shaped(piece, BF))
        scratch += [
            pltpu.VMEM((width, cut), BF), pltpu.VMEM((cut, width), BF),
            pltpu.VMEM((planes,) + piece, BF), pltpu.VMEM((planes - 1,) + piece, BF),
            DMA((2,)), DMA((planes - 1,)), DMA((planes - 1,)),
        ]
    else:
        extra_specs = [held(s) for s in sums]
    return pl.pallas_call(
        functools.partial(backward_kernel, packed, blocks, nb, planes, first),
        grid=(blocks,),
        in_specs=[
            row_block, row_block, row_block, col_block(rows), group_block, group_block,
            col_block(width), col_block(heads), row_block, held(k.shape), held(v.shape),
            held(kt.shape), col_block(1), held(g1.shape), held(g2.shape), held(wc.shape),
            held(wqt.shape), held(wk.shape), held(wv.shape), held(wo.shape),
        ] + extra_specs,
        out_specs=out_specs,
        out_shape=out_shape,
        scratch_shapes=scratch,
        compiler_params=params(4 if first else 5),
        name="attention_backward",
    )(x, cot, h, gate, eo, dmg, ob, lse, q, k, v, kt, start, g1, g2, wc, wqt, wk, wv, wo, *extra)


def tail_call(gall, small, piece, ff):
    nb = lax.axis_size("blk")
    planes = lax.axis_size("dp") // 2
    total, width = gall.shape
    members = len(plane_steps(nb)) + 1
    half, quarter = total // 2, total // 2 // members
    share = quarter // planes
    copies = 5 + 5 * (planes - 1) + 5 * (members - 1)
    vm = pl.BlockSpec(memory_space=pltpu.VMEM)
    return pl.pallas_call(
        functools.partial(tail_kernel, nb, planes),
        in_specs=[vm, vm, vm],
        out_specs=[vm, vm, ANY, ANY],
        out_shape=[
            shaped((total, width), BF), shaped(small.shape, F32),
            shaped((2, width, ff), BF), shaped((2, ff, width), BF),
        ],
        scratch_shapes=[
            pltpu.VMEM((half, width), BF), pltpu.VMEM((half, width), BF),
            pltpu.VMEM((members - 1, quarter, width), BF),
            pltpu.VMEM((members - 1, quarter, width), BF), pltpu.VMEM((quarter, width), BF),
            pltpu.VMEM((planes - 1, share, width), BF), pltpu.VMEM((total, width), BF),
            pltpu.VMEM((half, width), F32),
            pltpu.VMEM((members + planes - 1,) + small.shape, F32),
            pltpu.VMEM((2,) + small.shape, F32),
            DMA((2,)), DMA((copies,)), DMA((copies,)),
        ],
        compiler_params=params(6),
        name="gradient_sums",
    )(gall, small, piece)


def local(block_input, segment_ids, gain_one, w_query, w_key, w_value, w_out, gain_two, w_ctrl,
          w_in, w_back, cotangent):
    micros, seqs, rows, width = block_input.shape
    experts, _, ff = w_in.shape
    nb = lax.axis_size("blk")
    length = nb * rows
    per = BLOCK // GROUP

    g1, g2 = gain_one.reshape(1, width), gain_two.reshape(1, width)
    wqkv = jnp.concatenate([w_query, w_key, w_value], axis=1)
    wkvt = jnp.concatenate([w_key, w_value], axis=1).T
    wqt = w_query.T
    wc = jnp.repeat(w_ctrl.T, per, axis=0)
    no_start = jnp.zeros((1, length), jnp.int32)

    seg_src = segment_ids.reshape(nb, 2, rows // 2)
    *fwd0, x1, seg, x0 = forward_call(
        False, block_input[0], no_start, g1, wqkv, wkvt, w_out, g2, wc, (block_input[1], seg_src)
    )
    seg = seg.reshape(1, length)
    start = jnp.sum((seg.reshape(length, 1) < seg).astype(jnp.int32), axis=0, keepdims=True)
    x1 = x1.reshape(length, width)
    *fwd1, cot0, cot1 = forward_call(
        True, x1, start, g1, wqkv, wkvt, w_out, g2, wc, (cotangent[0], cotangent[1])
    )
    xs = [x0.reshape(length, width), x1]
    cots = [cot0.reshape(length, width), cot1.reshape(length, width)]
    fwd = [fwd0, fwd1]
    starts = [no_start, start]
    eo, dmg, factors = experts_call(
        [f[8] for f in fwd], [f[7] for f in fwd], jnp.stack(cots), w_in, w_back
    )
    acts, gis = [], []
    extra = (factors, w_in, w_back)
    for m in range(micros):
        q, k, v, kt, ob, lse, h, gate, _ = fwd[m]
        act, gi, *sums = backward_call(
            m > 0, m, xs[m], cots[m], h, gate, eo, dmg, ob, lse, q, k, v, kt, starts[m], g1, g2, wc,
            wqt, w_key, w_value, w_out, extra, m == 0,
        )
        acts.append(act)
        gis.append(gi)
        if m == 0:
            *sums, piece = sums
        extra = sums
    flat, small, grad_in, grad_back = tail_call(*sums, piece, ff)
    flat = flat.astype(F32).reshape(4, width, width)
    ctrl = jnp.sum(small[: experts * per].reshape(experts, per, width), axis=1).T
    return (
        jnp.stack(acts), jnp.stack(gis), small[experts * per + 8], flat[0].T, flat[1], flat[2],
        flat[3], small[experts * per], ctrl, grad_in.astype(F32), grad_back.astype(F32),
    )


def solution(mesh):
    data = P(None, "dp", "blk", None)
    in_specs = (data, P("dp", "blk")) + (P(),) * 9 + (data,)
    out_specs = (data, data) + (P(),) * 9
    return jax.shard_map(local, mesh=mesh, in_specs=in_specs, out_specs=out_specs, check_vma=False)
```

time: 542 us -> 336 us (0.62)
  waiting for transfers between devices: 207 us -> 0 us
  Pallas kernels: 136 us -> 292 us
  local copies, waits for them, and re-layouts: 93.9 us -> 18.8 us
  starting transfers between devices: 66.9 us -> 0 us
  matrix products: 5.93 us -> 0 us
    ppermute x65 -> x0, waiting for transfers between devices: 207 us -> none  [the longest x7 62.3 us: local(): lax.ppermute(piece, ('dp', 'blk'), [(i * nb + j, (i ^ far) * nb + (j ^ d)...]
    pallas_call x5 -> x6, Pallas kernels: 136 us -> 292 us  [the longest x2 103 us: backward_call(): pl.pallas_call(functools.partial(backward_kernel, packed, blocks, nb, pla...]
    ppermute x65 -> x0, starting transfers between devices: 66.9 us -> none  [the longest x15 27.2 us: plane_swap(): return lax.ppermute(a, 'dp', [(i, i ^ 2 * d) for i in range(nd)])]
    dynamic_update_slice x56 -> x0, local copies, waits for them, and re-layouts: 25.8 us -> none  [the longest x9 8.16 us: trade(): lax.dynamic_update_index_in_dim(jnp.zeros_like(pieces), take(pieces, me),...]
    transpose x3 -> x1, local copies, waits for them, and re-layouts: 24 us -> 0.07 us  [local(): flat[0]]
    squeeze x8 -> x2, local copies, waits for them, and re-layouts: 11.9 us -> 3.09 us  [the longest x1 1.54 us: local(): block_input[1]]
    dot_general x3 -> x0, matrix products: 5.93 us -> none  [dot(): lax.dot_general(a, b, (((ca,), (cb,)), ((), ())), preferred_element_type=...]
    unnamed x62 -> x30, local copies, waits for them, and re-layouts: 14.2 us -> 8.48 us
  transfers between devices with their start and end apart: 65 -> 0, of which waited for: 23 -> 0; matrix products, arithmetic and copies ran while one was open for 20% -> 0% of each run, Pallas kernels for 10% -> 0%
where the time goes in v2:
time: 336 us; the launch traced here: 334 us
  Pallas kernels  292 us (87%)
  other arithmetic  23.2 us (7%)
  local copies, waits for them, and re-layouts  18.8 us (6%)
    pallas_call x2, Pallas kernels, backward_call(): pl.pallas_call(functools.partial(backward_kernel, packed, blocks, nb, pla...  103 us
    pallas_call x1, Pallas kernels, tail_call(): pl.pallas_call(functools.partial(tail_kernel, nb, planes), in_specs=[vm,...  92.4 us
    pallas_call x2, Pallas kernels, forward_call(): pl.pallas_call(functools.partial(forward_kernel, packed, blocks, nb, move...  74 us
    pallas_call x1, Pallas kernels, experts_call(): pl.pallas_call(functools.partial(experts_kernel, micros, blocks, nb), gri...  21.8 us
    unnamed x30, local copies, waits for them, and re-layouts  8.48 us
    convert_element_type x1, other arithmetic, local(): grad_in.astype(F32)  6.8 us

profile of v2, /device:TPU:0, one launch (start us, length us, event | category | flops | bytes accessed | tf_op | source)
XLA Modules:
  0.0 334.3 jit_solution(17724070866500714005)
XLA Ops:
  0.6 0.0 copy-start
  0.7 0.0 copy-start.5
  0.7 0.7 copy-done
  1.3 1.3 reshape.64.refs_9_
  2.6 0.6 broadcast_bitcast_fusion.refs_7_.wc_ref
  3.2 2.0 copy.29
  5.3 0.0 copy-start.9
  5.3 1.3 copy.27
  6.6 0.0 copy-done.5
  6.6 0.0 copy-start.4
  6.6 0.2 copy.28
  6.8 1.0 maximum_bitcast_fusion.refs_4_
  7.9 0.0 copy-done.9
  7.9 0.0 copy-start.7
  7.9 0.0 copy-done.4
  8.0 1.5 copy-done.7
  9.5 0.0 copy-start.3
  9.5 0.0 copy-start.8
  9.5 1.5 slice_bitcast_fusion.3
  11.0 0.3 copy-done.3
  11.3 1.0 copy-done.8
  12.4 1.5 slice_bitcast_fusion.1
  13.9 0.6 broadcast_in_dim.9.refs_1_.start_ref
  14.5 43.7 %attention_forward.2 = (bf16[1024,512]{1,0:T(8,128)(2,1)}, bf16[1024,512]{1,0:T(8,128)(2,1)}, bf16[1024,512]{1,0:T(8,128)(2,1)}, bf16[512,1024]{1,0:T(8,128)(2,1...) custom-call(bf16[4,256,512]{2,1,0:T(8,128)(2,1)} %get-tuple-element., ...), custom_call_target="tpu_custom_call" | custom-call | tf_op jit(solution)/shard_map/attention_forward/pallas_call | solution.py:679
  58.2 1.8 convert_reduce_fusion
  60.0 30.4 %attention_forward.3 = (bf16[1024,512]{1,0:T(8,128)(2,1)}, bf16[1024,512]{1,0:T(8,128)(2,1)}, bf16[1024,512]{1,0:T(8,128)(2,1)}, bf16[512,1024]{1,0:T(8,128)(2,1...) custom-call(bf16[1024,512]{1,0:T(8,128)(2,1)} %bitcast.38, ...), custom_call_target="tpu_custom_call" | custom-call | tf_op jit(solution)/shard_map/attention_forward/pallas_call | solution.py:679
  90.4 3.1 pad_maximum_fusion.refs_4_
  93.4 21.8 %experts.1 = (f32[2,64,512]{2,1,0:T(8,128)}, f32[2,64,512]{2,1,0:T(8,128)}, bf16[2,512,512]{2,1,0:T(8,128)(2,1)}) custom-call(f32[2,32,512]{2,1,0:T(8,128)} %get-tuple-element.56.refs_0_, f32[2,32,512]{2,1,0:T(8,128)} %get-tuple-element.57.refs_1_, f32[16,1024]{1,0:T(8,128)} %get-tuple-element.55.refs_2_.gate_ref, ...), custom_call_target="tpu_custom_call" | custom-call | tf_op jit(solution)/shard_map/experts/pallas_call | solution.py:720
  115.2 54.0 %attention_backward.2 = (bf16[4,256,512]{2,1,0:T(8,128)(2,1)}, bf16[4,256,512]{2,1,0:T(8,128)(2,1)}, f32[2048,512]{1,0:T(8,128)}, f32[32,512]{1,0:T(8,128)}, bf16[2,128,512]{2,1,0:T(8,128)(2,1)}) custom-call(bf16[1024,512]{1,0:T(8,128)(2,1)} %bitcast.44, bf16[1024,512]{1,0:T(8,128)(2,1)} %bitcast.43, f32[1024,512]{1,0:T(8,128)} %get-tuple-element.54.h_ref, ...), custom_call_target="tpu_custom_call" | custom-call | tf_op jit(solution)/shard_map/attention_backward/pallas_call | solution.py:782
  169.2 0.0 copy-start.10
  169.2 0.0 copy-start.11
  169.2 49.4 %attention_backward.3 = (bf16[4,256,512]{2,1,0:T(8,128)(2,1)}, bf16[4,256,512]{2,1,0:T(8,128)(2,1)}, f32[2048,512]{1,0:T(8,128)}, f32[32,512]{1,0:T(8,128)}) custom-call(bf16[1024,512]{1,0:T(8,128)(2,1)} %bitcast.39, bf16[1024,512]{1,0:T(8,128)(2,1)} %bitcast.41, f32[1024,512]{1,0:T(8,128)} %get-tuple-element.70.h_ref, ...), custom_call_target="tpu_custom_call" | custom-call | tf_op jit(solution)/shard_map/attention_backward/pallas_call | solution.py:782
  218.6 0.0 copy-done.10
  218.6 0.0 copy-done.11
  218.6 3.9 %pad_maximum_fusion.1 = (bf16[2,4,256,512]{3,2,1,0:T(8,128)(2,1)}, bf16[2,4,256,512]{3,2,1,0:T(8,128)(2,1)}) fusion(bf16[1,4,256,512]{3,2,1,0:T(8,128)(2,1)} %bitcast.47, bf16[1,4,256,512]{3,2,1,0:T(8,128)(2,1)S(1)} %bitcast.45, bf16[1,4,256,512]{3,2,1,0:T(8,128)(2,1)} %bitcast.48, bf16[1,4,256,512]{3,2,1,0:T(8,128)(2,1)S(1)} %bitcast.46), kind=kLoop, calls=%fused_computation.2 | loop fusion | flops 2097152 | bytes 8388608 | tf_op jit(solution)/shard_map/stack | solution.py:880
  222.5 92.4 %gradient_sums.1 = (bf16[2048,512]{1,0:T(8,128)(2,1)}, f32[32,512]{1,0:T(8,128)}, bf16[2,512,2048]{2,1,0:T(8,128)(2,1)}, bf16[2,2048,512]{2,1,0:T(8,128)(2,1)}) custom-call(f32[2048,512]{1,0:T(8,128)} %get-tuple-element.82.gall, f32[32,512]{1,0:T(8,128)} %get-tuple-element.83.small, bf16[2,128,512]{2,1,0:T(8,128)(2,1)} %get-tuple-element.84.piece), custom_call_target="tpu_custom_call" | custom-call | tf_op jit(solution)/shard_map/gradient_sums/pallas_call | solution.py:808
  314.9 1.4 bitcast_reduce_fusion
  316.3 1.3 fusion.1
  317.6 0.0 copy-start.2
  317.6 3.3 fusion
  320.9 0.0 copy-done.2
  320.9 0.6 convert_element_type.13
  321.5 0.1 slice_bitcast_fusion
  321.6 1.3 copy.30
  322.9 6.8 %convert_element_type.14 = f32[2,512,2048]{2,1,0:T(8,128)} convert(bf16[2,512,2048]{2,1,0:T(8,128)(2,1)} %get-tuple-element.87) | non-fusion elementwise | flops 2097152 | bytes 12582912 | tf_op jit(solution)/shard_map/convert_element_type | solution.py:881
  329.7 0.0 copy-done.6
  329.7 4.6 %convert_element_type.15 = f32[2,2048,512]{2,1,0:T(8,128)} convert(bf16[2,2048,512]{2,1,0:T(8,128)(2,1)S(1)} %copy-done.6) | non-fusion elementwise | flops 2097152 | bytes 12582912 | tf_op jit(solution)/shard_map/convert_element_type | solution.py:881
  334.3 0.0 copy-done.1
  (5 shorter events, 0.1 us)
Async XLA Ops:
  0.6 0.7 copy-start
  0.7 5.9 %copy-start.5 = (bf16[512,512]{1,0:T(8,128)(2,1)S(1)}, bf16[512,512]{1,0:T(8,128)(2,1)}, u32[]{:S(2)}) copy-start(bf16[512,512]{1,0:T(8,128)(2,1)} %wv_ref.3) | copy-start | bytes 1572868
  5.3 2.6 copy-start.9
  6.6 1.3 copy-start.4
  7.9 1.6 copy-start.7
  9.5 1.9 copy-start.3
  9.5 2.9 copy-start.8
  169.2 49.4 %copy-start.10 = (bf16[4,256,512]{2,1,0:T(8,128)(2,1)S(1)}, bf16[4,256,512]{2,1,0:T(8,128)(2,1)}, u32[]{:S(2)}) copy-start(bf16[4,256,512]{2,1,0:T(8,128)(2,1)} %get-tuple-element.69) | copy-start | bytes 3145732
  169.2 49.4 %copy-start.11 = (bf16[4,256,512]{2,1,0:T(8,128)(2,1)S(1)}, bf16[4,256,512]{2,1,0:T(8,128)(2,1)}, u32[]{:S(2)}) copy-start(bf16[4,256,512]{2,1,0:T(8,128)(2,1)} %get-tuple-element.80) | copy-start | bytes 3145732
  317.6 3.3 copy-start.2
  322.9 6.8 %copy-start.6 = (bf16[2,2048,512]{2,1,0:T(8,128)(2,1)S(1)}, bf16[2,2048,512]{2,1,0:T(8,128)(2,1)}, u32[]{:S(2)}) copy-start(bf16[2,2048,512]{2,1,0:T(8,128)(2,1)} %get-tuple-element.88) | copy-start | bytes 12582916
  329.7 4.6 %copy-start.1 = (bf16[512,2]{0,1:T(2,128)(2,1)S(1)}, bf16[512,2]{0,1:T(2,128)(2,1)}, u32[]{:S(2)}) copy-start(bf16[512,2]{0,1:T(2,128)(2,1)} %param.20) | copy-start | bytes 6148

commit v3 on v2

v3 whole, which is shorter than its diff:
```python
import functools

import jax
import jax.numpy as jnp
from jax import lax
from jax.experimental import pallas as pl
from jax.experimental.pallas import tpu as pltpu
from jax.sharding import PartitionSpec as P

HEAD_DIM = 64
GROUP = 32
EPSILON = 1e-05
BLOCK = 256
CHUNK = 512
SCALE = 0.125
MASKED = -1e30
VMEM_LIMIT = 60 * 1024 * 1024
BF = jnp.bfloat16
F32 = jnp.float32
MESH = pl.DeviceIdType.MESH


def dot(a, b, ca, cb):
    return lax.dot_general(a, b, (((ca,), (cb,)), ((), ())), preferred_element_type=F32)


def nn(a, b):
    return dot(a, b, 1, 0)


def nt(a, b):
    return dot(a, b, 1, 1)


def tn(a, b):
    return dot(a, b, 0, 0)


def key_range(packed, i):
    low = max(0, i * BLOCK - BLOCK - BLOCK // 2) if packed else 0
    return low, (i + 1) * BLOCK - low


def head_masks():
    lane = lax.broadcasted_iota(jnp.int32, (1, 2 * HEAD_DIM), 1)
    first = (lane < HEAD_DIM).astype(F32).astype(BF)
    return first, (lane >= HEAD_DIM).astype(F32).astype(BF)


def group_match(rows, tokens):
    row = lax.broadcasted_iota(jnp.int32, (rows, tokens), 0)
    col = lax.broadcasted_iota(jnp.int32, (rows, tokens), 1)
    return (row % (tokens // GROUP)) == (col // GROUP)


def fill_bias(bias_ref, start_ref, packed, i):
    low, count = key_range(packed, i)
    q_pos = i * BLOCK + lax.broadcasted_iota(jnp.int32, (1, BLOCK), 1)
    if packed:
        k_pos = low + lax.broadcasted_iota(jnp.int32, (count, BLOCK), 0)
        allowed = (k_pos <= q_pos) & (k_pos >= start_ref[...])
        bias_ref[0:count, :] = jnp.where(allowed, 0.0, MASKED)
    else:
        k_pos = i * BLOCK + lax.broadcasted_iota(jnp.int32, (BLOCK, BLOCK), 0)
        bias_ref[0:BLOCK, :] = jnp.where(k_pos <= q_pos, 0.0, MASKED)


def add_bias(scores, bias_ref, packed, count):
    if packed:
        return scores + bias_ref[0:count, :]
    last = scores[count - BLOCK :, :] + bias_ref[0:BLOCK, :]
    if count == BLOCK:
        return last
    return jnp.concatenate([scores[: count - BLOCK, :], last], axis=0)


def rms(values):
    return lax.rsqrt(jnp.mean(values * values, axis=-1, keepdims=True) + EPSILON)


def peer(axis, me, d):
    return {axis: me ^ d}


def arrive(partners):
    barrier = pltpu.get_barrier_semaphore()
    for p in partners:
        pl.semaphore_signal(barrier, inc=1, device_id=p, device_id_type=MESH)
    pl.semaphore_wait(barrier, len(partners))


def remote(src, dst, sems, k, where):
    return pltpu.make_async_remote_copy(
        src_ref=src, dst_ref=dst, send_sem=sems[0].at[k], recv_sem=sems[1].at[k],
        device_id=where, device_id_type=MESH,
    )


class Exchange:
    def __init__(self, nb, src, dst, own, sems, base):
        self.nb, self.src, self.dst, self.own, self.sems, self.base = nb, src, dst, own, sems, base
        self.me = lax.axis_index("blk")

    def local(self):
        return pltpu.make_async_copy(
            self.src.at[self.me], self.dst.at[self.me], self.own.at[self.base]
        )

    def copy(self, d):
        return remote(
            self.src.at[self.me ^ d], self.dst.at[self.me], self.sems,
            self.base * (self.nb - 1) + d - 1, peer("blk", self.me, d),
        )

    def start(self):
        self.local().start()
        for d in range(1, self.nb):
            self.copy(d).start()

    def wait(self):
        self.local().wait()
        for d in range(1, self.nb):
            self.copy(d).wait()


def unit(n):
    row = lax.broadcasted_iota(jnp.int32, (n, n), 0)
    col = lax.broadcasted_iota(jnp.int32, (n, n), 1)
    return (row == col).astype(F32).astype(BF)


def split_three(a):
    high = a.astype(BF)
    rest = a - high.astype(F32)
    mid = rest.astype(BF)
    return [high, mid, (rest - mid.astype(F32)).astype(BF)]


def head_rows(heads, width):
    row = lax.broadcasted_iota(jnp.int32, (heads, width), 0)
    col = lax.broadcasted_iota(jnp.int32, (heads, width), 1)
    return (row == col // HEAD_DIM).astype(F32).astype(BF)


def forward_kernel(micros, blocks, nb, x_src, seg_src, cot_src, g1_ref, wq_ref, wk_ref, wv_ref, wo_ref,
                   g2_ref, wc_ref, q_ref, k_ref, v_ref, kt_ref, ob_ref, lse_ref, h_ref, gate_ref,
                   mg_ref, start_ref, x_out, cot_out, x_all, seg_all, bias, o_acc, sums, eye, own,
                   send_sem, recv_sem):
    sems = (send_sem, recv_sem)
    now = pl.program_id(0)
    span = 2 * blocks
    micro, step = now // span, now % span
    width = wo_ref.shape[0]
    pairs = width // (2 * HEAD_DIM)
    me = lax.axis_index("blk")
    xs = [Exchange(nb, x_src.at[m], x_all.at[m], own, sems, m) for m in range(micros)]
    segs = Exchange(nb, seg_src, seg_all, own, sems, micros)
    cots = [
        Exchange(nb, cot_src.at[m], cot_out.at[m], own, sems, micros + 1 + m) for m in range(micros)
    ]
    keep = pltpu.make_async_copy(x_all, x_out, own.at[2 * micros + 1])

    @pl.when(now == 0)
    def _():
        xs[0].local().start()
        eye[...] = unit(width)
        arrive([peer("blk", me, d) for d in range(1, nb)])
        for d in range(1, nb):
            xs[0].copy(d).start()

    @pl.when(step < blocks)
    def _():
        block = me ^ step
        for m in range(micros):
            pl.when((micro == m) & (step == 0))(xs[m].local().wait)
            for d in range(1, nb):
                pl.when((micro == m) & (step == d))(xs[m].copy(d).wait_recv)
        x = x_all[micro, block].astype(F32)
        n1 = (x * rms(x) * g1_ref[...]).astype(BF)
        at = pl.ds(pl.multiple_of(block * BLOCK, BLOCK), BLOCK)
        q_ref[0, at, :] = nn(n1, wq_ref[...]).astype(BF)
        k = nn(n1, wk_ref[...]).astype(BF)
        k_ref[0, at, :] = k
        v_ref[0, at, :] = nn(n1, wv_ref[...]).astype(BF)
        kt_ref[0, :, at] = nt(eye[...], k).astype(BF)

    @pl.when(now == nb - 1)
    def _():
        segs.start()
        for m in range(1, micros):
            xs[m].start()

    @pl.when(now == blocks)
    def _():
        for c in cots:
            c.start()

    @pl.when(now == span)
    def _():
        segs.wait()
        counts = [
            jnp.sum(jnp.sum((seg_all[...] < d).astype(F32), axis=0), keepdims=True)
            for d in range(1, nb * seg_all.shape[1] * seg_all.shape[2] // BLOCK)
        ]
        for b in range(blocks):
            seg = jnp.concatenate([seg_all[b, n : n + 1, :] for n in range(seg_all.shape[1])], axis=1)
            start = jnp.zeros(seg.shape, F32)
            for d, count in enumerate(counts):
                start = jnp.where(seg == d + 1, count, start)
            start_ref[b] = start.astype(jnp.int32)

    masks = head_masks()

    def attend(packed, i):
        low, count = key_range(packed, i)
        fill_bias(bias, start_ref[i], packed, i)
        for hp in range(pairs):
            lanes = slice(hp * 2 * HEAD_DIM, (hp + 1) * 2 * HEAD_DIM)
            q_pair = q_ref[0, i * BLOCK : (i + 1) * BLOCK, lanes]
            k_pair = k_ref[0, low : low + count, lanes]
            v_pair = v_ref[0, low : low + count, lanes]
            o_pair = None
            for h in range(2):
                scores = add_bias(nt(k_pair, q_pair * masks[h]), bias, packed, count)
                top = jnp.max(scores, axis=0, keepdims=True)
                p = jnp.exp((scores - top) * SCALE)
                total = jnp.sum(p, axis=0, keepdims=True)
                o = tn(p.astype(BF), v_pair * masks[h])
                o_pair = o if o_pair is None else o_pair + o
                sums[hp * 2 + h : hp * 2 + h + 1, :] = 1.0 / total
                lse_ref[0, hp * 2 + h : hp * 2 + h + 1, :] = top * SCALE + jnp.log(total)
            o_acc[:, lanes] = o_pair

    for m in range(micros):
        for i in range(blocks):
            pl.when(now == m * span + blocks + i)(functools.partial(attend, m > 0, i))

    @pl.when(step >= blocks)
    def _():
        heads = head_rows(sums.shape[0], width)
        scale = tn(
            jnp.concatenate(split_three(sums[...]), axis=0), jnp.concatenate([heads] * 3, axis=0)
        )
        ob = (o_acc[...] * scale).astype(BF)
        ob_ref[0] = ob
        h = x_all[micro, step - blocks].astype(F32) + nn(ob, wo_ref[...])
        h_ref[0] = h
        n2 = (h * rms(h) * g2_ref[...]).astype(BF)
        logits = nt(wc_ref[...], n2)
        rows = logits.shape[0]
        match = group_match(rows, BLOCK)
        logits = jnp.where(match, logits, MASKED)
        e = jnp.where(match, jnp.exp(logits - jnp.max(logits, axis=1, keepdims=True)), 0.0)
        gate = e / jnp.sum(e, axis=1, keepdims=True)
        gate_ref[...] = gate
        mg = nn(gate.astype(BF), n2).astype(BF).astype(F32)
        half = rows // mg_ref.shape[0]
        for j in range(mg_ref.shape[0]):
            mg_ref[j] = mg[j * half : (j + 1) * half]

    @pl.when(now == span + nb)
    def _():
        keep.start()

    @pl.when(now == micros * span - 1)
    def _():
        keep.wait()
        for x in xs:
            for d in range(1, nb):
                x.copy(d).wait_send()
        for c in cots:
            c.wait()


def gelu_both(u):
    c = 0.7978845608028654
    t = jnp.tanh(c * (u + 0.044715 * (u * u * u)))
    act = 0.5 * u * (1.0 + t)
    slope = 0.5 * (1.0 + t) + 0.5 * u * (1.0 - t * t) * (c * (1.0 + 3 * 0.044715 * (u * u)))
    return act, slope


def same_plane(far, d):
    return {"dp": lax.axis_index("dp") ^ far, "blk": lax.axis_index("blk") ^ d}


def plane_steps(nb):
    return [(far, d) for far in (0, 1) for d in range(0, nb, 2) if far or d]


def experts_kernel(micros, blocks, nb, *refs):
    mg_ref, gate_ref, cot_ref, win_ref, wback_ref = refs[:5]
    eo_ref, dmg_ref, all_ref, factors, mine, gathered, send_sem, recv_sem = refs[5:]
    sems = (send_sem, recv_sem)
    e, c = pl.program_id(0), pl.program_id(1)
    at = e * pl.num_programs(1) + c
    last = pl.num_programs(0) * pl.num_programs(1) - 1
    per = BLOCK // GROUP
    n_exp = factors.shape[0]
    groups = micros * blocks * per
    blk = lax.axis_index("blk")
    kind = blk % n_exp
    steps = plane_steps(nb)

    def core_copy():
        return remote(factors.at[1 - kind], mine.at[1], sems, 0, peer("blk", blk, 1))

    def plane_copy(n):
        return remote(mine, gathered.at[n], sems, 1 + n, same_plane(*steps[n]))

    @pl.when(at == 0)
    def _():
        deo = []
        for m in range(micros):
            for i in range(blocks):
                at_rows = (m * blocks + i) * BLOCK
                deo.append(nn(gate_ref[:, at_rows : at_rows + BLOCK].astype(BF), cot_ref[m, i]))
        for j in range(n_exp):
            factors[j, 0] = mg_ref[j].astype(BF)
            factors[j, 1] = jnp.concatenate(
                [d[j * per : (j + 1) * per] for d in deo], axis=0
            ).astype(BF)
        arrive([peer("blk", blk, 1)] + [same_plane(*s) for s in steps])
        core_copy().start()
        mine[0] = factors[kind]

    mg, deo = factors[e, 0], factors[e, 1]
    act, slope = gelu_both(nn(mg, win_ref[0]))
    eo_part = nn(act.astype(BF), wback_ref[0])
    du = (slope * nt(deo, wback_ref[0])).astype(BF)
    dmg_part = nt(du, win_ref[0])

    @pl.when(c == 0)
    def _():
        eo_ref[0] = eo_part
        dmg_ref[0] = dmg_part

    @pl.when(c > 0)
    def _():
        eo_ref[0] += eo_part
        dmg_ref[0] += dmg_part

    @pl.when(at == 2)
    def _():
        core_copy().wait()
        for n in range(len(steps)):
            plane_copy(n).start()

    @pl.when(at == last)
    def _():
        for n in range(len(steps)):
            plane_copy(n).wait()
        for n in range(len(steps) + 1):
            piece = mine[...] if n == 0 else gathered[n - 1]
            for f in range(2):
                for j in range(2):
                    rows = slice((2 * n + j) * groups, (2 * n + j + 1) * groups)
                    all_ref[f, rows, :] = piece[j, f]


class Return:
    def __init__(self, nb, buf, out, own, sems, base):
        self.nb, self.buf, self.out, self.own, self.sems, self.base = nb, buf, out, own, sems, base
        self.me = lax.axis_index("blk")

    def local(self):
        return pltpu.make_async_copy(
            self.buf.at[self.me], self.out.at[self.me], self.own.at[self.base]
        )

    def copy(self, d):
        return remote(
            self.buf.at[self.me ^ d], self.out.at[self.me], self.sems,
            self.base * (self.nb - 1) + d - 1, peer("blk", self.me, d),
        )

    def start(self, i):
        pl.when(i == self.me)(lambda: self.local().start())
        for d in range(1, self.nb):
            pl.when(i == (self.me ^ d))(lambda d=d: self.copy(d).start())

    def wait(self):
        self.local().wait()
        for d in range(1, self.nb):
            self.copy(d).wait()


class Plan:
    def __init__(self, sems):
        self.sems, self.count, self.sets = sems, 0, {}

    def add(self, name, makers):
        self.sets[name] = list(enumerate(makers, self.count))
        self.count += len(makers)

    def each(self, name):
        for k, maker in self.sets[name]:
            src, dst, where = maker()
            yield remote(src, dst, self.sems, k, where)

    def start(self, name):
        for c in self.each(name):
            c.start()

    def arrived(self, name):
        for c in self.each(name):
            c.wait_recv()

    def sent(self, name):
        for c in self.each(name):
            c.wait_send()


def other_plane(d):
    return {"dp": lax.axis_index("dp") ^ (2 * d)}


def pair_sum(parts):
    while len(parts) > 1:
        parts = [parts[n] + parts[n + 1] for n in range(0, len(parts), 2)]
    return parts[0]


def rows_of(n, size):
    return pl.ds(pl.multiple_of(n * size, size), size)


def backward_kernel(micros, blocks, nb, planes, x_ref, cot_ref, h_ref, gate_ref, eo_ref, dmg_ref, ob_ref,
                    lse_ref, q_ref, k_ref, v_ref, kt_ref, start_ref, g1_ref, g2_ref, wc_ref, wq_ref,
                    wk_ref, wv_ref, wo_ref, factors, win_hbm, wback_hbm, act_ref, gi_ref, flat_ref,
                    small_ref, gin, gback, dh_all, n1_all, dob, delta, dq_all, dk_all, dv_all, dk_acc,
                    dv_acc, gacc, go_acc, bias, act_buf, gi_buf, win, wback, ours, theirs, piece, s1,
                    r1, s2, r2, s3, r3, fl, small, rs, own, load_sem, ret_send, ret_recv, send_sem,
                    recv_sem):
    now = pl.program_id(0)
    width = wo_ref.shape[0]
    pairs = width // (2 * HEAD_DIM)
    pair_lanes = 2 * HEAD_DIM
    span = 2 * blocks + pairs
    micro, step = now // span, now % span
    last = (micros - 1) * span
    blk, dp = lax.axis_index("blk"), lax.axis_index("dp")
    kind, plane = blk % 2, dp // 2
    steps = plane_steps(nb)
    members = len(steps) + 1
    core = lambda: peer("blk", lax.axis_index("blk"), 1)

    def part_of(far, d):
        return ((blk ^ d) // 2) + (nb // 2) * ((dp % 2) ^ far)

    part = part_of(0, 0)
    cut = win.shape[1]
    rets = (ret_send, ret_recv)
    acts = [Return(nb, act_buf.at[m], act_ref.at[m], own, rets, 2 * m) for m in range(micros)]
    gis = [Return(nb, gi_buf.at[m], gi_ref.at[m], own, rets, 2 * m + 1) for m in range(micros)]
    columns = rows_of(part, cut)
    loads = [
        lambda: pltpu.make_async_copy(win_hbm.at[kind, :, columns], win, load_sem.at[0]),
        lambda: pltpu.make_async_copy(wback_hbm.at[kind, columns, :], wback, load_sem.at[1]),
    ]
    rows = width // planes

    def window(which, p, z):
        if which == 0:
            return gin.at[kind, rows_of(z, rows), rows_of(p, cut)]
        at = pl.multiple_of(p * cut + z * rows, rows)
        return gback.at[kind, pl.ds(at, rows), :]

    def slab(which, p):
        if which == 0:
            return gin.at[kind, :, rows_of(p, cut)]
        return gback.at[kind, rows_of(p, cut), :]

    mine = [
        lambda: pltpu.make_async_copy(piece.at[0], window(0, part, plane), load_sem.at[2]),
        lambda: pltpu.make_async_copy(piece.at[1], window(1, part, plane), load_sem.at[3]),
    ]
    y_peer, x_peer = steps[0], steps[1]
    others = range(1, planes)
    both = range(2)
    half = fl.shape[1] // 2
    quarter = half // members
    plan = Plan((send_sem, recv_sem))
    plan.add("rs", [lambda d=d: (ours.at[plane ^ d], theirs.at[d - 1], other_plane(d)) for d in others])
    plan.add("z", [
        lambda d=d, w=w: (piece.at[w], window(w, part, plane), other_plane(d)) for d in others for w in both
    ])
    for name, to in (("y0", y_peer), ("x0", x_peer)):
        plan.add(name, [
            lambda w=w, to=to: (piece.at[w], window(w, part, plane), same_plane(*to)) for w in both
        ])

    def onward(p, z, w, to):
        return window(w, p, z), window(w, p, z), same_plane(*to)

    part_y = part_of(*y_peer)
    plan.add("yx0", [lambda w=w: onward(part_y, plane, w, x_peer) for w in both])
    for name, p, to in (("y1", part, y_peer), ("x1", part, x_peer), ("yx1", part_y, x_peer)):
        plan.add(name, [
            lambda d=d, w=w, p=p, to=to: onward(p, plane ^ d, w, to) for d in others for w in both
        ])
    for name, p in zip(("c_own", "c_y", "c_x", "c_d"), [part] + [part_of(*t) for t in steps]):
        plan.add(name, [lambda w=w, p=p: (slab(w, p), slab(w, p), core()) for w in both])
    for c in range(pairs):
        plan.add(f"a{c}", [lambda c=c: (s1.at[c], r1.at[c], core())])
        plan.add(f"b{c}", [
            lambda c=c, n=n: (s2.at[c, n], r2.at[c, n], same_plane(*steps[n])) for n in range(members - 1)
        ])
        plan.add(f"z{c}", [lambda c=c, d=d: (s3.at[c], r3.at[c, d - 1], other_plane(d)) for d in others])

        def share(c, n):
            at = pl.multiple_of(kind * half + part * quarter, quarter)
            ref = fl.at[c, pl.ds(at, quarter), :]
            return ref, ref, same_plane(*steps[n])

        def side(c):
            ref = fl.at[c, rows_of(kind, half), :]
            return ref, ref, core()

        plan.add(f"g{c}", [lambda c=c, n=n: share(c, n) for n in range(members - 1)])
        plan.add(f"h{c}", [lambda c=c: side(c)])
    plan.add("sa", [lambda: (small.at[0], rs.at[0], core())])
    plan.add("sb", [lambda n=n: (small.at[1], rs.at[1 + n], same_plane(*steps[n])) for n in range(members - 1)])
    plan.add("sz", [lambda d=d: (small.at[2], rs.at[members + d - 1], other_plane(d)) for d in others])
    assert plan.count <= send_sem.shape[0]

    def chunk_start(c):
        s1[c] = gacc[c, rows_of(1 - kind, half), :].astype(BF)
        plan.start(f"a{c}")

    def chunk_b(c):
        plan.arrived(f"a{c}")
        at = rows_of(kind, half)
        gacc[c, at, :] = gacc[c, at, :] + r1[c].astype(F32)
        for n, to in enumerate(steps):
            s2[c, n] = gacc[c, pl.ds(pl.multiple_of(kind * half + part_of(*to) * quarter, quarter), quarter), :].astype(BF)
        plan.start(f"b{c}")

    def chunk_z(c):
        plan.arrived(f"b{c}")
        at = pl.ds(pl.multiple_of(kind * half + part * quarter, quarter), quarter)
        total = pair_sum([gacc[c, at, :]] + [r2[c, n].astype(F32) for n in range(members - 1)])
        s3[c] = total.astype(BF)
        plan.start(f"z{c}")

    def chunk_g(c):
        plan.arrived(f"z{c}")
        total = pair_sum([s3[c].astype(F32)] + [r3[c, d - 1].astype(F32) for d in others])
        at = pl.ds(pl.multiple_of(kind * half + part * quarter, quarter), quarter)
        fl[c, at, :] = total.astype(BF)
        plan.start(f"g{c}")

    def chunk_h(c):
        plan.arrived(f"g{c}")
        plan.start(f"h{c}")

    def out_copy(c):
        return pltpu.make_async_copy(fl.at[c], flat_ref.at[c], load_sem.at[4 + c])

    def chunk_done(c):
        plan.arrived(f"h{c}")
        out_copy(c).start()

    stages = [chunk_start, chunk_b, chunk_z, chunk_g, chunk_h, chunk_done]

    @pl.when(now == 0)
    def _():
        for c in loads:
            c().start()
        partners = [peer("blk", blk, d) for d in range(1, nb)]
        partners += [same_plane(*s) for s in steps if s[0]] + [other_plane(d) for d in others]
        arrive(partners)
        small[0] = jnp.zeros(small.shape[1:], F32)
        go_acc[...] = jnp.zeros_like(go_acc)
        fill_bias(bias.at[0], None, False, 0)
        for c in loads:
            c().wait()
        mg, deo = factors[0], factors[1]
        act, slope = gelu_both(nn(mg, win[...]))
        du = (slope * nt(deo, wback[...])).astype(BF)
        g_in = tn(mg, du).astype(BF)
        g_back = tn(act.astype(BF), deo).astype(BF)
        for n in range(planes):
            ours[n, 0] = g_in[n * rows : (n + 1) * rows]
            ours[n, 1] = g_back[n * rows : (n + 1) * rows]
        plan.start("rs")

    gate_rows = gate_ref.shape[0]

    @pl.when(step < blocks)
    def _():
        at = rows_of(step, BLOCK)
        h = h_ref[0]
        cot_b = cot_ref[0, 0]
        dout = cot_b.astype(F32)
        r2_ = rms(h)
        z = h * r2_
        n2 = (z * g2_ref[...]).astype(BF)
        gate = gate_ref[...]
        gate_b = gate.astype(BF)
        gate_low = (gate - gate_b.astype(F32)).astype(BF)
        eo = jnp.concatenate([eo_ref[j] for j in range(eo_ref.shape[0])], axis=0)
        dmg = jnp.concatenate([dmg_ref[j] for j in range(dmg_ref.shape[0])], axis=0).astype(BF)
        eo_b = eo.astype(BF)
        eo_low = (eo - eo_b.astype(F32)).astype(BF)
        mixed = tn(
            jnp.concatenate([gate_b, gate_low, gate_b], axis=0),
            jnp.concatenate([eo_b, eo_b, eo_low], axis=0),
        )
        act_buf[micro, step] = (h + mixed).astype(BF)
        for m in range(micros):
            pl.when(micro == m)(functools.partial(acts[m].start, step))
        dw2 = nt(jnp.concatenate([eo_b, eo_low], axis=0), cot_b)
        dw = dw2[:gate_rows] + dw2[gate_rows:] + nt(dmg, n2)
        wdw = gate * dw
        dlog = (wdw - gate * jnp.sum(wdw, axis=1, keepdims=True)).astype(BF)
        dn2 = tn(
            jnp.concatenate([gate_b, dlog], axis=0),
            jnp.concatenate([dmg, wc_ref[...]], axis=0),
        )
        small[0, 0:gate_rows, :] += nn(dlog, n2)
        small[0, gate_rows : gate_rows + 1, :] += jnp.sum(dn2 * z, axis=0, keepdims=True)
        a = dn2 * g2_ref[...]
        dh = dout + r2_ * (a - z * jnp.mean(a * z, axis=-1, keepdims=True))
        dh_all[at, :] = dh
        da = dh.astype(BF)
        dob_b = nt(da, wo_ref[...]).astype(BF)
        dob[at, :] = dob_b
        ob = ob_ref[0]
        go_acc[...] += tn(ob, da)
        prod = dob_b.astype(F32) * ob.astype(F32)
        high = prod.astype(BF)
        low = (prod - high.astype(F32)).astype(BF)
        heads = head_rows(delta.shape[0], width)
        delta[:, at] = nt(heads, high) + nt(heads, low)
        x = x_ref[0, 0].astype(F32)
        n1_all[at, :] = (x * rms(x) * g1_ref[...]).astype(BF)

    for m in range(1, micros):
        for i in range(blocks):
            pl.when(now == m * span + i)(
                functools.partial(fill_bias, bias.at[i], start_ref[i], True, i)
            )

    masks = head_masks()

    def attend(packed):
        hp = step - blocks
        lanes = rows_of(hp, pair_lanes)
        for i in range(blocks):
            low, count = key_range(packed, i)
            at = slice(i * BLOCK, (i + 1) * BLOCK)
            q_pair, dob_pair = q_ref[0, at, :], dob[at, lanes]
            k_pair, v_pair = k_ref[0, low : low + count, :], v_ref[0, low : low + count, :]
            dk_sum = dv_sum = None
            dqs = []
            for h in range(2):
                qm, dm = q_pair * masks[h], dob_pair * masks[h]
                scores = add_bias(nt(k_pair, qm), bias.at[i if packed else 0], packed, count)
                p = jnp.exp(scores * SCALE - lse_ref[0, pl.ds(hp * 2 + h, 1), at])
                dp_ = nt(v_pair, dm)
                ds = (p * (dp_ - delta[pl.ds(hp * 2 + h, 1), at])).astype(BF)
                kt = kt_ref[0, h * HEAD_DIM : (h + 1) * HEAD_DIM, low : low + count]
                dqs.append(nn(kt, ds) * SCALE)
                dk_part, dv_part = nn(ds, qm), nn(p.astype(BF), dm)
                dk_sum = dk_part if dk_sum is None else dk_sum + dk_part
                dv_sum = dv_part if dv_sum is None else dv_sum + dv_part
            old = i * BLOCK - low
            dk_acc[at, :] = dk_sum[old:]
            dv_acc[at, :] = dv_sum[old:]
            if old:
                dk_acc[low : i * BLOCK, :] += dk_sum[:old]
                dv_acc[low : i * BLOCK, :] += dv_sum[:old]
            dq_all[at, lanes] = jnp.concatenate(dqs, axis=0).T.astype(BF)
        dk = (dk_acc[...] * SCALE).astype(BF)
        dv = dv_acc[...].astype(BF)
        dk_all[:, lanes] = dk
        dv_all[:, lanes] = dv
        g = tn(jnp.concatenate([dq_all[:, lanes], dk, dv], axis=1), n1_all[...])
        top = 3 * pair_lanes
        if packed:
            gacc[hp, 0:top, :] += g
            gacc[hp, top:, :] = go_acc[rows_of(hp, pair_lanes), :]
        else:
            gacc[hp, 0:top, :] = g

    for m in range(micros):
        in_phase = (micro == m) & (step >= blocks) & (step < blocks + pairs)
        pl.when(in_phase)(functools.partial(attend, m > 0))

    @pl.when(step >= blocks + pairs)
    def _():
        i = step - blocks - pairs
        at = rows_of(i, BLOCK)
        x = x_ref[0, 0].astype(F32)
        r1_ = rms(x)
        z1 = x * r1_
        dn1 = (
            nt(dq_all[at, :], wq_ref[...]) + nt(dk_all[at, :], wk_ref[...]) + nt(dv_all[at, :], wv_ref[...])
        )
        small[0, gate_rows + 8 : gate_rows + 9, :] += jnp.sum(dn1 * z1, axis=0, keepdims=True)
        b = dn1 * g1_ref[...]
        gi = dh_all[at, :] + r1_ * (b - z1 * jnp.mean(b * z1, axis=-1, keepdims=True))
        gi_buf[micro, i] = gi.astype(BF)
        for m in range(micros):
            pl.when(micro == m)(functools.partial(gis[m].start, i))

    @pl.when(now == blocks + pairs)
    def _():
        plan.arrived("rs")
        total = pair_sum([ours[plane].astype(F32)] + [theirs[d - 1].astype(F32) for d in others])
        piece[...] = total.astype(BF)
        for c in mine:
            c().start()
        for name in ("z", "y0", "x0"):
            plan.start(name)

    @pl.when(now == last + blocks - 1)
    def _():
        plan.arrived("y0")
        plan.start("yx0")

    @pl.when(now == last + blocks + 1)
    def _():
        for c in mine:
            c().wait()
        plan.arrived("z")
        for name in ("y1", "x1", "c_own"):
            plan.start(name)

    final = micros * span - 1
    late = []
    for at in range(len(stages) + pairs - 1):
        todo = [(at - n, n) for n in reversed(range(len(stages))) if 0 <= at - n < pairs]
        if last + blocks + at > final:
            late += todo
            continue

        @pl.when(now == last + blocks + at)
        def _(todo=todo):
            for c, n in todo:
                stages[n](c)

    @pl.when(now == final)
    def _():
        plan.start("sa")
        plan.arrived("y1")
        for name in ("yx1", "c_y"):
            plan.start(name)
        plan.arrived("sa")
        small[1] = small[0] + rs[0]
        plan.start("sb")
        for c, n in late:
            stages[n](c)
        plan.arrived("sb")
        small[2] = pair_sum([small[1]] + [rs[1 + n] for n in range(members - 1)])
        plan.start("sz")
        for name in ("x0", "x1"):
            plan.arrived(name)
        plan.start("c_x")
        plan.arrived("sz")
        small_ref[...] = pair_sum([small[2]] + [rs[members + d - 1] for d in others])
        for name in ("yx0", "yx1"):
            plan.arrived(name)
        plan.start("c_d")
        for name in ("c_own", "c_y", "c_x", "c_d"):
            plan.arrived(name)
        for c in range(pairs):
            out_copy(c).wait()
        for name in plan.sets:
            plan.sent(name)
        for r in acts + gis:
            r.wait()


def whole(shape):
    return pl.BlockSpec(shape, lambda *_: (0,) * len(shape))


def held(shape):
    return pl.BlockSpec(shape, lambda *_: (0,) * len(shape), pipeline_mode=pl.Buffered(1))


ANY = pl.BlockSpec(memory_space=pl.ANY)
DMA = pltpu.SemaphoreType.DMA


def shaped(shape, dtype):
    return jax.ShapeDtypeStruct(shape, dtype)


def params(number):
    return pltpu.CompilerParams(
        vmem_limit_bytes=VMEM_LIMIT, collective_id=number, has_side_effects=True
    )


def forward_call(x, seg, cot, g1, wq, wk, wv, wo, g2, wc):
    nb = lax.axis_size("blk")
    micros, _, rows_in, width = x.shape
    length = nb * rows_in
    blocks = length // BLOCK
    assert x.shape[1] == nb and rows_in == BLOCK
    rows = wc.shape[0]
    heads = width // HEAD_DIM
    per = BLOCK // GROUP
    experts = rows // per
    span = 2 * blocks
    phase = lambda s: jnp.maximum(s % span - blocks, 0)
    whole_micro = lambda a, b: pl.BlockSpec((1, a, b), lambda s: (s // span, 0, 0))
    flat = lambda s: (s // span) * blocks + phase(s)
    moves = 2 * micros + 1
    return pl.pallas_call(
        functools.partial(forward_kernel, micros, blocks, nb),
        grid=(micros * span,),
        in_specs=[ANY, ANY, ANY] + [held(a.shape) for a in (g1, wq, wk, wv, wo, g2, wc)],
        out_specs=[
            whole_micro(length, width), whole_micro(length, width), whole_micro(length, width),
            whole_micro(width, length),
            pl.BlockSpec((1, BLOCK, width), lambda s: (s // span, phase(s), 0)),
            pl.BlockSpec((1, heads, BLOCK), lambda s: (s // span, 0, phase(s))),
            pl.BlockSpec((1, BLOCK, width), lambda s: (s // span, phase(s), 0)),
            pl.BlockSpec((rows, BLOCK), lambda s: (0, flat(s))),
            pl.BlockSpec((experts, per, width), lambda s: (0, flat(s), 0)),
            whole((blocks, 1, BLOCK)), ANY, ANY,
        ],
        out_shape=[
            shaped((micros, length, width), BF), shaped((micros, length, width), BF),
            shaped((micros, length, width), BF), shaped((micros, width, length), BF),
            shaped((micros, length, width), BF), shaped((micros, heads, length), F32),
            shaped((micros, length, width), F32), shaped((rows, micros * length), F32),
            shaped((experts, micros * length // GROUP, width), F32),
            shaped((blocks, 1, BLOCK), jnp.int32), shaped(x.shape, BF), shaped(x.shape, BF),
        ],
        scratch_shapes=[
            pltpu.VMEM(x.shape, BF), pltpu.VMEM(seg.shape, seg.dtype),
            pltpu.VMEM((length, BLOCK), F32), pltpu.VMEM((BLOCK, width), F32),
            pltpu.VMEM((heads, BLOCK), F32), pltpu.VMEM((width, width), BF),
            DMA((moves + 1,)), DMA((moves * (nb - 1),)), DMA((moves * (nb - 1),)),
        ],
        compiler_params=params(1),
        name="attention_forward",
    )(x, seg, cot, g1, wq, wk, wv, wo, g2, wc)


def experts_call(mg, gate, cot, w_in, w_back):
    micros, nb, _, width = cot.shape
    experts, groups, _ = mg.shape
    ff = w_in.shape[2]
    blocks = gate.shape[1] // BLOCK // micros
    chunk = min(CHUNK, ff)
    by_expert = lambda n: pl.BlockSpec((1, n, width), lambda e, c: (e, 0, 0))
    members = len(plane_steps(nb))
    return pl.pallas_call(
        functools.partial(experts_kernel, micros, blocks, nb),
        grid=(experts, ff // chunk),
        in_specs=[
            held(mg.shape), held(gate.shape), held(cot.shape),
            pl.BlockSpec((1, width, chunk), lambda e, c: (e, 0, c)),
            pl.BlockSpec((1, chunk, width), lambda e, c: (e, c, 0)),
        ],
        out_specs=[by_expert(groups)] * 2 + [whole((2, 2 * (members + 1) * groups, width))],
        out_shape=[shaped((experts, groups, width), F32)] * 2
        + [shaped((2, 2 * (members + 1) * groups, width), BF)],
        scratch_shapes=[
            pltpu.VMEM((experts, 2, groups, width), BF), pltpu.VMEM((2, 2, groups, width), BF),
            pltpu.VMEM((members, 2, 2, groups, width), BF), DMA((members + 1,)), DMA((members + 1,)),
        ],
        compiler_params=params(2),
        name="experts",
    )(mg, gate, cot, w_in, w_back)


def backward_call(x, cot, h, gate, eo, dmg, ob, lse, q, k, v, kt, start, g1, g2, wc, wq, wk, wv, wo,
                  factors, w_in, w_back):
    micros, nb, _, width = x.shape
    planes = lax.axis_size("dp") // 2
    length = q.shape[1]
    blocks = length // BLOCK
    rows = wc.shape[0]
    per = BLOCK // GROUP
    experts = rows // per
    heads = width // HEAD_DIM
    pairs = heads // 2
    ff = w_in.shape[2]
    cut = ff // nb
    assert cut == width
    members = len(plane_steps(nb)) + 1
    span = 2 * blocks + pairs
    m_of = lambda s: s // span
    early = lambda s: jnp.minimum(s % span, blocks - 1)
    pair_of = lambda s: jnp.clip(s % span - blocks, 0, pairs - 1)

    def early_or_late(s):
        t = s % span
        return jnp.where(t < blocks + pairs, jnp.minimum(t, blocks - 1), t - blocks - pairs)

    flat = lambda s: m_of(s) * blocks + early(s)
    row_block = pl.BlockSpec((1, BLOCK, width), lambda s: (m_of(s), early(s), 0))
    group_block = pl.BlockSpec((experts, per, width), lambda s: (0, flat(s), 0))
    pair_block = pl.BlockSpec((1, length, 2 * HEAD_DIM), lambda s: (m_of(s), 0, pair_of(s)))
    piece = (2, width // planes, cut)
    chunk = 4 * 2 * HEAD_DIM
    half = chunk // 2
    quarter = half // members
    reach = max(key_range(True, i)[1] for i in range(blocks))
    small = (rows + 16, width)
    vm = pltpu.VMEM
    copies = 64 + 16 * pairs + 24 * planes
    return pl.pallas_call(
        functools.partial(backward_kernel, micros, blocks, nb, planes),
        grid=(micros * span,),
        in_specs=[
            pl.BlockSpec((1, 1, BLOCK, width), lambda s: (m_of(s), early_or_late(s), 0, 0)),
            pl.BlockSpec((1, 1, BLOCK, width), lambda s: (m_of(s), early(s), 0, 0)),
            row_block,
            pl.BlockSpec((rows, BLOCK), lambda s: (0, flat(s))),
            group_block, group_block, row_block,
            pl.BlockSpec((1, heads, length), lambda s: (m_of(s), 0, 0)),
            pair_block, pair_block, pair_block,
            pl.BlockSpec((1, 2 * HEAD_DIM, length), lambda s: (m_of(s), pair_of(s), 0)),
        ] + [held(a.shape) for a in (start, g1, g2, wc, wq, wk, wv, wo, factors)] + [ANY, ANY],
        out_specs=[ANY, ANY, ANY, whole(small), ANY, ANY],
        out_shape=[
            shaped(x.shape, BF), shaped(x.shape, BF), shaped((pairs, chunk, width), BF),
            shaped(small, F32), shaped(w_in.shape, BF), shaped(w_back.shape, BF),
        ],
        scratch_shapes=[
            vm((length, width), F32), vm((length, width), BF), vm((length, width), BF),
            vm((heads, length), F32), vm((length, width), BF), vm((length, width), BF),
            vm((length, width), BF), vm((length, 2 * HEAD_DIM), F32), vm((length, 2 * HEAD_DIM), F32),
            vm((pairs, chunk, width), F32), vm((width, width), F32), vm((blocks, reach, BLOCK), F32),
            vm(x.shape, BF), vm(x.shape, BF), vm((width, cut), BF), vm((cut, width), BF),
            vm((planes,) + piece, BF), vm((planes - 1,) + piece, BF), vm(piece, BF),
            vm((pairs, half, width), BF), vm((pairs, half, width), BF),
            vm((pairs, members - 1, quarter, width), BF), vm((pairs, members - 1, quarter, width), BF),
            vm((pairs, quarter, width), BF), vm((pairs, planes - 1, quarter, width), BF),
            vm((pairs, chunk, width), BF), vm((3,) + small, F32),
            vm((members + planes - 1,) + small, F32),
            DMA((2 * micros,)), DMA((4 + pairs,)), DMA((2 * micros * (nb - 1),)),
            DMA((2 * micros * (nb - 1),)), DMA((copies,)), DMA((copies,)),
        ],
        compiler_params=params(3),
        name="attention_backward",
    )(x, cot, h, gate, eo, dmg, ob, lse, q, k, v, kt, start, g1, g2, wc, wq, wk, wv, wo, factors, w_in,
      w_back)


def local(block_input, segment_ids, gain_one, w_query, w_key, w_value, w_out, gain_two, w_ctrl,
          w_in, w_back, cotangent):
    micros, seqs, rows, width = block_input.shape
    experts, _, ff = w_in.shape
    nb = lax.axis_size("blk")
    per = BLOCK // GROUP
    g1, g2 = gain_one.reshape(1, width), gain_two.reshape(1, width)
    wc = jnp.repeat(w_ctrl.T, per, axis=0)
    seg = segment_ids.reshape(nb, 2, rows // 2)
    q, k, v, kt, ob, lse, h, gate, mg, start, x, cot = forward_call(
        block_input, seg, cotangent, g1, w_query, w_key, w_value, w_out, g2, wc
    )
    eo, dmg, factors = experts_call(mg, gate, cot, w_in, w_back)
    acts, gis, flat, small, grad_in, grad_back = backward_call(
        x, cot, h, gate, eo, dmg, ob, lse, q, k, v, kt, start, g1, g2, wc, w_query, w_key, w_value,
        w_out, factors, w_in, w_back,
    )
    flat = flat.reshape(width // (2 * HEAD_DIM), 4, 2 * HEAD_DIM, width)
    one = lambda n: flat[:, n].reshape(width, width).astype(F32)
    ctrl = jnp.sum(small[: experts * per].reshape(experts, per, width), axis=1).T
    return (
        acts, gis, small[experts * per + 8], one(0).T, one(1).T, one(2).T, one(3),
        small[experts * per], ctrl, grad_in.astype(F32), grad_back.astype(F32),
    )


def solution(mesh):
    data = P(None, "dp", "blk", None)
    in_specs = (data, P("dp", "blk")) + (P(),) * 9 + (data,)
    out_specs = (data, data) + (P(),) * 9
    return jax.shard_map(local, mesh=mesh, in_specs=in_specs, out_specs=out_specs, check_vma=False)
```

time: 336 us -> 278 us (0.83)
  Pallas kernels: 292 us -> 249 us
  other arithmetic: 23.2 us -> 14.4 us
  local copies, waits for them, and re-layouts: 18.8 us -> 13.2 us
    pallas_call x5 -> x2, Pallas kernels: 270 us -> 227 us  [the longest x1 157 us: backward_call(): pl.pallas_call(functools.partial(backward_kernel, micros, blocks, nb, pla...]
    another operation x2 -> x0, other arithmetic: 6.99 us -> none  [the longest x1 3.93 us: local(): jnp.stack(acts)]
    unnamed x30 -> x12, local copies, waits for them, and re-layouts: 8.48 us -> 4.36 us
    transpose x1 -> x3, local copies, waits for them, and re-layouts: 0.07 us -> 3.92 us  [the longest x1 1.31 us: local(): one(1)]
where the time goes in v3:
time: 278 us; the launch traced here: 277 us
  Pallas kernels  249 us (90%)
  other arithmetic  14.4 us (5%)
  local copies, waits for them, and re-layouts  13.2 us (5%)
    pallas_call x1, Pallas kernels, backward_call(): pl.pallas_call(functools.partial(backward_kernel, micros, blocks, nb, pla...  157 us
    pallas_call x1, Pallas kernels, forward_call(): pl.pallas_call(functools.partial(forward_kernel, micros, blocks, nb), gri...  70.2 us
    pallas_call x1, Pallas kernels, experts_call(): pl.pallas_call(functools.partial(experts_kernel, micros, blocks, nb), gri...  21.5 us
    convert_element_type x1, other arithmetic, local(): grad_in.astype(F32)  6.8 us

profile of v3, /device:TPU:0, one launch (start us, length us, event | category | flops | bytes accessed | tf_op | source)
XLA Modules:
  0.0 277.3 jit_solution(7872867439822136947)
XLA Ops:
  0.6 0.0 copy-start
  0.7 0.7 copy-done
  1.3 1.3 reshape.48.seg_src
  2.6 0.6 broadcast_bitcast_fusion.wc_ref
  3.2 70.2 %attention_forward.1 = (bf16[2,1024,512]{2,1,0:T(8,128)(2,1)}, bf16[2,1024,512]{2,1,0:T(8,128)(2,1)}, bf16[2,1024,512]{2,1,0:T(8,128)(2,1)}, bf16[2,512,1024]{2,...) custom-call(bf16[2,4,256,512]{3,2,1,0:T(8,128)(2,1)} %x_src.1, ...), custom_call_target="tpu_custom_call" | custom-call | tf_op jit(solution)/shard_map/attention_forward/pallas_call | solution.py:813
  73.5 21.5 %experts.1 = (f32[2,64,512]{2,1,0:T(8,128)}, f32[2,64,512]{2,1,0:T(8,128)}, bf16[2,512,512]{2,1,0:T(8,128)(2,1)}) custom-call(f32[2,64,512]{2,1,0:T(8,128)} %get-tuple-element.36.refs_0_, f32[16,2048]{1,0:T(8,128)} %get-tuple-element.35.refs_1_.gate_ref, bf16[2,4,256,512]{3,2,1,0:T(8,128)(2,1)} %get-tuple-element.33.refs_2_.cot_ref, ...), custom_call_target="tpu_custom_call" | custom-call | tf_op jit(solution)/shard_map/experts/pallas_call | solution.py:854
  95.0 156.9 %attention_backward.1 = (bf16[2,4,256,512]{3,2,1,0:T(8,128)(2,1)}, bf16[2,4,256,512]{3,2,1,0:T(8,128)(2,1)}, bf16[4,512,512]{2,1,0:T(8,128)(2,1)}, f32[32,512]{1...) custom-call(bf16[2,4,256,512]{3,2,1,0:T(8,128)(2,1)} %get-tuple-element.32.x_ref, ...), custom_call_target="tpu_custom_call" | custom-call | tf_op jit(solution)/shard_map/attention_backward/pallas_call | solution.py:910
  251.9 1.4 bitcast_reduce_fusion
  253.3 1.3 fusion.1
  254.6 1.7 fusion
  256.3 1.3 bitcast_convert_fusion
  257.6 1.3 copy.28
  258.9 0.3 bitcast_convert_fusion.2
  259.3 1.3 copy.27
  260.6 1.3 copy.26
  261.9 0.0 copy-start.2
  261.9 6.8 %convert_element_type.29 = f32[2,512,2048]{2,1,0:T(8,128)} convert(bf16[2,512,2048]{2,1,0:T(8,128)(2,1)} %get-tuple-element.51) | non-fusion elementwise | flops 2097152 | bytes 12582912 | tf_op jit(solution)/shard_map/convert_element_type | solution.py:971
  268.7 0.0 copy-done.2
  268.7 0.0 copy-start.4
  268.7 4.6 %convert_element_type.30 = f32[2,2048,512]{2,1,0:T(8,128)} convert(bf16[2,2048,512]{2,1,0:T(8,128)(2,1)S(1)} %copy-done.2) | non-fusion elementwise | flops 2097152 | bytes 12582912 | tf_op jit(solution)/shard_map/convert_element_type | solution.py:971
  273.3 0.0 copy-done.4
  273.3 0.0 copy-start.3
  273.3 0.0 copy-start.1
  273.3 1.3 copy.31
  274.7 1.0 copy-done.3
  275.7 1.3 copy.32
  277.0 0.0 copy-done.1
Async XLA Ops:
  0.6 0.7 copy-start
  261.9 6.8 %copy-start.2 = (bf16[2,2048,512]{2,1,0:T(8,128)(2,1)S(1)}, bf16[2,2048,512]{2,1,0:T(8,128)(2,1)}, u32[]{:S(2)}) copy-start(bf16[2,2048,512]{2,1,0:T(8,128)(2,1)} %get-tuple-element.52) | copy-start | bytes 12582916
  268.7 4.6 %copy-start.4 = (bf16[2,4,256,512]{3,2,1,0:T(8,128)(2,1)S(1)}, bf16[2,4,256,512]{3,2,1,0:T(8,128)(2,1)}, u32[]{:S(2)}) copy-start(bf16[2,4,256,512]{3,2,1,0:T(8,128)(2,1)} %get-tuple-element.74) | copy-start | bytes 6291460
  273.3 2.3 copy-start.3
  273.3 3.7 %copy-start.1 = (bf16[512,2]{0,1:T(2,128)(2,1)S(1)}, bf16[512,2]{0,1:T(2,128)(2,1)}, u32[]{:S(2)}) copy-start(bf16[512,2]{0,1:T(2,128)(2,1)} %param.20) | copy-start | bytes 6148

commit v4 on v3

--- a/solution.py
+++ b/solution.py
@@ -290,7 +290,7 @@
 
 def experts_kernel(micros, blocks, nb, *refs):
     mg_ref, gate_ref, cot_ref, win_ref, wback_ref = refs[:5]
-    eo_ref, dmg_ref, all_ref, factors, mine, gathered, send_sem, recv_sem = refs[5:]
+    eo_ref, dmg_ref, all_ref, factors, gathered, send_sem, recv_sem = refs[5:]
     sems = (send_sem, recv_sem)
     e, c = pl.program_id(0), pl.program_id(1)
     at = e * pl.num_programs(1) + c
@@ -300,13 +300,11 @@
     groups = micros * blocks * per
     blk = lax.axis_index("blk")
     kind = blk % n_exp
-    steps = plane_steps(nb)
-
-    def core_copy():
-        return remote(factors.at[1 - kind], mine.at[1], sems, 0, peer("blk", blk, 1))
+    steps = [(far, d) for far in (0, 1) for d in range(nb) if far or d]
 
     def plane_copy(n):
-        return remote(mine, gathered.at[n], sems, 1 + n, same_plane(*steps[n]))
+        far, d = steps[n]
+        return remote(factors.at[kind ^ (d & 1)], gathered.at[n], sems, n, same_plane(far, d))
 
     @pl.when(at == 0)
     def _():
@@ -320,9 +318,9 @@
             factors[j, 1] = jnp.concatenate(
                 [d[j * per : (j + 1) * per] for d in deo], axis=0
             ).astype(BF)
-        arrive([peer("blk", blk, 1)] + [same_plane(*s) for s in steps])
-        core_copy().start()
-        mine[0] = factors[kind]
+        arrive([same_plane(*s) for s in steps])
+        for n in range(len(steps)):
+            plane_copy(n).start()
 
     mg, deo = factors[e, 0], factors[e, 1]
     act, slope = gelu_both(nn(mg, win_ref[0]))
@@ -340,22 +338,14 @@
         eo_ref[0] += eo_part
         dmg_ref[0] += dmg_part
 
-    @pl.when(at == 2)
-    def _():
-        core_copy().wait()
-        for n in range(len(steps)):
-            plane_copy(n).start()
-
     @pl.when(at == last)
     def _():
         for n in range(len(steps)):
             plane_copy(n).wait()
         for n in range(len(steps) + 1):
-            piece = mine[...] if n == 0 else gathered[n - 1]
+            piece = factors[kind] if n == 0 else gathered[n - 1]
             for f in range(2):
-                for j in range(2):
-                    rows = slice((2 * n + j) * groups, (2 * n + j + 1) * groups)
-                    all_ref[f, rows, :] = piece[j, f]
+                all_ref[f, n * groups : (n + 1) * groups, :] = piece[f]
 
 
 class Return:
@@ -430,7 +420,7 @@
                     wk_ref, wv_ref, wo_ref, factors, win_hbm, wback_hbm, act_ref, gi_ref, flat_ref,
                     small_ref, gin, gback, dh_all, n1_all, dob, delta, dq_all, dk_all, dv_all, dk_acc,
                     dv_acc, gacc, go_acc, bias, act_buf, gi_buf, win, wback, ours, theirs, piece, s1,
-                    r1, s2, r2, s3, r3, fl, small, rs, own, load_sem, ret_send, ret_recv, send_sem,
+                    r1, s2, r2, s3, r3, fl, small, few, rs, own, load_sem, ret_send, ret_recv, send_sem,
                     recv_sem):
     now = pl.program_id(0)
     width = wo_ref.shape[0]
@@ -472,94 +462,148 @@
         return gback.at[kind, rows_of(p, cut), :]
 
     mine = [
-        lambda: pltpu.make_async_copy(piece.at[0], window(0, part, plane), load_sem.at[2]),
-        lambda: pltpu.make_async_copy(piece.at[1], window(1, part, plane), load_sem.at[3]),
+        lambda w=w: pltpu.make_async_copy(piece.at[w], window(w, part, plane), load_sem.at[2 + w])
+        for w in range(2)
     ]
     y_peer, x_peer = steps[0], steps[1]
     others = range(1, planes)
     both = range(2)
-    half = fl.shape[1] // 2
-    quarter = half // members
     plan = Plan((send_sem, recv_sem))
-    plan.add("rs", [lambda d=d: (ours.at[plane ^ d], theirs.at[d - 1], other_plane(d)) for d in others])
-    plan.add("z", [
-        lambda d=d, w=w: (piece.at[w], window(w, part, plane), other_plane(d)) for d in others for w in both
-    ])
-    for name, to in (("y0", y_peer), ("x0", x_peer)):
-        plan.add(name, [
-            lambda w=w, to=to: (piece.at[w], window(w, part, plane), same_plane(*to)) for w in both
+    for w in both:
+        plan.add(f"rs{w}", [
+            lambda d=d, w=w: (ours.at[w, plane ^ d], theirs.at[w, d - 1], other_plane(d)) for d in others
         ])
+        plan.add(f"z{w}", [
+            lambda d=d, w=w: (piece.at[w], window(w, part, plane), other_plane(d)) for d in others
+        ])
+        for name, to in ((f"y0{w}", y_peer), (f"x0{w}", x_peer)):
+            plan.add(name, [
+                lambda w=w, to=to: (piece.at[w], window(w, part, plane), same_plane(*to))
+            ])
 
     def onward(p, z, w, to):
         return window(w, p, z), window(w, p, z), same_plane(*to)
 
     part_y = part_of(*y_peer)
-    plan.add("yx0", [lambda w=w: onward(part_y, plane, w, x_peer) for w in both])
-    for name, p, to in (("y1", part, y_peer), ("x1", part, x_peer), ("yx1", part_y, x_peer)):
-        plan.add(name, [
-            lambda d=d, w=w, p=p, to=to: onward(p, plane ^ d, w, to) for d in others for w in both
+    for w in both:
+        plan.add(f"yx0{w}", [lambda w=w: onward(part_y, plane, w, x_peer)])
+        for name, p, to in ((f"y1{w}", part, y_peer), (f"x1{w}", part, x_peer), (f"yx1{w}", part_y, x_peer)):
+            plan.add(name, [
+                lambda d=d, w=w, p=p, to=to: onward(p, plane ^ d, w, to) for d in others
+            ])
+        for name, p in zip("oyxd", [part] + [part_of(*t) for t in steps]):
+            plan.add(f"c{name}{w}", [lambda w=w, p=p: (slab(w, p), slab(w, p), core())])
+
+    sizes = [width] + [3 * pair_lanes] * pairs
+    halves = [n // 2 for n in sizes]
+    quarters = [n // 2 // members for n in sizes]
+
+    def held_sum(c):
+        return go_acc if c == 0 else gacc.at[c - 1]
+
+    def quarter_at(c, p):
+        at = pl.multiple_of(kind * halves[c] + p * quarters[c], quarters[c])
+        return pl.ds(at, quarters[c])
+
+    for c in range(pairs + 1):
+        n_half, n_quarter = halves[c], quarters[c]
+        plan.add(f"ha{c}", [lambda c=c, r=n_half: (s1.at[c, 0:r], r1.at[c, 0:r], core())])
+        plan.add(f"hb{c}", [
+            lambda c=c, n=n, r=n_quarter: (s2.at[c, n, 0:r], r2.at[c, n, 0:r], same_plane(*steps[n]))
+            for n in range(members - 1)
         ])
-    for name, p in zip(("c_own", "c_y", "c_x", "c_d"), [part] + [part_of(*t) for t in steps]):
-        plan.add(name, [lambda w=w, p=p: (slab(w, p), slab(w, p), core()) for w in both])
-    for c in range(pairs):
-        plan.add(f"a{c}", [lambda c=c: (s1.at[c], r1.at[c], core())])
-        plan.add(f"b{c}", [
-            lambda c=c, n=n: (s2.at[c, n], r2.at[c, n], same_plane(*steps[n])) for n in range(members - 1)
+        plan.add(f"hz{c}", [
+            lambda c=c, d=d, r=n_quarter: (s3.at[c, 0:r], r3.at[c, d - 1, 0:r], other_plane(d))
+            for d in others
         ])
-        plan.add(f"z{c}", [lambda c=c, d=d: (s3.at[c], r3.at[c, d - 1], other_plane(d)) for d in others])
 
         def share(c, n):
-            at = pl.multiple_of(kind * half + part * quarter, quarter)
-            ref = fl.at[c, pl.ds(at, quarter), :]
+            ref = fl.at[c, quarter_at(c, part), :]
             return ref, ref, same_plane(*steps[n])
 
         def side(c):
-            ref = fl.at[c, rows_of(kind, half), :]
+            ref = fl.at[c, rows_of(kind, halves[c]), :]
             return ref, ref, core()
 
-        plan.add(f"g{c}", [lambda c=c, n=n: share(c, n) for n in range(members - 1)])
-        plan.add(f"h{c}", [lambda c=c: side(c)])
-    plan.add("sa", [lambda: (small.at[0], rs.at[0], core())])
-    plan.add("sb", [lambda n=n: (small.at[1], rs.at[1 + n], same_plane(*steps[n])) for n in range(members - 1)])
-    plan.add("sz", [lambda d=d: (small.at[2], rs.at[members + d - 1], other_plane(d)) for d in others])
+        plan.add(f"hg{c}", [lambda c=c, n=n: share(c, n) for n in range(members - 1)])
+        plan.add(f"hh{c}", [lambda c=c: side(c)])
+    near = [(far, d) for far in (0, 1) for d in range(nb) if far or d]
+    plan.add("sb", [lambda n=n: (few.at[0], rs.at[n], same_plane(*near[n])) for n in range(len(near))])
+    plan.add("sz", [lambda d=d: (few.at[1], rs.at[len(near) + d - 1], other_plane(d)) for d in others])
     assert plan.count <= send_sem.shape[0]
 
     def chunk_start(c):
-        s1[c] = gacc[c, rows_of(1 - kind, half), :].astype(BF)
-        plan.start(f"a{c}")
+        s1[c, 0 : halves[c]] = held_sum(c)[rows_of(1 - kind, halves[c]), :].astype(BF)
+        plan.start(f"ha{c}")
 
     def chunk_b(c):
-        plan.arrived(f"a{c}")
-        at = rows_of(kind, half)
-        gacc[c, at, :] = gacc[c, at, :] + r1[c].astype(F32)
+        plan.arrived(f"ha{c}")
+        at = rows_of(kind, halves[c])
+        ref = held_sum(c)
+        ref[at, :] = ref[at, :] + r1[c, 0 : halves[c]].astype(F32)
         for n, to in enumerate(steps):
-            s2[c, n] = gacc[c, pl.ds(pl.multiple_of(kind * half + part_of(*to) * quarter, quarter), quarter), :].astype(BF)
-        plan.start(f"b{c}")
+            s2[c, n, 0 : quarters[c]] = ref[quarter_at(c, part_of(*to)), :].astype(BF)
+        plan.start(f"hb{c}")
 
     def chunk_z(c):
-        plan.arrived(f"b{c}")
-        at = pl.ds(pl.multiple_of(kind * half + part * quarter, quarter), quarter)
-        total = pair_sum([gacc[c, at, :]] + [r2[c, n].astype(F32) for n in range(members - 1)])
-        s3[c] = total.astype(BF)
-        plan.start(f"z{c}")
+        plan.arrived(f"hb{c}")
+        r = quarters[c]
+        total = pair_sum(
+            [held_sum(c)[quarter_at(c, part), :]] + [r2[c, n, 0:r].astype(F32) for n in range(members - 1)]
+        )
+        s3[c, 0:r] = total.astype(BF)
+        plan.start(f"hz{c}")
 
     def chunk_g(c):
-        plan.arrived(f"z{c}")
-        total = pair_sum([s3[c].astype(F32)] + [r3[c, d - 1].astype(F32) for d in others])
-        at = pl.ds(pl.multiple_of(kind * half + part * quarter, quarter), quarter)
-        fl[c, at, :] = total.astype(BF)
-        plan.start(f"g{c}")
+        plan.arrived(f"hz{c}")
+        r = quarters[c]
+        total = pair_sum([s3[c, 0:r].astype(F32)] + [r3[c, d - 1, 0:r].astype(F32) for d in others])
+        fl[c, quarter_at(c, part), :] = total.astype(BF)
+        plan.start(f"hg{c}")
 
     def chunk_h(c):
-        plan.arrived(f"g{c}")
-        plan.start(f"h{c}")
+        plan.arrived(f"hg{c}")
+        plan.start(f"hh{c}")
 
     def out_copy(c):
         return pltpu.make_async_copy(fl.at[c], flat_ref.at[c], load_sem.at[4 + c])
 
     def chunk_done(c):
-        plan.arrived(f"h{c}")
+        plan.arrived(f"hh{c}")
         out_copy(c).start()
+
+    def reduced(w):
+        plan.arrived(f"rs{w}")
+        total = pair_sum([ours[w, plane].astype(F32)] + [theirs[w, d - 1].astype(F32) for d in others])
+        piece[w] = total.astype(BF)
+        mine[w]().start()
+        for name in ("z", "y0", "x0"):
+            plan.start(f"{name}{w}")
+
+    def own_y(w):
+        plan.arrived(f"y0{w}")
+        plan.start(f"yx0{w}")
+
+    def whole_slice(w):
+        mine[w]().wait()
+        plan.arrived(f"z{w}")
+        for name in ("y1", "x1", "co"):
+            plan.start(f"{name}{w}")
+
+    def slice_y(w):
+        plan.arrived(f"y1{w}")
+        for name in ("yx1", "cy"):
+            plan.start(f"{name}{w}")
+
+    def slice_x(w):
+        plan.arrived(f"x0{w}")
+        plan.arrived(f"x1{w}")
+        plan.start(f"cx{w}")
+
+    def slice_d(w):
+        plan.arrived(f"yx0{w}")
+        plan.arrived(f"yx1{w}")
+        plan.start(f"cd{w}")
 
     stages = [chunk_start, chunk_b, chunk_z, chunk_g, chunk_h, chunk_done]
 
@@ -568,9 +612,9 @@
         for c in loads:
             c().start()
         partners = [peer("blk", blk, d) for d in range(1, nb)]
-        partners += [same_plane(*s) for s in steps if s[0]] + [other_plane(d) for d in others]
+        partners += [same_plane(1, d) for d in range(nb)] + [other_plane(d) for d in others]
         arrive(partners)
-        small[0] = jnp.zeros(small.shape[1:], F32)
+        small[...] = jnp.zeros_like(small)
         go_acc[...] = jnp.zeros_like(go_acc)
         fill_bias(bias.at[0], None, False, 0)
         for c in loads:
@@ -579,11 +623,12 @@
         act, slope = gelu_both(nn(mg, win[...]))
         du = (slope * nt(deo, wback[...])).astype(BF)
         g_in = tn(mg, du).astype(BF)
+        for n in range(planes):
+            ours[0, n] = g_in[n * rows : (n + 1) * rows]
+        plan.start("rs0")
         g_back = tn(act.astype(BF), deo).astype(BF)
         for n in range(planes):
-            ours[n, 0] = g_in[n * rows : (n + 1) * rows]
-            ours[n, 1] = g_back[n * rows : (n + 1) * rows]
-        plan.start("rs")
+            ours[1, n] = g_back[n * rows : (n + 1) * rows]
 
     gate_rows = gate_ref.shape[0]
 
@@ -618,8 +663,8 @@
             jnp.concatenate([gate_b, dlog], axis=0),
             jnp.concatenate([dmg, wc_ref[...]], axis=0),
         )
-        small[0, 0:gate_rows, :] += nn(dlog, n2)
-        small[0, gate_rows : gate_rows + 1, :] += jnp.sum(dn2 * z, axis=0, keepdims=True)
+        small[0:gate_rows, :] += nn(dlog, n2)
+        small[gate_rows : gate_rows + 1, :] += jnp.sum(dn2 * z, axis=0, keepdims=True)
         a = dn2 * g2_ref[...]
         dh = dout + r2_ * (a - z * jnp.mean(a * z, axis=-1, keepdims=True))
         dh_all[at, :] = dh
@@ -633,7 +678,7 @@
         low = (prod - high.astype(F32)).astype(BF)
         heads = head_rows(delta.shape[0], width)
         delta[:, at] = nt(heads, high) + nt(heads, low)
-        x = x_ref[0, 0].astype(F32)
+        x = x_ref[0, step].astype(F32)
         n1_all[at, :] = (x * rms(x) * g1_ref[...]).astype(BF)
 
     for m in range(1, micros):
@@ -677,12 +722,10 @@
         dk_all[:, lanes] = dk
         dv_all[:, lanes] = dv
         g = tn(jnp.concatenate([dq_all[:, lanes], dk, dv], axis=1), n1_all[...])
-        top = 3 * pair_lanes
         if packed:
-            gacc[hp, 0:top, :] += g
-            gacc[hp, top:, :] = go_acc[rows_of(hp, pair_lanes), :]
+            gacc[hp] += g
         else:
-            gacc[hp, 0:top, :] = g
+            gacc[hp] = g
 
     for m in range(micros):
         in_phase = (micro == m) & (step >= blocks) & (step < blocks + pairs)
@@ -690,83 +733,84 @@
 
     @pl.when(step >= blocks + pairs)
     def _():
-        i = step - blocks - pairs
+        i = blk ^ (nb - 1 - (step - blocks - pairs))
         at = rows_of(i, BLOCK)
-        x = x_ref[0, 0].astype(F32)
+        x = x_ref[0, i].astype(F32)
         r1_ = rms(x)
         z1 = x * r1_
         dn1 = (
             nt(dq_all[at, :], wq_ref[...]) + nt(dk_all[at, :], wk_ref[...]) + nt(dv_all[at, :], wv_ref[...])
         )
-        small[0, gate_rows + 8 : gate_rows + 9, :] += jnp.sum(dn1 * z1, axis=0, keepdims=True)
+        small[gate_rows + 8 : gate_rows + 9, :] += jnp.sum(dn1 * z1, axis=0, keepdims=True)
         b = dn1 * g1_ref[...]
         gi = dh_all[at, :] + r1_ * (b - z1 * jnp.mean(b * z1, axis=-1, keepdims=True))
         gi_buf[micro, i] = gi.astype(BF)
         for m in range(micros):
             pl.when(micro == m)(functools.partial(gis[m].start, i))
 
-    @pl.when(now == blocks + pairs)
-    def _():
-        plan.arrived("rs")
-        total = pair_sum([ours[plane].astype(F32)] + [theirs[d - 1].astype(F32) for d in others])
-        piece[...] = total.astype(BF)
-        for c in mine:
-            c().start()
-        for name in ("z", "y0", "x0"):
-            plan.start(name)
-
-    @pl.when(now == last + blocks - 1)
-    def _():
-        plan.arrived("y0")
-        plan.start("yx0")
-
-    @pl.when(now == last + blocks + 1)
-    def _():
-        for c in mine:
-            c().wait()
-        plan.arrived("z")
-        for name in ("y1", "x1", "c_own"):
-            plan.start(name)
-
     final = micros * span - 1
-    late = []
-    for at in range(len(stages) + pairs - 1):
-        todo = [(at - n, n) for n in reversed(range(len(stages))) if 0 <= at - n < pairs]
-        if last + blocks + at > final:
-            late += todo
-            continue
-
-        @pl.when(now == last + blocks + at)
-        def _(todo=todo):
-            for c, n in todo:
-                stages[n](c)
+    sums_from = last + blocks - 1
+    tasks = {}
+
+    def after(at, task, *args):
+        tasks.setdefault(min(at, final), []).append(functools.partial(task, *args))
+
+    def start_second():
+        plan.start("rs1")
+
+    after(blocks - 1, start_second)
+    after(blocks, reduced, 0)
+    after(blocks + pairs - 1, reduced, 1)
+    after(blocks + pairs - 1, own_y, 0)
+    after(last, whole_slice, 0)
+    after(last, own_y, 1)
+    after(last + blocks - 1, whole_slice, 1)
+    after(last + blocks, slice_y, 0)
+    after(last + blocks + 1, slice_x, 0)
+    after(last + blocks + 2, slice_y, 1)
+    after(last + blocks + 2, slice_x, 1)
+    after(last + blocks + 3, slice_d, 0)
+    for c in range(pairs):
+        for n, stage in enumerate(stages):
+            after(sums_from + c + n, stage, c)
+    c = pairs
+    after(sums_from + c, chunk_start, c)
+    after(sums_from + c + 1, chunk_b, c)
+    after(sums_from + c + 3, chunk_z, c)
+    for at, todo in tasks.items():
+        if at < final:
+
+            @pl.when(now == at)
+            def _(todo=todo):
+                for task in todo:
+                    task()
 
     @pl.when(now == final)
     def _():
-        plan.start("sa")
-        plan.arrived("y1")
-        for name in ("yx1", "c_y"):
-            plan.start(name)
-        plan.arrived("sa")
-        small[1] = small[0] + rs[0]
+        per = gate_rows // 2
+        few[0] = jnp.concatenate(
+            [jnp.sum(small[n * per : (n + 1) * per, :], axis=0, keepdims=True) for n in range(2)]
+            + [small[gate_rows : gate_rows + 1, :], small[gate_rows + 8 : gate_rows + 9, :]]
+            + [jnp.zeros((4, width), F32)],
+            axis=0,
+        )
         plan.start("sb")
-        for c, n in late:
-            stages[n](c)
+        for task in tasks[final]:
+            task()
+        chunk_g(c)
         plan.arrived("sb")
-        small[2] = pair_sum([small[1]] + [rs[1 + n] for n in range(members - 1)])
+        few[1] = pair_sum([few[0]] + [rs[n] for n in range(len(near))])
         plan.start("sz")
-        for name in ("x0", "x1"):
-            plan.arrived(name)
-        plan.start("c_x")
+        chunk_h(c)
+        slice_d(1)
+        chunk_done(c)
         plan.arrived("sz")
-        small_ref[...] = pair_sum([small[2]] + [rs[members + d - 1] for d in others])
-        for name in ("yx0", "yx1"):
-            plan.arrived(name)
-        plan.start("c_d")
-        for name in ("c_own", "c_y", "c_x", "c_d"):
-            plan.arrived(name)
-        for c in range(pairs):
-            out_copy(c).wait()
+        small_ref[...] = pair_sum([few[1]] + [rs[len(near) + d - 1] for d in others])
+        for w in both:
+            for name in "oyxd":
+                plan.arrived(f"c{name}{w}")
+        for n in range(pairs + 1):
+            out_copy(n).wait()
         for name in plan.sets:
             plan.sent(name)
         for r in acts + gis:
@@ -850,7 +894,7 @@
     blocks = gate.shape[1] // BLOCK // micros
     chunk = min(CHUNK, ff)
     by_expert = lambda n: pl.BlockSpec((1, n, width), lambda e, c: (e, 0, 0))
-    members = len(plane_steps(nb))
+    members = 2 * nb
     return pl.pallas_call(
         functools.partial(experts_kernel, micros, blocks, nb),
         grid=(experts, ff // chunk),
@@ -859,12 +903,12 @@
             pl.BlockSpec((1, width, chunk), lambda e, c: (e, 0, c)),
             pl.BlockSpec((1, chunk, width), lambda e, c: (e, c, 0)),
         ],
-        out_specs=[by_expert(groups)] * 2 + [whole((2, 2 * (members + 1) * groups, width))],
+        out_specs=[by_expert(groups)] * 2 + [whole((2, members * groups, width))],
         out_shape=[shaped((experts, groups, width), F32)] * 2
-        + [shaped((2, 2 * (members + 1) * groups, width), BF)],
+        + [shaped((2, members * groups, width), BF)],
         scratch_shapes=[
-            pltpu.VMEM((experts, 2, groups, width), BF), pltpu.VMEM((2, 2, groups, width), BF),
-            pltpu.VMEM((members, 2, 2, groups, width), BF), DMA((members + 1,)), DMA((members + 1,)),
+            pltpu.VMEM((experts, 2, groups, width), BF),
+            pltpu.VMEM((members - 1, 2, groups, width), BF), DMA((members - 1,)), DMA((members - 1,)),
         ],
         compiler_params=params(2),
         name="experts",
@@ -891,27 +935,25 @@
     early = lambda s: jnp.minimum(s % span, blocks - 1)
     pair_of = lambda s: jnp.clip(s % span - blocks, 0, pairs - 1)
 
-    def early_or_late(s):
-        t = s % span
-        return jnp.where(t < blocks + pairs, jnp.minimum(t, blocks - 1), t - blocks - pairs)
-
     flat = lambda s: m_of(s) * blocks + early(s)
     row_block = pl.BlockSpec((1, BLOCK, width), lambda s: (m_of(s), early(s), 0))
     group_block = pl.BlockSpec((experts, per, width), lambda s: (0, flat(s), 0))
     pair_block = pl.BlockSpec((1, length, 2 * HEAD_DIM), lambda s: (m_of(s), 0, pair_of(s)))
     piece = (2, width // planes, cut)
-    chunk = 4 * 2 * HEAD_DIM
+    chunk = width
+    chunks = pairs + 1
     half = chunk // 2
     quarter = half // members
     reach = max(key_range(True, i)[1] for i in range(blocks))
     small = (rows + 16, width)
+    few = (8, width)
     vm = pltpu.VMEM
-    copies = 64 + 16 * pairs + 24 * planes
+    copies = 96 + 16 * chunks + 32 * planes
     return pl.pallas_call(
         functools.partial(backward_kernel, micros, blocks, nb, planes),
         grid=(micros * span,),
         in_specs=[
-            pl.BlockSpec((1, 1, BLOCK, width), lambda s: (m_of(s), early_or_late(s), 0, 0)),
+            pl.BlockSpec((1, nb, BLOCK, width), lambda s: (m_of(s), 0, 0, 0)),
             pl.BlockSpec((1, 1, BLOCK, width), lambda s: (m_of(s), early(s), 0, 0)),
             row_block,
             pl.BlockSpec((rows, BLOCK), lambda s: (0, flat(s))),
@@ -920,24 +962,24 @@
             pair_block, pair_block, pair_block,
             pl.BlockSpec((1, 2 * HEAD_DIM, length), lambda s: (m_of(s), pair_of(s), 0)),
         ] + [held(a.shape) for a in (start, g1, g2, wc, wq, wk, wv, wo, factors)] + [ANY, ANY],
-        out_specs=[ANY, ANY, ANY, whole(small), ANY, ANY],
+        out_specs=[ANY, ANY, ANY, whole(few), ANY, ANY],
         out_shape=[
-            shaped(x.shape, BF), shaped(x.shape, BF), shaped((pairs, chunk, width), BF),
-            shaped(small, F32), shaped(w_in.shape, BF), shaped(w_back.shape, BF),
+            shaped(x.shape, BF), shaped(x.shape, BF), shaped((chunks, chunk, width), BF),
+            shaped(few, F32), shaped(w_in.shape, BF), shaped(w_back.shape, BF),
         ],
         scratch_shapes=[
             vm((length, width), F32), vm((length, width), BF), vm((length, width), BF),
             vm((heads, length), F32), vm((length, width), BF), vm((length, width), BF),
             vm((length, width), BF), vm((length, 2 * HEAD_DIM), F32), vm((length, 2 * HEAD_DIM), F32),
-            vm((pairs, chunk, width), F32), vm((width, width), F32), vm((blocks, reach, BLOCK), F32),
+            vm((pairs, 6 * HEAD_DIM, width), F32), vm((width, width), F32), vm((blocks, reach, BLOCK), F32),
             vm(x.shape, BF), vm(x.shape, BF), vm((width, cut), BF), vm((cut, width), BF),
-            vm((planes,) + piece, BF), vm((planes - 1,) + piece, BF), vm(piece, BF),
-            vm((pairs, half, width), BF), vm((pairs, half, width), BF),
-            vm((pairs, members - 1, quarter, width), BF), vm((pairs, members - 1, quarter, width), BF),
-            vm((pairs, quarter, width), BF), vm((pairs, planes - 1, quarter, width), BF),
-            vm((pairs, chunk, width), BF), vm((3,) + small, F32),
-            vm((members + planes - 1,) + small, F32),
-            DMA((2 * micros,)), DMA((4 + pairs,)), DMA((2 * micros * (nb - 1),)),
+            vm((2, planes) + piece[1:], BF), vm((2, planes - 1) + piece[1:], BF), vm(piece, BF),
+            vm((chunks, half, width), BF), vm((chunks, half, width), BF),
+            vm((chunks, members - 1, quarter, width), BF), vm((chunks, members - 1, quarter, width), BF),
+            vm((chunks, quarter, width), BF), vm((chunks, planes - 1, quarter, width), BF),
+            vm((chunks, chunk, width), BF), vm(small, F32), vm((2,) + few, F32),
+            vm((2 * nb + planes - 2,) + few, F32),
+            DMA((2 * micros,)), DMA((5 + pairs,)), DMA((2 * micros * (nb - 1),)),
             DMA((2 * micros * (nb - 1),)), DMA((copies,)), DMA((copies,)),
         ],
         compiler_params=params(3),
@@ -963,12 +1005,11 @@
         x, cot, h, gate, eo, dmg, ob, lse, q, k, v, kt, start, g1, g2, wc, w_query, w_key, w_value,
         w_out, factors, w_in, w_back,
     )
-    flat = flat.reshape(width // (2 * HEAD_DIM), 4, 2 * HEAD_DIM, width)
-    one = lambda n: flat[:, n].reshape(width, width).astype(F32)
-    ctrl = jnp.sum(small[: experts * per].reshape(experts, per, width), axis=1).T
+    lanes = 2 * HEAD_DIM
+    one = lambda n: flat[1:, n * lanes : (n + 1) * lanes].reshape(width, width).astype(F32).T
     return (
-        acts, gis, small[experts * per + 8], one(0).T, one(1).T, one(2).T, one(3),
-        small[experts * per], ctrl, grad_in.astype(F32), grad_back.astype(F32),
+        acts, gis, small[3], one(0), one(1), one(2), flat[0].astype(F32), small[2], small[:experts].T,
+        grad_in.astype(F32), grad_back.astype(F32),
     )
 
 

time: 278 us -> 262 us (0.942)
  Pallas kernels: 249 us -> 232 us
    pallas_call x1, Pallas kernels: 157 us -> 143 us  [backward_call(): pl.pallas_call(functools.partial(backward_kernel, micros, blocks, nb, pla...]
    pallas_call x1, Pallas kernels: 21.5 us -> 18.5 us  [experts_call(): pl.pallas_call(functools.partial(experts_kernel, micros, blocks, nb), gri...]
where the time goes in v4:
time: 262 us
  Pallas kernels  232 us (89%)
  local copies, waits for them, and re-layouts  14.4 us (5%)
  other arithmetic  14.1 us (5%)
    pallas_call x1, Pallas kernels, backward_call(): pl.pallas_call(functools.partial(backward_kernel, micros, blocks, nb, pla...  143 us
    pallas_call x1, Pallas kernels, forward_call(): pl.pallas_call(functools.partial(forward_kernel, micros, blocks, nb), gri...  70.3 us
    pallas_call x1, Pallas kernels, experts_call(): pl.pallas_call(functools.partial(experts_kernel, micros, blocks, nb), gri...  18.5 us
    convert_element_type x1, other arithmetic, local(): grad_in.astype(F32)  6.8 us

profile of v4, /device:TPU:0, one launch (start us, length us, event | category | flops | bytes accessed | tf_op | source)
XLA Modules:
  0.0 261.7 jit_solution(394980388573526957)
XLA Ops:
  0.6 0.0 copy-start
  0.7 0.7 copy-done
  1.3 1.3 reshape.45.seg_src
  2.6 0.6 broadcast_bitcast_fusion.wc_ref
  3.2 70.3 %attention_forward.1 = (bf16[2,1024,512]{2,1,0:T(8,128)(2,1)}, bf16[2,1024,512]{2,1,0:T(8,128)(2,1)}, bf16[2,1024,512]{2,1,0:T(8,128)(2,1)}, bf16[2,512,1024]{2,...) custom-call(bf16[2,4,256,512]{3,2,1,0:T(8,128)(2,1)} %x_src.1, ...), custom_call_target="tpu_custom_call" | custom-call | tf_op jit(solution)/shard_map/attention_forward/pallas_call | solution.py:857
  73.6 18.5 %experts.1 = (f32[2,64,512]{2,1,0:T(8,128)}, f32[2,64,512]{2,1,0:T(8,128)}, bf16[2,512,512]{2,1,0:T(8,128)(2,1)}) custom-call(f32[2,64,512]{2,1,0:T(8,128)} %get-tuple-element.36.refs_0_, f32[16,2048]{1,0:T(8,128)} %get-tuple-element.35.refs_1_.gate_ref, bf16[2,4,256,512]{3,2,1,0:T(8,128)(2,1)} %get-tuple-element.33.refs_2_.cot_ref, ...), custom_call_target="tpu_custom_call" | custom-call | tf_op jit(solution)/shard_map/experts/pallas_call | solution.py:898
  92.1 143.4 %attention_backward.1 = (bf16[2,4,256,512]{3,2,1,0:T(8,128)(2,1)}, bf16[2,4,256,512]{3,2,1,0:T(8,128)(2,1)}, bf16[5,512,512]{2,1,0:T(8,128)(2,1)}, f32[8,512]{1,...) custom-call(bf16[2,4,256,512]{3,2,1,0:T(8,128)(2,1)} %get-tuple-element.32.x_ref, ...), custom_call_target="tpu_custom_call" | custom-call | tf_op jit(solution)/shard_map/attention_backward/pallas_call | solution.py:952
  235.5 1.3 slice_bitcast_fusion
  236.8 1.4 fusion.1
  238.2 2.1 bitcast_convert_fusion
  240.3 1.5 fusion
  241.8 0.2 bitcast_convert_fusion.3
  242.0 1.3 copy.23
  243.3 0.3 bitcast_convert_fusion.1
  243.7 1.3 copy.25
  245.0 1.3 copy.24
  246.3 0.0 copy-start.2
  246.3 6.8 %convert_element_type.29 = f32[2,512,2048]{2,1,0:T(8,128)} convert(bf16[2,512,2048]{2,1,0:T(8,128)(2,1)} %get-tuple-element.51) | non-fusion elementwise | flops 2097152 | bytes 12582912 | tf_op jit(solution)/shard_map/convert_element_type | solution.py:1012
  253.1 0.0 copy-done.2
  253.1 0.0 copy-start.4
  253.1 4.6 %convert_element_type.30 = f32[2,2048,512]{2,1,0:T(8,128)} convert(bf16[2,2048,512]{2,1,0:T(8,128)(2,1)S(1)} %copy-done.2) | non-fusion elementwise | flops 2097152 | bytes 12582912 | tf_op jit(solution)/shard_map/convert_element_type | solution.py:1012
  257.7 0.0 copy-done.4
  257.7 0.0 copy-start.3
  257.7 0.0 copy-start.1
  257.7 1.3 copy.28
  259.0 1.0 copy-done.3
  260.0 1.3 copy.29
  261.4 0.0 copy-done.1
Async XLA Ops:
  0.6 0.7 copy-start
  246.3 6.8 %copy-start.2 = (bf16[2,2048,512]{2,1,0:T(8,128)(2,1)S(1)}, bf16[2,2048,512]{2,1,0:T(8,128)(2,1)}, u32[]{:S(2)}) copy-start(bf16[2,2048,512]{2,1,0:T(8,128)(2,1)} %get-tuple-element.52) | copy-start | bytes 12582916
  253.1 4.6 %copy-start.4 = (bf16[2,4,256,512]{3,2,1,0:T(8,128)(2,1)S(1)}, bf16[2,4,256,512]{3,2,1,0:T(8,128)(2,1)}, u32[]{:S(2)}) copy-start(bf16[2,4,256,512]{3,2,1,0:T(8,128)(2,1)} %get-tuple-element.71) | copy-start | bytes 6291460
  257.7 2.3 copy-start.3
  257.7 3.7 %copy-start.1 = (bf16[512,2]{0,1:T(2,128)(2,1)S(1)}, bf16[512,2]{0,1:T(2,128)(2,1)}, u32[]{:S(2)}) copy-start(bf16[512,2]{0,1:T(2,128)(2,1)} %param.20) | copy-start | bytes 6148
